TPU v7x, 32 devices: a whole 2x2x4 slice. The times are simulated.
32 devices in a mesh: dp: 4 (over z), expert: 8 (over y, x, core).
Axes of the slice: x: 2, y: 2, z: 4, core: 2. Of those that a mesh axis runs over, the one named last changes fastest.
Arguments:
- tokens: bfloat16 [92160, 512], P(('dp', 'expert')), may hold values from -6 to 6
- cotangent: bfloat16 [92160, 512], P(('dp', 'expert')), may hold values from -6 to 6
- expert_ids: int32 [92160, 2], P(('dp', 'expert')), may hold values from 0 to 7, all different within a row
- priority: int32 [32, 5760], P(('dp', 'expert')), may hold values from 0 to 5759, each once within a row
- step: int32 [], replicated, may hold values from 2 to 20
- attn_qkv: float32 [512, 1536], P(None, 'dp'), may hold values from -0.25 to 0.25
- attn_out: float32 [512, 512], P('dp'), may hold values from -4 to 4
- router: float32 [512, 8], P(None, 'dp'), may hold values from -0.1875 to 0.1875
- norms: float32 [4, 512], P(None, 'dp'), as said below
- expert_in: float32 [8, 512, 2048], P('expert', None, 'dp'), may hold values from -0.25 to 0.25
- expert_out: float32 [8, 2048, 512], P('expert', 'dp'), as said below
- moments_qkv: float32 [2, 512, 1536], P(None, None, 'dp'), as said below
- moments_out: float32 [2, 512, 512], P(None, 'dp'), as said below
- moments_router: float32 [2, 512, 8], P(None, None, 'dp'), as said below
- moments_norms: float32 [2, 4, 512], P(None, None, 'dp'), as said below
- moments_in: float32 [2, 8, 512, 2048], P(None, 'expert', None, 'dp'), as said below
- moments_exp: float32 [2, 8, 2048, 512], P(None, 'expert', 'dp'), as said below
Outputs:
- activations: bfloat16 [92160, 512], P(('dp', 'expert'))
- grad_input: float32 [92160, 512], P(('dp', 'expert'))
- grad_norm: float32 [], replicated
- new_qkv: float32 [512, 1536], P(None, 'dp')
- first_qkv: float32 [512, 1536], P(None, 'dp')
- second_qkv: float32 [512, 1536], P(None, 'dp')
- copy_qkv: bfloat16 [512, 1536], P(None, 'dp')
- new_out: float32 [512, 512], P('dp')
- first_out: float32 [512, 512], P('dp')
- second_out: float32 [512, 512], P('dp')
- copy_out: bfloat16 [512, 512], P('dp')
- new_router: float32 [512, 8], P(None, 'dp')
- first_router: float32 [512, 8], P(None, 'dp')
- second_router: float32 [512, 8], P(None, 'dp')
- copy_router: bfloat16 [512, 8], P(None, 'dp')
- new_norms: float32 [4, 512], P(None, 'dp')
- first_norms: float32 [4, 512], P(None, 'dp')
- second_norms: float32 [4, 512], P(None, 'dp')
- copy_norms: bfloat16 [4, 512], P(None, 'dp')
- new_expert_in: float32 [8, 512, 2048], P('expert', None, 'dp')
- first_expert_in: float32 [8, 512, 2048], P('expert', None, 'dp')
- second_expert_in: float32 [8, 512, 2048], P('expert', None, 'dp')
- copy_expert_in: bfloat16 [8, 512, 2048], P('expert', None, 'dp')
- new_expert_out: float32 [8, 2048, 512], P('expert', 'dp')
- first_expert_out: float32 [8, 2048, 512], P('expert', 'dp')
- second_expert_out: float32 [8, 2048, 512], P('expert', 'dp')
- copy_expert_out: bfloat16 [8, 2048, 512], P('expert', 'dp')
Inputs may be any that keep to these rules, and one draw needn't show every extreme that they name: `norms`: rows 0 and 2 are gains near one, rows 1 and 3 small biases. `expert_out`: entries of both signs. `moments_qkv`: index 1 (second moments) is positive. `moments_out`: index 1 (second moments) is positive. `moments_router`: index 1 (second moments) is positive. `moments_norms`: index 1 (second moments) is positive. `moments_in`: index 1 (second moments) is positive. `moments_exp`: index 1 (second moments) is positive.
All inputs are finite; a program needn't handle non-finite values.
Results may differ from a plain program's by a relative error of at most 0.015.
Values may be sent and summed in bfloat16 or wider, within the bound.
No kernel may reach another device: no remote copies, remote signals or barrier semaphores. Data moves between devices by JAX's collectives and lax.ppermute only.
A program may use at most 320 MiB of HBM per device.

v0:
```python
import jax
import jax.numpy as jnp
from jax import lax
from jax.sharding import PartitionSpec as P

D = 512
HEADS = 8
HEAD = 64
FF = 2048
SEQ = 720


EPS_NORM = 1e-06
BETA_ONE = 0.9
BETA_TWO = 0.999
ADAM_EPS = 1e-08
DECAY_RATE = 0.1
MAX_NORM = 1.0


def layer_norm(values, gain_row, shift_row):
    center = values - jnp.mean(values, axis=-1, keepdims=True)
    spread = jnp.mean(center * center, axis=-1, keepdims=True)
    return center * lax.rsqrt(spread + EPS_NORM) * gain_row + shift_row


def gelu_exact(values):
    return jax.nn.gelu(values, approximate=False)


def gelu_slope(values):
    return (
        0.5 * (1.0 + jax.scipy.special.erf(values * 0.7071067811865476))
        + values * jnp.exp(-0.5 * values * values) * 0.3989422804014327
    )


def split_heads(packed, part_index):
    length = packed.shape[0]
    return packed[:, part_index * D : (part_index + 1) * D].reshape(length, HEADS, HEAD)


def attend_forward(normed_b, qkv_w, out_w):
    head_scale = HEAD ** (-0.5)
    proj_b = jnp.dot(normed_b, qkv_w, preferred_element_type=jnp.float32).astype(jnp.bfloat16)
    queries = split_heads(proj_b, 0)
    keys_all = split_heads(proj_b, 1)
    values_all = split_heads(proj_b, 2)
    scores = (
        jnp.einsum("qhd,khd->hqk", queries, keys_all, preferred_element_type=jnp.float32)
        * head_scale
    )
    row_top = jnp.max(scores, axis=-1, keepdims=True)
    log_total = row_top + jnp.log(jnp.sum(jnp.exp(scores - row_top), axis=-1, keepdims=True))
    probs_b = jnp.exp(scores - log_total).astype(jnp.bfloat16)
    context = jnp.einsum("hqk,khd->qhd", probs_b, values_all, preferred_element_type=jnp.float32)
    context_b = context.reshape(-1, D).astype(jnp.bfloat16)
    attended = jnp.dot(context_b, out_w, preferred_element_type=jnp.float32)
    return (attended, (proj_b, log_total, context_b))


def attend_backward(grad_b, saved, normed_b, qkv_w, out_w):
    head_scale = HEAD ** (-0.5)
    proj_b, log_total, context_b = saved
    length = proj_b.shape[0]
    grad_context = jnp.einsum("sf,df->sd", grad_b, out_w, preferred_element_type=jnp.float32)
    grad_context = grad_context.astype(jnp.bfloat16).reshape(length, HEADS, HEAD)
    queries = split_heads(proj_b, 0)
    keys_all = split_heads(proj_b, 1)
    values_all = split_heads(proj_b, 2)
    scores = (
        jnp.einsum("qhd,khd->hqk", queries, keys_all, preferred_element_type=jnp.float32)
        * head_scale
    )
    probs = jnp.exp(scores - log_total)
    grad_probs = jnp.einsum(
        "qhd,khd->hqk", grad_context, values_all, preferred_element_type=jnp.float32
    )
    grad_values = jnp.einsum(
        "hqk,qhd->khd", probs.astype(jnp.bfloat16), grad_context, preferred_element_type=jnp.float32
    )
    inner = jnp.sum(probs * grad_probs, axis=-1, keepdims=True)
    grad_scores = (probs * (grad_probs - inner)).astype(jnp.bfloat16)
    grad_queries = (
        jnp.einsum("hqk,khd->qhd", grad_scores, keys_all, preferred_element_type=jnp.float32)
        * head_scale
    )
    grad_keys = (
        jnp.einsum("hqk,qhd->khd", grad_scores, queries, preferred_element_type=jnp.float32)
        * head_scale
    )
    grad_proj = jnp.concatenate(
        [
            grad_queries.reshape(length, D),
            grad_keys.reshape(length, D),
            grad_values.reshape(length, D),
        ],
        axis=1,
    ).astype(jnp.bfloat16)
    grad_qkv = jnp.einsum("sd,sf->df", normed_b, grad_proj, preferred_element_type=jnp.float32)
    grad_normed = jnp.einsum("sf,df->sd", grad_proj, qkv_w, preferred_element_type=jnp.float32)
    grad_out = jnp.einsum("sd,sf->df", context_b, grad_b, preferred_element_type=jnp.float32)
    return (grad_normed, grad_qkv, grad_out)


def step_rates(experts):
    return (
        D ** (-0.5),
        2.0 ** (-0.5),
        (2 * D) ** (-0.5),
        0.1,
        D ** (-0.5),
        2.0 * experts / (1.2 * FF**0.5),
    )


def adam_update(weight, moments, grad, factor, rate, decay, step_float):
    clipped = grad * factor
    first = BETA_ONE * moments[0] + (1.0 - BETA_ONE) * clipped
    second = BETA_TWO * moments[1] + (1.0 - BETA_TWO) * clipped * clipped
    fix_one = 1.0 - jnp.power(BETA_ONE, step_float)
    fix_two = 1.0 - jnp.power(BETA_TWO, step_float)
    updated = weight - rate * (
        first / fix_one / (jnp.sqrt(second / fix_two) + ADAM_EPS) + decay * weight
    )
    return (updated, first, second, updated.astype(jnp.bfloat16))


def take_share(whole, axis_dim, width):
    return lax.dynamic_slice_in_dim(whole, lax.axis_index("dp") * width, width, axis_dim)


def square_sum(arrays):
    total = jnp.zeros((), jnp.float32)
    for member in arrays:
        total = total + jnp.sum(member * member)
    return total


def rank_in_expert(pair_expert, pair_rank, experts):
    pair_count = pair_expert.shape[0]
    order = (
        jnp.zeros((pair_count,), jnp.int32)
        .at[pair_rank]
        .set(jnp.arange(pair_count, dtype=jnp.int32))
    )
    ordered_expert = pair_expert[order]
    onehot = (ordered_expert[:, None] == jnp.arange(experts, dtype=jnp.int32)[None, :]).astype(
        jnp.int32
    )
    before = jnp.cumsum(onehot, axis=0) - onehot
    ordered_rank = jnp.sum(before * onehot, axis=1)
    return ordered_rank[pair_rank]


def shards(
    tokens,
    cotangent,
    expert_ids,
    priority,
    step,
    attn_qkv,
    attn_out,
    router,
    norms,
    expert_in,
    expert_out,
    moments_qkv,
    moments_out,
    moments_router,
    moments_norms,
    moments_in,
    moments_exp,
):
    tok_dev = tokens.shape[0]
    groups = lax.axis_size("expert")
    local = expert_in.shape[0]
    experts = local * groups
    capacity = (tok_dev + experts - 1) // experts
    pair_count = 2 * tok_dev
    pictures = tok_dev // SEQ
    working = (
        lax.all_gather(attn_qkv.astype(jnp.bfloat16), "dp", axis=1, tiled=True),
        lax.all_gather(attn_out.astype(jnp.bfloat16), "dp", axis=0, tiled=True),
        lax.all_gather(router.astype(jnp.bfloat16), "dp", axis=1, tiled=True),
        lax.all_gather(norms.astype(jnp.bfloat16), "dp", axis=1, tiled=True),
        lax.all_gather(expert_in.astype(jnp.bfloat16), "dp", axis=2, tiled=True),
        lax.all_gather(expert_out.astype(jnp.bfloat16), "dp", axis=1, tiled=True),
    )
    qkv_w, out_w, router_w, norm_w, in_w, exp_w = working
    gain_rows = norm_w.astype(jnp.float32)
    inputs = tokens.astype(jnp.float32)
    first, norm_one_back = jax.vjp(layer_norm, inputs, gain_rows[0], gain_rows[1])
    first_b = first.astype(jnp.bfloat16).reshape(pictures, SEQ, D)
    attended, saved = lax.map(lambda picture: attend_forward(picture, qkv_w, out_w), first_b)
    middle = inputs + attended.reshape(tok_dev, D)
    second, norm_two_back = jax.vjp(layer_norm, middle, gain_rows[2], gain_rows[3])
    second_b = second.astype(jnp.bfloat16)
    logits = jnp.dot(second_b, router_w, preferred_element_type=jnp.float32)
    gates_all = jax.nn.softmax(logits, axis=-1)
    pair_expert = expert_ids.reshape(pair_count)
    pair_rank = priority.reshape(pair_count)
    slot_rank = rank_in_expert(pair_expert, pair_rank, experts)
    kept_mask = slot_rank < capacity
    expert_axis = jnp.arange(experts, dtype=jnp.int32)
    chosen = pair_expert[:, None] == expert_axis[None, :]
    gates_pair = jnp.repeat(gates_all, 2, axis=0)
    gate_value = jnp.where(kept_mask, jnp.sum(jnp.where(chosen, gates_pair, 0.0), axis=1), 0.0)
    position = jnp.where(kept_mask, pair_expert * capacity + slot_rank, experts * capacity)
    slot_pair = (
        jnp.full((experts * capacity,), pair_count, jnp.int32)
        .at[position]
        .set(jnp.arange(pair_count, dtype=jnp.int32), mode="drop")
    )
    slot_token = slot_pair // 2
    second_pad = jnp.concatenate([second_b, jnp.zeros((1, D), jnp.bfloat16)], axis=0)
    send_rows = second_pad[slot_token].reshape(experts, capacity, D)
    arrived = lax.all_to_all(send_rows, "expert", split_axis=0, concat_axis=0, tiled=True)
    items = arrived.shape[1]
    grid = arrived.reshape(groups, local, items, D)
    hidden = jnp.einsum("slcd,ldf->slcf", grid, in_w, preferred_element_type=jnp.float32)
    act_b = gelu_exact(hidden).astype(jnp.bfloat16)
    output = jnp.einsum("slcf,lfd->slcd", act_b, exp_w, preferred_element_type=jnp.float32).astype(
        jnp.bfloat16
    )
    received, hidden, act_b, returned = (
        arrived,
        hidden.reshape(groups * local, items, FF),
        act_b.reshape(groups * local, items, FF),
        output.reshape(groups * local, items, D),
    )
    coming = lax.all_to_all(returned, "expert", split_axis=0, concat_axis=0, tiled=True)
    coming_pad = jnp.concatenate(
        [coming.reshape(experts * capacity, D), jnp.zeros((1, D), jnp.bfloat16)], axis=0
    )
    picked = coming_pad[position].astype(jnp.float32)
    mixed = jnp.sum((gate_value[:, None] * picked).reshape(tok_dev, 2, D), axis=1)
    activations = (middle + mixed).astype(jnp.bfloat16)
    upstream = cotangent.astype(jnp.float32)
    gate_pad = jnp.concatenate([gate_value, jnp.zeros((1,), jnp.float32)])
    upstream_pad = jnp.concatenate([upstream, jnp.zeros((1, D), jnp.float32)], axis=0)
    grad_slots = (
        (gate_pad[slot_pair][:, None] * upstream_pad[slot_token])
        .astype(jnp.bfloat16)
        .reshape(experts, capacity, D)
    )
    grad_gate = jnp.where(kept_mask, jnp.sum(jnp.repeat(upstream, 2, axis=0) * picked, axis=1), 0.0)
    grad_returned = lax.all_to_all(grad_slots, "expert", split_axis=0, concat_axis=0, tiled=True)
    grad_grid = grad_returned.reshape(groups, local, capacity, D)
    act_grid = act_b.reshape(groups, local, capacity, FF)
    hidden_grid = hidden.reshape(groups, local, capacity, FF)
    rows_grid = received.reshape(groups, local, capacity, D)
    grad_exp = jnp.einsum("slcf,slcd->lfd", act_grid, grad_grid, preferred_element_type=jnp.float32)
    grad_act = jnp.einsum("slcd,lfd->slcf", grad_grid, exp_w, preferred_element_type=jnp.float32)
    grad_hidden = (grad_act * gelu_slope(hidden_grid)).astype(jnp.bfloat16)
    grad_in = jnp.einsum(
        "slcd,slcf->ldf", rows_grid, grad_hidden, preferred_element_type=jnp.float32
    )
    grad_rows = jnp.einsum("slcf,ldf->slcd", grad_hidden, in_w, preferred_element_type=jnp.float32)
    grad_rows = grad_rows.astype(jnp.bfloat16).reshape(groups * local, capacity, D)
    grad_sent = lax.all_to_all(grad_rows, "expert", split_axis=0, concat_axis=0, tiled=True)
    sent_pad = jnp.concatenate(
        [grad_sent.reshape(experts * capacity, D), jnp.zeros((1, D), jnp.bfloat16)], axis=0
    )
    grad_picked = sent_pad[position].astype(jnp.float32)
    grad_gates = jnp.sum(
        jnp.where(chosen, grad_gate[:, None], 0.0).reshape(tok_dev, 2, experts), axis=1
    )
    inner = jnp.sum(gates_all * grad_gates, axis=-1, keepdims=True)
    grad_logits = (gates_all * (grad_gates - inner)).astype(jnp.bfloat16)
    grad_router = jnp.einsum("td,te->de", second_b, grad_logits, preferred_element_type=jnp.float32)
    grad_second = jnp.sum(grad_picked.reshape(tok_dev, 2, D), axis=1)
    grad_second = grad_second + jnp.einsum(
        "te,de->td", grad_logits, router_w, preferred_element_type=jnp.float32
    )
    grad_middle, grad_gain_two, grad_shift_two = norm_two_back(grad_second)
    grad_middle = grad_middle + upstream
    grad_attn = grad_middle.astype(jnp.bfloat16).reshape(pictures, SEQ, D)
    grad_first, grad_qkv_each, grad_out_each = lax.map(
        lambda packed: attend_backward(packed[0], packed[1], packed[2], qkv_w, out_w),
        (grad_attn, saved, first_b),
    )
    grad_qkv = jnp.sum(grad_qkv_each, axis=0)
    grad_out = jnp.sum(grad_out_each, axis=0)
    grad_enter, grad_gain_one, grad_shift_one = norm_one_back(grad_first.reshape(tok_dev, D))
    grad_input = grad_middle + grad_enter
    grad_norms = jnp.stack([grad_gain_one, grad_shift_one, grad_gain_two, grad_shift_two])
    dense = lax.psum((grad_qkv, grad_out, grad_router, grad_norms), ("dp", "expert"))
    owned = (
        lax.psum(grad_in.astype(jnp.bfloat16), "dp").astype(jnp.float32),
        lax.psum(grad_exp.astype(jnp.bfloat16), "dp").astype(jnp.float32),
    )
    share_qkv = take_share(dense[0], 1, attn_qkv.shape[1])
    share_out = take_share(dense[1], 0, attn_out.shape[0])
    share_router = take_share(dense[2], 1, router.shape[1])
    share_norms = take_share(dense[3], 1, norms.shape[1])
    share_in = take_share(owned[0], 2, expert_in.shape[2])
    share_exp = take_share(owned[1], 1, expert_out.shape[1])
    term = square_sum((share_qkv, share_out, share_router, share_norms)) / groups + square_sum(
        (share_in, share_exp)
    )
    grad_norm = jnp.sqrt(lax.psum(term, ("dp", "expert")))
    factor = MAX_NORM / grad_norm
    rates = step_rates(experts)
    step_float = step.astype(jnp.float32)
    new_qkv, first_qkv, second_qkv, copy_qkv = adam_update(
        attn_qkv, moments_qkv, share_qkv, factor, rates[0], DECAY_RATE, step_float
    )
    new_out, first_out, second_out, copy_out = adam_update(
        attn_out, moments_out, share_out, factor, rates[1], DECAY_RATE, step_float
    )
    new_router, first_router, second_router, copy_router = adam_update(
        router, moments_router, share_router, factor, rates[2], DECAY_RATE, step_float
    )
    new_norms, first_norms, second_norms, copy_norms = adam_update(
        norms, moments_norms, share_norms, factor, rates[3], 0.0, step_float
    )
    new_in, first_in, second_in, copy_in = adam_update(
        expert_in, moments_in, share_in, factor, rates[4], DECAY_RATE, step_float
    )
    new_exp, first_exp, second_exp, copy_exp = adam_update(
        expert_out, moments_exp, share_exp, factor, rates[5], DECAY_RATE, step_float
    )
    return (
        activations,
        grad_input,
        grad_norm,
        new_qkv,
        first_qkv,
        second_qkv,
        copy_qkv,
        new_out,
        first_out,
        second_out,
        copy_out,
        new_router,
        first_router,
        second_router,
        copy_router,
        new_norms,
        first_norms,
        second_norms,
        copy_norms,
        new_in,
        first_in,
        second_in,
        copy_in,
        new_exp,
        first_exp,
        second_exp,
        copy_exp,
    )


def solution(mesh):
    in_specs = (
        P(("dp", "expert"), None),
        P(("dp", "expert"), None),
        P(("dp", "expert"), None),
        P(("dp", "expert"), None),
        P(),
        P(None, "dp"),
        P("dp", None),
        P(None, "dp"),
        P(None, "dp"),
        P("expert", None, "dp"),
        P("expert", "dp", None),
        P(None, None, "dp"),
        P(None, "dp", None),
        P(None, None, "dp"),
        P(None, None, "dp"),
        P(None, "expert", None, "dp"),
        P(None, "expert", "dp", None),
    )
    out_specs = (
        P(("dp", "expert"), None),
        P(("dp", "expert"), None),
        P(),
        P(None, "dp"),
        P(None, "dp"),
        P(None, "dp"),
        P(None, "dp"),
        P("dp", None),
        P("dp", None),
        P("dp", None),
        P("dp", None),
        P(None, "dp"),
        P(None, "dp"),
        P(None, "dp"),
        P(None, "dp"),
        P(None, "dp"),
        P(None, "dp"),
        P(None, "dp"),
        P(None, "dp"),
        P("expert", None, "dp"),
        P("expert", None, "dp"),
        P("expert", None, "dp"),
        P("expert", None, "dp"),
        P("expert", "dp", None),
        P("expert", "dp", None),
        P("expert", "dp", None),
        P("expert", "dp", None),
    )
    return jax.shard_map(shards, mesh=mesh, in_specs=in_specs, out_specs=out_specs, check_vma=False)
```

profile of v0, /device:TPU:0, one launch (start us, length us, event | category | flops | bytes accessed | tf_op | source)
XLA Modules:
  0.0 1331.0 jit_solution(421663060470408425)
XLA Ops:
  29.3 21.4 %all_gather.20 = bf16[512,512]{1,0:T(8,128)(2,1)} all-gather(bf16[128,512]{1,0:T(8,128)(2,1)S(1)} %convert_element_type.171), channel_id=1, replica_groups=mesh['dp'=4,'expert'=8] {'dp'}, dimensions={0}, use_global_device_ids=true | all-gather | bytes 655360 | tf_op jit(solution)/shard_map/all_gather | solution.py:184
  50.8 27.6 %scatter_custom_fusion = s32[5760]{0:T(1024)S(1)} fusion(s32[5760]{0:T(1024)S(1)} %fusion.110, s32[5760]{0:T(1024)S(1)} %iota.23, s32[]{:T(128)} %copy.170), kind=kCustom, calls=%fused_computation.208 | custom fusion | bytes 23044 | tf_op jit(solution)/shard_map/scatter | solution.py:145
  80.6 30.0 %gather_fusion = s32[5760]{0:T(1024)S(1)} fusion(s32[5760]{0:T(1024)S(1)} %reshape.504, s32[6144]{0:T(1024)S(1)} %pad_clamp_fusion.2), kind=kCustom, calls=%fused_computation | custom fusion | bytes 69120 | tf_op jit(solution)/shard_map/gather | solution.py:147
  117.7 30.0 %gather_fusion.1 = s32[5760]{0:T(1024)S(1)} fusion(s32[5760]{0:T(1024)S(1)} %fusion.107, s32[6144]{0:T(1024)S(1)} %pad_clamp_fusion.1), kind=kCustom, calls=%fused_computation.1 | custom fusion | bytes 69120 | tf_op jit(solution)/shard_map/gather | solution.py:153
  148.5 27.6 %scatter_custom_fusion.1 = s32[2880]{0:T(1024)S(1)} fusion(s32[5760]{0:T(1024)S(1)} %get-tuple-element.190, s32[5760]{0:T(1024)S(1)} %iota.24, s32[]{:T(128)} %constant.89.clone.1), kind=kCustom, calls=%fused_computation.219 | custom fusion | bytes 11524 | tf_op jit(solution)/shard_map/scatter | solution.py:213
  182.8 143.6 %while.30 = (s32[]{:T(128)}, f32[4,720,512]{2,1,0:T(8,128)}, bf16[4,720,1536]{2,1,0:T(8,128)(2,1)}, f32[4,8,720,1]{2,1,3,0:T(8,128)}, bf16[4,720,512]{2,1,0:T(8,...) while((s32[]{:T(128)}, f32[4,720,512]{2,1,0:T(8,128)}, ...), condition=%wide.region_5.6_spmd, body=%wide.region_2.5_spmd.sunk | while | flops 2606279168 | bytes 76267640 | solution.py:195
  350.3 34.8 %all-to-all-done = bf16[8,360,512]{2,1,0:T(8,128)(2,1)} async-done(((bf16[8,360,512]{2,1,0:T(8,128)(2,1)}), bf16[8,360,512]{2,1,0:T(8,128)(2,1)}, u32[]{:S(2)}, u32[]{:S(2)}) %all-to-all-start) | async-done | bytes 2949152 | tf_op jit(solution)/shard_map/all_to_all | solution.py:218
  398.3 54.5 %fusion.85 = bf16[8,360,512]{2,1,0:T(8,128)(2,1)} fusion(f32[8,360,2048]{2,1,0:T(8,128)} %fusion.91, bf16[1,2048,512]{2,1,0:T(8,128)(2,1)} %all-gather.9.cloned.1.call-done), kind=kOutput, calls=%fused_computation.129 | convolution fusion | flops 6424657920 | bytes 28639232 | tf_op jit(solution)/shard_map/slcf,lfd->slcd/dot_general | solution.py:223
  469.4 15.3 %broadcast_in_dim.130 = f32[2880,2,512]{2,1,0:T(2,128)} broadcast(bf16[2880,512]{1,0:T(8,128)(2,1)S(1)} %copy-done.11), dimensions={0,2} | broadcast | bytes 14745600 | tf_op jit(solution)/shard_map/broadcast_in_dim | solution.py:247
  521.7 17.3 %gather_fusion.3 = bf16[5760,512]{1,0:T(8,128)(2,1)} fusion(bf16[2881,512]{1,0:T(8,128)(2,1)S(1)} %concatenate.20, s32[6144]{0:T(1024)S(1)} %pad_clamp_fusion), kind=kCustom, calls=%fused_computation.3 | custom fusion | bytes 11819520 | tf_op jit(solution)/shard_map/gather | solution.py:236
  563.2 15.3 %gather_fusion.4 = f32[2880]{0:T(1024)S(1)} fusion(f32[5761]{0:T(1024)S(1)} %pad_maximum_fusion.3, s32[3072]{0:T(1024)S(1)} %copy-done.52), kind=kCustom, calls=%fused_computation.4 | custom fusion | bytes 34560 | tf_op jit(solution)/shard_map/gather | solution.py:243
  589.4 21.8 %multiply_reduce_fusion.3 = f32[2880,512]{1,0:T(8,128)} fusion(f32[2880,2,512]{2,1,0:T(2,128)} %reshape.520, f32[2880,2]{1,0:T(8,128)S(1)} %copy.95), kind=kLoop, calls=%fused_computation.98 | loop fusion | flops 4423680 | bytes 17717760 | tf_op jit(solution)/shard_map/reduce_sum | solution.py:237
  624.0 15.4 %fusion.36 = bf16[8,1,360,2048]{3,2,0,1:T(8,128)(2,1)S(1)} fusion(f32[8,360,2048]{2,1,0:T(8,128)} %fusion.91, bf16[8,360,512]{2,1,0:T(8,128)(2,1)} %all-to-all-done.2, bf16[1,2048,512]{2,1,0:T(8,128)(2,1)} %all-gather.9.cloned.1.call-done), kind=kOutput, calls=%fused_computation.65 | convolution fusion | flops 6098780160 | bytes 40435712 | tf_op jit(solution)/shard_map/slcd,lfd->slcf/dot_general | solution.py:254
  657.0 57.5 %fusion.79 = bf16[1,2048,512]{2,1,0:T(8,128)(2,1)} fusion(bf16[8,360,512]{2,1,0:T(8,128)(2,1)} %all-to-all-done.2, f32[8,360,2048]{2,1,0:T(8,128)} %fusion.91), kind=kOutput, calls=%fused_computation.127 | convolution fusion | flops 6424231936 | bytes 28639232 | tf_op jit(solution)/shard_map/slcf,slcd->lfd/dot_general | solution.py:253
  725.8 17.5 %gather_fusion.6 = bf16[5760,512]{1,0:T(8,128)(2,1)} fusion(bf16[2881,512]{1,0:T(8,128)(2,1)S(1)} %concatenate.23, s32[6144]{0:T(1024)S(1)} %copy-done.33), kind=kCustom, calls=%fused_computation.6 | custom fusion | bytes 11819520 | tf_op jit(solution)/shard_map/gather | solution.py:265
  756.9 21.1 %reduce_sum.315 = f32[2880,512]{1,0:T(8,128)} reduce(f32[2880,2,512]{2,1,0:T(2,128)} %reshape.521, f32[]{:T(128)} %constant.85.clone.1), dimensions={1}, to_apply=%region_17.18 | reduce | flops 1474560 | bytes 17694724 | tf_op jit(solution)/shard_map/reduce_sum | solution.py:272
  807.2 293.6 %while.31 = (s32[]{:T(128)}, f32[4,720,512]{2,1,0:T(8,128)}, f32[4,512,1536]{2,1,0:T(8,128)}, f32[4,512,512]{2,1,0:T(8,128)}, bf16[4,720,1536]{2,1,0:T(8,128)(2,...) while((s32[]{:T(128)}, f32[4,720,512]{2,1,0:T(8,128)}, ...), condition=%wide.region_25.26_spmd, body=%wide.region_23.25_spmd.sunk | while | flops 5739350528 | bytes 265680336 | solution.py:279
  827.0 15.0 %multiply_reduce_fusion.15 = (f32[8,720]{1,0:T(8,128)S(1)}, f32[8,720,720]{1,2,0:T(8,128)}) fusion(f32[8,720,720]{1,2,0:T(8,128)} %fusion.293, f32[8,720]{1,0:T(8,128)S(1)} %dynamic-slice_bitcast_fusion.2, bf16[720,8,64]{0,2,1:T(8,128)(2,1)} %bitcast.369, bf16[720,8,64]{0,2,1:T(8,128)(2,1)} %bitcast.374), kind=kOutput, calls=%fused_computation.25.clone.1 | convolution fusion | flops 547424640 | bytes 34698240 | tf_op jit(solution)/shard_map/while/body/eval_jaxpr/qhd,khd->hqk/dot_general | solution.py:76
  900.4 15.0 %multiply_reduce_fusion.15 = (f32[8,720]{1,0:T(8,128)S(1)}, f32[8,720,720]{1,2,0:T(8,128)}) fusion(f32[8,720,720]{1,2,0:T(8,128)} %fusion.293, f32[8,720]{1,0:T(8,128)S(1)} %dynamic-slice_bitcast_fusion.2, bf16[720,8,64]{0,2,1:T(8,128)(2,1)} %bitcast.369, bf16[720,8,64]{0,2,1:T(8,128)(2,1)} %bitcast.374), kind=kOutput, calls=%fused_computation.25.clone.1 | convolution fusion | flops 547424640 | bytes 34698240 | tf_op jit(solution)/shard_map/while/body/eval_jaxpr/qhd,khd->hqk/dot_general | solution.py:76
  973.7 15.0 %multiply_reduce_fusion.15 = (f32[8,720]{1,0:T(8,128)S(1)}, f32[8,720,720]{1,2,0:T(8,128)}) fusion(f32[8,720,720]{1,2,0:T(8,128)} %fusion.293, f32[8,720]{1,0:T(8,128)S(1)} %dynamic-slice_bitcast_fusion.2, bf16[720,8,64]{0,2,1:T(8,128)(2,1)} %bitcast.369, bf16[720,8,64]{0,2,1:T(8,128)(2,1)} %bitcast.374), kind=kOutput, calls=%fused_computation.25.clone.1 | convolution fusion | flops 547424640 | bytes 34698240 | tf_op jit(solution)/shard_map/while/body/eval_jaxpr/qhd,khd->hqk/dot_general | solution.py:76
  1046.8 15.0 %multiply_reduce_fusion.15 = (f32[8,720]{1,0:T(8,128)S(1)}, f32[8,720,720]{1,2,0:T(8,128)}) fusion(f32[8,720,720]{1,2,0:T(8,128)} %fusion.293, f32[8,720]{1,0:T(8,128)S(1)} %dynamic-slice_bitcast_fusion.2, bf16[720,8,64]{0,2,1:T(8,128)(2,1)} %bitcast.369, bf16[720,8,64]{0,2,1:T(8,128)(2,1)} %bitcast.374), kind=kOutput, calls=%fused_computation.25.clone.1 | convolution fusion | flops 547424640 | bytes 34698240 | tf_op jit(solution)/shard_map/while/body/eval_jaxpr/qhd,khd->hqk/dot_general | solution.py:76
  1130.1 39.3 %all-reduce.4 = (f32[512,8]{0,1:T(8,128)S(1)}, f32[4,512]{1,0:T(4,128)S(1)}) all-reduce(f32[512,8]{0,1:T(8,128)S(1)} %fusion.205, f32[4,512]{1,0:T(4,128)S(1)} %pad_maximum_fusion.4), channel_id=1, replica_groups=mesh['dp'=4,'expert'=8] {'dp','expert'}, use_global_device_ids=true, to_apply=%region_34.35 | all-reduce | flops 6144 | bytes 49152 | tf_op jit(solution)/shard_map/psum | solution.py:288
  1175.7 78.0 %all-reduce.10.cloned.1.call-done = (f32[512,1536]{1,0:T(8,128)}, f32[512,512]{1,0:T(8,128)}) async-done(((f32[512,1536]{1,0:T(8,128)}, f32[512,512]{1,0:T(8,128)}), (f32[512,1536]{1,0:T(8,128)}, f32[512,512]{1,0:T(8,128)})) %all-reduce.10.cloned.1.call-update) | async-done | bytes 4194320 | tf_op jit(solution)/shard_map/psum | solution.py:288
  1268.7 39.2 %psum.55 = f32[]{:T(128)} all-reduce(f32[]{:T(128)S(6)} %add.312), channel_id=1, replica_groups=mesh['dp'=4,'expert'=8] {'dp','expert'}, use_global_device_ids=true, to_apply=%region_46.47 | all-reduce | flops 1 | bytes 8 | tf_op jit(solution)/shard_map/psum | solution.py:302
  (459 shorter events, 684.3 us)
Async XLA Ops:
  7.2 22.1 %copy-start.21 = (f32[128,512]{1,0:T(8,128)S(1)}, f32[128,512]{1,0:T(8,128)}, u32[]{:S(2)}) copy-start(f32[128,512]{1,0:T(8,128)} %param.27) | copy-start | bytes 786436
  7.2 43.5 %copy-start.55 = (s32[1,5760]{1,0:T(1,128)S(1)}, s32[1,5760]{1,0:T(1,128)}, u32[]{:S(2)}) copy-start(s32[1,5760]{1,0:T(1,128)} %param.24) | copy-start | bytes 69124
  7.2 172.2 %all-gather.5.cloned.1.call-start = ((), (), s32[]{:S(2)}) async-start(), calls=%async_computation.4 | async-start | bytes 1966080 | tf_op jit(solution)/shard_map/all_gather | solution.py:183
  9.4 340.9 %all-gather.7.cloned.1.call-start = ((), (), s32[]{:S(2)}) async-start(), calls=%async_computation.5 | async-start | bytes 2621440 | tf_op jit(solution)/shard_map/all_gather | solution.py:187
  15.2 161.6 %copy-start.24 = (f32[2880]{0:T(1024)}, f32[2880]{0:T(1024)S(1)}, u32[]{:S(2)}) copy-start(f32[2880]{0:T(1024)S(1)} %broadcast_multiply_fusion.2) | copy-start | bytes 34564
  16.5 62.0 %copy-start.41 = (f32[2880]{0:T(1024)}, f32[2880]{0:T(1024)S(1)}, u32[]{:S(2)}) copy-start(f32[2880]{0:T(1024)S(1)} %fusion.68) | copy-start | bytes 34564
  16.6 160.2 %copy-start.35 = (f32[2880]{0:T(1024)}, f32[2880]{0:T(1024)S(1)}, u32[]{:S(2)}) copy-start(f32[2880]{0:T(1024)S(1)} %fusion.117) | copy-start | bytes 34564
  29.3 147.4 %copy-start.50 = (f32[1,512]{1,0:T(1,128)}, f32[1,512]{1,0:T(1,128)S(1)}, u32[]{:S(2)}) copy-start(f32[1,512]{1,0:T(1,128)S(1)} %get-tuple-element.282) | copy-start | bytes 6148
  29.3 302.6 %copy-start.53 = (f32[1,512]{1,0:T(1,128)}, f32[1,512]{1,0:T(1,128)S(1)}, u32[]{:S(2)}) copy-start(f32[1,512]{1,0:T(1,128)S(1)} %get-tuple-element.280) | copy-start | bytes 6148
  147.7 35.1 %copy-start.28 = (s32[5760]{0:T(1024)}, s32[5760]{0:T(1024)S(1)}, u32[]{:S(2)}) copy-start(s32[5760]{0:T(1024)S(1)} %gather_fusion.1) | copy-start | bytes 69124
  176.7 158.5 %copy-start.45 = (s32[3072]{0:T(1024)}, s32[3072]{0:T(1024)S(1)}, u32[]{:S(2)}) copy-start(s32[3072]{0:T(1024)S(1)} %get-tuple-element.288) | copy-start | bytes 36868
  344.7 40.4 %all-to-all-start = ((bf16[8,360,512]{2,1,0:T(8,128)(2,1)}), bf16[8,360,512]{2,1,0:T(8,128)(2,1)}, u32[]{:S(2)}, u32[]{:S(2)}) async-start(bf16[8,360,512]{2,1,0:T(8,128)(2,1)} %bitcast.383), calls=%async_computation | async-start | bytes 5898240 | tf_op jit(solution)/shard_map/all_to_all | solution.py:218
  349.3 49.0 %all-gather.9.cloned.1.call-start = ((), (), s32[]{:S(2)}) async-start(), calls=%async_computation.6 | async-start | bytes 2621440 | tf_op jit(solution)/shard_map/all_gather | solution.py:188
  452.8 66.9 %all-to-all-start.1 = ((bf16[8,360,512]{2,1,0:T(8,128)(2,1)}), bf16[8,360,512]{2,1,0:T(8,128)(2,1)}, u32[]{:S(2)}, u32[]{:S(2)}) async-start(bf16[8,360,512]{2,1,0:T(8,128)(2,1)} %fusion.85), calls=%async_computation.1 | async-start | bytes 5898240 | tf_op jit(solution)/shard_map/all_to_all | solution.py:232
  469.4 49.3 %copy-start.48 = (bf16[8,512]{1,0:T(8,128)(2,1)}, bf16[8,512]{1,0:T(8,128)(2,1)S(1)}, u32[]{:S(2)}) copy-start(bf16[8,512]{1,0:T(8,128)(2,1)S(1)} %reshape.599) | copy-start | bytes 24580
  583.3 40.6 %all-to-all-start.2 = ((bf16[8,360,512]{2,1,0:T(8,128)(2,1)}), bf16[8,360,512]{2,1,0:T(8,128)(2,1)}, u32[]{:S(2)}, u32[]{:S(2)}) async-start(bf16[8,360,512]{2,1,0:T(8,128)(2,1)} %multiply_convert_fusion.3), calls=%async_computation.2 | async-start | bytes 5898240 | tf_op jit(solution)/shard_map/all_to_all | solution.py:248
  611.2 32.4 %copy-start.64 = (bf16[1,512,2048]{2,1,0:T(8,128)(2,1)S(1)}, bf16[1,512,2048]{2,1,0:T(8,128)(2,1)}, u32[]{:S(2)}) copy-start(bf16[1,512,2048]{2,1,0:T(8,128)(2,1)} %all-gather.7.cloned.1.call-done) | copy-start | bytes 6291460
  652.5 71.3 %all-to-all-start.3 = ((bf16[8,360,512]{2,1,0:T(8,128)(2,1)}), bf16[8,360,512]{2,1,0:T(8,128)(2,1)}, u32[]{:S(2)}, u32[]{:S(2)}) async-start(bf16[8,360,512]{2,1,0:T(8,128)(2,1)} %fusion.82), calls=%async_computation.3 | async-start | bytes 5898240 | tf_op jit(solution)/shard_map/all_to_all | solution.py:261
  656.9 513.6 %all-reduce.12.cloned.1.call-start = ((), (), s32[]{:S(2)}) async-start(), calls=%async_computation.8 | async-start | bytes 8388608 | tf_op jit(solution)/shard_map/psum | solution.py:290
  657.0 57.5 %copy-start.66 = (bf16[8,1,360,2048]{3,2,0,1:T(8,128)(2,1)S(1)}, bf16[8,1,360,2048]{3,2,0,1:T(8,128)(2,1)}, u32[]{:S(2)}) copy-start(bf16[8,1,360,2048]{3,2,0,1:T(8,128)(2,1)} %copy-done.65) | copy-start | bytes 35389444
  723.7 530.0 %all-reduce.10.cloned.1.call-start = ((), (), s32[]{:S(2)}) async-start(), calls=%async_computation.7 | async-start | bytes 8388608 | tf_op jit(solution)/shard_map/psum | solution.py:288
  1123.0 136.8 %copy-start.40 = (f32[2880]{0:T(1024)S(1)}, f32[2880]{0:T(1024)}, u32[]{:S(2)}) copy-start(f32[2880]{0:T(1024)} %copy-done.39) | copy-start | bytes 34564
  1268.7 44.5 %copy-start.17 = (f32[1,512,512]{2,1,0:T(8,128)S(1)}, f32[1,512,512]{2,1,0:T(8,128)}, u32[]{:S(2)}) copy-start(f32[1,512,512]{2,1,0:T(8,128)} %param.30) | copy-start | bytes 3145732
  1268.7 44.5 %copy-start.19 = (f32[2,1,512,512]{3,2,1,0:T(8,128)S(1)}, f32[2,1,512,512]{3,2,1,0:T(8,128)}, u32[]{:S(2)}) copy-start(f32[2,1,512,512]{3,2,1,0:T(8,128)} %param.36) | copy-start | bytes 6291460
  (96 other events, 907.3 us)
Sparse Core Ops, SparseCore 0:
  10.2 48.0 all-gather.4
  60.5 44.9 all-gather.6
  352.3 45.8 all-gather.8
  723.8 154.2 all-reduce.11
  1112.7 140.9 all-reduce.9
where the time goes:
time: 1340 us; the launch traced here: 1330 us
  matrix products  475 us (35%)
  local copies, waits for them, and re-layouts  340 us (25%)
  other arithmetic  224 us (17%)
  waiting for transfers between devices  126 us (9%)
  blocking collectives  124 us (9%)
  between operations  21.5 us (2%)
  starting transfers between devices  18.8 us (1%)
    psum x1, waiting for transfers between devices, shards(): lax.psum((grad_qkv, grad_out, grad_router, grad_norms), ('dp', 'expert'))  78 us
    dot_general x4, matrix products, attend_backward(): jnp.einsum('qhd,khd->hqk', grad_context, values_all, preferred_element_ty...  59.9 us
    dot_general x1, matrix products, shards(): jnp.einsum('slcf,slcd->lfd', act_grid, grad_grid, preferred_element_type=...  57.5 us
    dot_general x1, matrix products, shards(): jnp.einsum('slcf,lfd->slcd', act_b, exp_w, preferred_element_type=jnp.flo...  54.5 us
    psum x1, blocking collectives, shards(): lax.psum((grad_qkv, grad_out, grad_router, grad_norms), ('dp', 'expert'))  39.3 us
    psum x1, blocking collectives, shards(): grad_norm = jnp.sqrt(lax.psum(term, ('dp', 'expert')))  39.2 us
    dot_general x4, matrix products, attend_forward(): jnp.einsum('hqk,khd->qhd', probs_b, values_all, preferred_element_type=jn...  37 us
    reduce_sum x4, other arithmetic, attend_forward(): jnp.sum(jnp.exp(scores - row_top), axis=-1, keepdims=True)  36.1 us
  transfers between devices with their start and end apart: 9, of which 3 were waited for; matrix products, arithmetic and copies ran while one was open for 64% of the time, Pallas kernels for 0%

commit v1 on v0

v1 whole, which is shorter than its diff:
```python
import functools

import jax
import jax.numpy as jnp
from jax import lax
from jax.experimental import pallas as pl
from jax.experimental.pallas import tpu as pltpu
from jax.sharding import PartitionSpec as P

D = 512
HEADS = 8
HEAD = 64
FF = 2048
SEQ = 720

EPS_NORM = 1e-06
BETA_ONE = 0.9
BETA_TWO = 0.999
ADAM_EPS = 1e-08
DECAY_RATE = 0.1
MAX_NORM = 1.0

f32, bf16, i32 = jnp.float32, jnp.bfloat16, jnp.int32
NN = (((1,), (0,)), ((), ()))
NT = (((1,), (1,)), ((), ()))
TN = (((0,), (0,)), ((), ()))
LOG2E = 1.4426950408889634
SCALE = HEAD**-0.5
FAR = 1 << 20
VMEM_LIMIT = 60 * 2**20


def mm(a, b, dims=NN):
    return lax.dot_general(a, b, dims, preferred_element_type=f32)


def full(a):
    return pl.BlockSpec(a.shape, lambda *i: (0,) * a.ndim)


def whole(*shape):
    return pl.BlockSpec(shape, lambda *i: (0,) * len(shape))


def per_image(cols):
    return pl.BlockSpec((SEQ, cols), lambda i: (i, 0))


def per_image_t(rows):
    return pl.BlockSpec((1, rows, SEQ), lambda i: (i, 0, 0))


def sds(shape, dtype):
    return jax.ShapeDtypeStruct(shape, dtype)


def call(body, name, cost, **kw):
    flops, moved = cost
    return pl.pallas_call(
        body,
        name=name,
        compiler_params=pltpu.CompilerParams(vmem_limit_bytes=VMEM_LIMIT),
        cost_estimate=pl.CostEstimate(
            flops=int(flops), bytes_accessed=int(moved), transcendentals=0
        ),
        **kw,
    )


def normalize(v):
    c = v - jnp.mean(v, axis=-1, keepdims=True)
    r = lax.rsqrt(jnp.mean(c * c, axis=-1, keepdims=True) + EPS_NORM)
    return c * r, r


def assemble_kernel(experts, where, own, r1, r2, r3, s1, s2, s3, wT, ow, rT, nm):
    me, core = where[0], where[1]
    per = experts // 4

    def put(d, hh, piece):
        wT[d * 384 + hh * 192 : d * 384 + hh * 192 + 192, :] = piece[:192, :]
        ow[d * 128 + hh * 64 : d * 128 + hh * 64 + 64, :] = piece[192:256, :]
        if hh == 0:
            misc = piece[256:272, :].astype(f32)
            rT[d * per : (d + 1) * per, :] = misc[:per, :]
            for j in range(4):
                nm[j : j + 1, d * 128 : (d + 1) * 128] = misc[
                    per : per + 1, j * 128 : (j + 1) * 128
                ]

    for d in range(4):
        for k in range(4):

            @pl.when((me ^ k) == d)
            def _(d=d, k=k):
                if k == 0:
                    put(d, 0, own[0])
                    put(d, 1, own[1])
                else:
                    mine = (r1, r2, r3)[k - 1]
                    other = (s1, s2, s3)[k - 1]

                    @pl.when(core == 0)
                    def _():
                        put(d, 0, mine)
                        put(d, 1, other)

                    @pl.when(core == 1)
                    def _():
                        put(d, 0, other)
                        put(d, 1, mine)


def assemble(where, own, got, sib, experts):
    args = (own, *got, *sib)
    return call(
        functools.partial(assemble_kernel, experts),
        "assemble",
        (1e6, 5e6),
        in_specs=[pl.BlockSpec(memory_space=pltpu.SMEM)] + [whole(*a.shape) for a in args],
        out_specs=[whole(3 * D, D), whole(D, D), whole(experts, D), whole(4, D)],
        out_shape=[
            sds((3 * D, D), bf16),
            sds((D, D), bf16),
            sds((experts, D), f32),
            sds((4, D), f32),
        ],
    )(where, *args)


def dispatch(pos, x, u, pad, step):
    io = lax.broadcasted_iota(i32, (pad, SEQ), 0)
    acc = None
    for i in range(pos.shape[0]):
        hit = jnp.where(io == pos[i, pl.ds(step, 1), :], 1.0, 0.0).astype(bf16)
        part = mm(hit, x[i * SEQ : (i + 1) * SEQ, :])
        acc = part if acc is None else acc + part
    u[0] = acc.astype(bf16)


def slots_kernel(cap, pad, ids, prio, cot, pos, cols, u):
    step = pl.program_id(0)
    n = ids.shape[0]
    experts = pos.shape[1]
    nh = -(-(2 * n * SEQ) // 2048) * 16

    @pl.when(step == 0)
    def _():
        hi_io = lax.broadcasted_iota(i32, (nh, SEQ), 0)
        lo_io = lax.broadcasted_iota(i32, (128, SEQ), 0)

        def hot(i, k):
            q = prio[i, k : k + 1, :]
            return hi_io == (q >> 7), lo_io == (q & 127)

        table = jnp.zeros((nh, 128), f32)
        for i in range(n):
            for k in range(2):
                a, b = hot(i, k)
                ex = (ids[i, k : k + 1, :] + 1).astype(f32)
                table += mm(
                    jnp.where(a, 1.0, 0.0).astype(bf16), jnp.where(b, ex, 0.0).astype(bf16), NT
                )
        upper = (
            lax.broadcasted_iota(i32, (128, 128), 0) < lax.broadcasted_iota(i32, (128, 128), 1)
        ).astype(bf16)
        lower = (
            lax.broadcasted_iota(i32, (nh, nh), 1) < lax.broadcasted_iota(i32, (nh, nh), 0)
        ).astype(bf16)
        ones = jnp.ones((128, 128), bf16)
        rank = jnp.zeros((nh, 128), f32)
        for e in range(experts):
            m = (table == float(e + 1)).astype(f32)
            mb = m.astype(bf16)
            rank += m * (mm(mb, upper) + mm(mm(lower, mb).astype(bf16), ones))
        ri = jnp.minimum(rank.astype(i32), 16383)
        rlo = (ri & 127).astype(bf16)
        rhi = (ri >> 7).astype(bf16)
        eio = lax.broadcasted_iota(i32, (experts, SEQ), 0)
        for i in range(n):
            out = jnp.full((experts, SEQ), FAR, i32)
            flat = []
            for k in range(2):
                a, b = hot(i, k)
                bb = jnp.where(b, 1.0, 0.0).astype(bf16)
                x = mm(rlo, bb) + 128.0 * mm(rhi, bb)
                r = jnp.sum(jnp.where(a, x, 0.0), axis=0, keepdims=True).astype(i32)
                ex = ids[i, k : k + 1, :]
                keep = r < cap
                out = jnp.where((eio == ex) & keep, r, out)
                flat.append(jnp.where(keep, ex * pad + r, FAR))
            pos[i] = out
            fl = jnp.concatenate(flat + [jnp.zeros((6, SEQ), i32)], axis=0).astype(f32)
            cols[i * SEQ : (i + 1) * SEQ, :] = fl.T.astype(i32)

    dispatch(pos, cot, u, pad, step)


def slots(ids, prio, cot, experts, cap, pad):
    n = ids.shape[0]
    t = n * SEQ
    return call(
        functools.partial(slots_kernel, cap, pad),
        "slots",
        (12e9, 8e6),
        grid=(experts,),
        in_specs=[full(ids), full(prio), full(cot)],
        out_specs=[
            whole(n, experts, SEQ),
            whole(t, 8),
            pl.BlockSpec((1, pad, D), lambda e: (e, 0, 0)),
        ],
        out_shape=[
            sds((n, experts, SEQ), i32),
            sds((t, 8), i32),
            sds((experts, pad, D), bf16),
        ],
    )(ids, prio, cot)


def spread_kernel(pad, pos, x, u):
    dispatch(pos, x, u, pad, pl.program_id(0))


def spread(pos, x, pad):
    experts = pos.shape[1]
    return call(
        functools.partial(spread_kernel, pad),
        "spread",
        (9e9, 6e6),
        grid=(experts,),
        in_specs=[full(pos), full(x)],
        out_specs=pl.BlockSpec((1, pad, D), lambda e: (e, 0, 0)),
        out_shape=sds((experts, pad, D), bf16),
    )(pos, x)


def head_masks():
    lane = lax.broadcasted_iota(i32, (1, 128), 1)
    return (lane < 64).astype(bf16), (lane >= 64).astype(bf16)


def attend_kernel(tok, wT, ow, rT, nm, proj, ctxT, lse, mid, sec, gatesT, vT, ct):
    x = tok[...].astype(f32)
    xh, _ = normalize(x)
    fb = (xh * nm[0:1, :] + nm[1:2, :]).astype(bf16)
    proj[...] = mm(fb, wT[...], NT).astype(bf16)
    vT[...] = proj[:, 2 * D :].T
    masks = head_masks()
    for h in range(HEADS):
        p = h // 2
        qm = proj[:, p * 128 : (p + 1) * 128] * masks[h % 2]
        kk = proj[:, D + p * 128 : D + (p + 1) * 128]
        s = mm(kk, qm, NT)
        m = jnp.max(s, axis=0, keepdims=True)
        e = jnp.exp2((s - m) * (SCALE * LOG2E))
        total = jnp.sum(e, axis=0, keepdims=True)
        c = mm(vT[h * 64 : (h + 1) * 64, :], e.astype(bf16))
        ct[h * 64 : (h + 1) * 64, :] = (c * (1.0 / total)).astype(bf16)
        lse[0, h : h + 1, :] = m * (SCALE * LOG2E) + jnp.log2(total)
    ctxT[0] = ct[...]
    middle = x + mm(ct[...], ow[...], TN)
    mid[...] = middle
    xh2, _ = normalize(middle)
    s2 = (xh2 * nm[2:3, :] + nm[3:4, :]).astype(bf16)
    sec[...] = s2
    logits = mm(rT[...].astype(bf16), s2, NT)
    ex = jnp.exp(logits - jnp.max(logits, axis=0, keepdims=True))
    gatesT[0] = ex / jnp.sum(ex, axis=0, keepdims=True)


def attend(tok, wT, ow, rT, nm):
    t = tok.shape[0]
    n = t // SEQ
    experts = rT.shape[0]
    return call(
        attend_kernel,
        "attend",
        (45e9, 30e6),
        grid=(n,),
        in_specs=[per_image(D), full(wT), full(ow), full(rT), full(nm)],
        out_specs=[
            per_image(3 * D),
            per_image_t(D),
            per_image_t(HEADS),
            per_image(D),
            per_image(D),
            per_image_t(experts),
        ],
        out_shape=[
            sds((t, 3 * D), bf16),
            sds((n, D, SEQ), bf16),
            sds((n, HEADS, SEQ), f32),
            sds((t, D), f32),
            sds((t, D), bf16),
            sds((n, experts, SEQ), f32),
        ],
        scratch_shapes=[pltpu.VMEM((D, SEQ), bf16), pltpu.VMEM((D, SEQ), bf16)],
    )(tok, wT, ow, rT, nm)


def normal_cdf(h):
    t = 1.0 / (1.0 + (0.3275911 * 0.7071067811865476) * jnp.abs(h))
    g = jnp.exp2((-0.5 * LOG2E) * h * h)
    poly = t * (
        0.5 * 0.254829592
        + t
        * (
            0.5 * -0.284496736
            + t * (0.5 * 1.421413741 + t * (0.5 * -1.453152027 + t * (0.5 * 1.061405429)))
        )
    )
    q = poly * g
    return jnp.where(h >= 0, 1.0 - q, q), g


def experts_kernel(cap, where, rows, u, iw, xw, rT, gb, dr, din, dexpT):
    s = pl.program_id(0)
    x = rows[0]
    up = u[0]
    pad = x.shape[0]
    chunks = iw.shape[0]
    cols = iw.shape[2]
    logits = mm(x, rT[...].astype(bf16), NT)
    ex = jnp.exp(logits - jnp.max(logits, axis=1, keepdims=True))
    mine = lax.broadcasted_iota(i32, ex.shape, 1) == where[2]
    gate = jnp.sum(jnp.where(mine, ex, 0.0), axis=1, keepdims=True) / jnp.sum(
        ex, axis=1, keepdims=True
    )
    upf = up.astype(f32)
    db = (gate * upf).astype(bf16)
    back = None
    drow = None
    for j in range(chunks):
        h = mm(x, iw[j])
        cdf, g = normal_cdf(h)
        act = (h * cdf).astype(bf16)
        part = mm(act, xw[j])
        back = part if back is None else back + part
        dact = mm(db, xw[j], NT)
        dh = (dact * (cdf + h * g * 0.3989422804014327)).astype(bf16)
        part = mm(dh, iw[j], NT)
        drow = part if drow is None else drow + part
        di = mm(x, dh, TN)
        de = mm(db, act, TN)

        @pl.when(s == 0)
        def _(j=j, di=di, de=de):
            din[j] = di
            dexpT[j] = de

        @pl.when(s > 0)
        def _(j=j, di=di, de=de):
            din[j] += di
            dexpT[j] += de

    b = back.astype(bf16).astype(f32)
    gb[0] = (gate * b).astype(bf16)
    prod = upf * b
    first = prod.astype(bf16)
    rest = (prod - first.astype(f32)).astype(bf16)
    ones = jnp.ones((8, D), bf16)
    dg = (mm(ones, first, NT) + mm(ones, rest, NT))[0:1, :]
    dg = jnp.concatenate([dg, jnp.zeros((1, D - pad), f32)], axis=1)
    dg_first = dg.astype(bf16).astype(f32)
    line = lax.broadcasted_iota(i32, (pad, D), 0)
    drow = jnp.where(line == cap, dg_first, jnp.where(line == cap + 1, dg - dg_first, drow))
    dr[0] = drow.astype(bf16)


def run_experts(where, rows, u, iw, xw, rT, cap):
    groups, pad, _ = rows.shape
    chunks, _, cols = iw.shape
    blk = pl.BlockSpec((1, pad, D), lambda i: (i, 0, 0))
    return call(
        functools.partial(experts_kernel, cap),
        "experts",
        (70e9, 25e6),
        grid=(groups,),
        in_specs=[pl.BlockSpec(memory_space=pltpu.SMEM), blk, blk, full(iw), full(xw), full(rT)],
        out_specs=[blk, blk, whole(chunks, D, cols), whole(chunks, D, cols)],
        out_shape=[sds((groups, pad, D), bf16)] * 2 + [sds((chunks, D, cols), f32)] * 2,
    )(where, rows, u, iw, xw, rT)


def pick(cols, count):
    io = lax.broadcasted_iota(i32, (SEQ, count), 1)
    return jnp.where((io == cols[:, 0:1]) | (io == cols[:, 1:2]), 1.0, 0.0).astype(bf16)


def combine_kernel(cap, experts, dr, cols, gatesT, sec, mid, cot, rT, nm, dmid, dn, drT):
    i = pl.program_id(0)
    pad = dr.shape[0] // experts
    hits = pick(cols[...], dr.shape[0])
    ds = mm(hits, dr[...])
    base = cap // 16 * 16
    off = cap - base
    width = -(-pad // 128) * 128
    dg = []
    for e in range(experts):
        two = dr[e * pad + base : (e + 1) * pad, :pad]
        x = mm(two, hits[:, e * pad : (e + 1) * pad], NT)
        dg.append(x[off : off + 1, :] + x[off + 1 : off + 2, :])
    dg = jnp.concatenate(dg, axis=0)
    g = gatesT[0]
    dl = (g * (dg - jnp.sum(g * dg, axis=0, keepdims=True))).astype(bf16)
    ds = ds + mm(dl, rT[...].astype(bf16), TN)
    xh, r = normalize(mid[...])
    y = ds * nm[2:3, :]
    dmid[...] = cot[...].astype(f32) + r * (
        y - jnp.mean(y, axis=-1, keepdims=True) - xh * jnp.mean(y * xh, axis=-1, keepdims=True)
    )
    gg = jnp.sum(ds * xh, axis=0, keepdims=True)
    gs = jnp.sum(ds, axis=0, keepdims=True)
    dR = mm(dl, sec[...])

    @pl.when(i == 0)
    def _():
        dn[0:1, :] = gg
        dn[1:2, :] = gs
        drT[...] = dR

    @pl.when(i > 0)
    def _():
        dn[0:1, :] += gg
        dn[1:2, :] += gs
        drT[...] += dR


def combine(dr, cols, gatesT, sec, mid, cot, rT, nm, cap):
    experts, pad, _ = dr.shape
    t = cols.shape[0]
    n = t // SEQ
    dr = dr.reshape(experts * pad, D)
    return call(
        functools.partial(combine_kernel, cap, experts),
        "combine",
        (20e9, 25e6),
        grid=(n,),
        in_specs=[
            full(dr),
            per_image(8),
            per_image_t(experts),
            per_image(D),
            per_image(D),
            per_image(D),
            full(rT),
            full(nm),
        ],
        out_specs=[per_image(D), whole(2, D), whole(experts, D)],
        out_shape=[sds((t, D), f32), sds((2, D), f32), sds((experts, D), f32)],
    )(dr, cols, gatesT, sec, mid, cot, rT, nm)


def finish_kernel(gb, cols, mid, out):
    out[...] = (mid[...] + mm(pick(cols[...], gb.shape[0]), gb[...])).astype(bf16)


def finish(gb, cols, mid):
    experts, pad, _ = gb.shape
    t = cols.shape[0]
    gb = gb.reshape(experts * pad, D)
    return call(
        finish_kernel,
        "finish",
        (10e9, 12e6),
        grid=(t // SEQ,),
        in_specs=[full(gb), per_image(8), per_image(D)],
        out_specs=per_image(D),
        out_shape=sds((t, D), bf16),
    )(gb, cols, mid)


def attend_back_kernel(
    tok, dmid, proj, ctxT, lse, wT, ow, nm, gin, dqkv, dout, dn, kT, dqT, dp
):
    i = pl.program_id(0)
    da = dmid[...].astype(bf16)
    do = mm(da, ow[...], NT).astype(bf16)
    doT = mm(ow[...], da, NT).astype(bf16)
    prod = doT.astype(f32) * ctxT[0].astype(f32)
    kT[...] = proj[:, D : 2 * D].T
    masks = head_masks()
    low = lax.broadcasted_iota(i32, (SEQ, 128), 1) < 64
    for p in range(HEADS // 2):
        dv = []
        dk = []
        qq = proj[:, p * 128 : (p + 1) * 128]
        kk = proj[:, D + p * 128 : D + (p + 1) * 128]
        vv = proj[:, 2 * D + p * 128 : 2 * D + (p + 1) * 128]
        dd = do[:, p * 128 : (p + 1) * 128]
        for j in range(2):
            h = 2 * p + j
            s = mm(kk, qq * masks[j], NT)
            prob = jnp.exp2(s * (SCALE * LOG2E) - lse[0, h : h + 1, :])
            dprob = mm(vv, dd * masks[j], NT)
            dv.append(mm(prob.astype(bf16), dd))
            inner = jnp.sum(prod[h * 64 : (h + 1) * 64, :], axis=0, keepdims=True)
            ds = (prob * (dprob - inner)).astype(bf16)
            dk.append(mm(ds, qq))
            dqT[h * 64 : (h + 1) * 64, :] = (
                mm(kT[h * 64 : (h + 1) * 64, :], ds) * SCALE
            ).astype(bf16)
        lo = p * 128
        dp[:, 2 * D + lo : 2 * D + lo + 128] = jnp.where(low, dv[0], dv[1]).astype(bf16)
        dp[:, D + lo : D + lo + 128] = (jnp.where(low, dk[0], dk[1]) * SCALE).astype(bf16)
    dp[:, :D] = dqT[...].T
    dproj = dp[...]
    xh, r = normalize(tok[...].astype(f32))
    fb = (xh * nm[0:1, :] + nm[1:2, :]).astype(bf16)
    gq = mm(fb, dproj, TN)
    go = mm(ctxT[0], da)
    df = mm(dproj, wT[...])
    y = df * nm[0:1, :]
    gin[...] = dmid[...] + r * (
        y - jnp.mean(y, axis=-1, keepdims=True) - xh * jnp.mean(y * xh, axis=-1, keepdims=True)
    )
    gg = jnp.sum(df * xh, axis=0, keepdims=True)
    gs = jnp.sum(df, axis=0, keepdims=True)

    @pl.when(i == 0)
    def _():
        dqkv[...] = gq
        dout[...] = go
        dn[0:1, :] = gg
        dn[1:2, :] = gs

    @pl.when(i > 0)
    def _():
        dqkv[...] += gq
        dout[...] += go
        dn[0:1, :] += gg
        dn[1:2, :] += gs


def attend_back(tok, dmid, proj, ctxT, lse, wT, ow, nm):
    t = tok.shape[0]
    n = t // SEQ
    return call(
        attend_back_kernel,
        "attend_back",
        (80e9, 40e6),
        grid=(n,),
        in_specs=[
            per_image(D),
            per_image(D),
            per_image(3 * D),
            per_image_t(D),
            per_image_t(HEADS),
            full(wT),
            full(ow),
            full(nm),
        ],
        out_specs=[per_image(D), whole(D, 3 * D), whole(D, D), whole(2, D)],
        out_shape=[
            sds((t, D), f32),
            sds((D, 3 * D), f32),
            sds((D, D), f32),
            sds((2, D), f32),
        ],
        scratch_shapes=[
            pltpu.VMEM((D, SEQ), bf16),
            pltpu.VMEM((D, SEQ), bf16),
            pltpu.VMEM((SEQ, 3 * D), bf16),
        ],
    )(tok, dmid, proj, ctxT, lse, wT, ow, nm)


def step_rates(experts):
    return (
        D ** (-0.5),
        2.0 ** (-0.5),
        (2 * D) ** (-0.5),
        0.1,
        D ** (-0.5),
        2.0 * experts / (1.2 * FF**0.5),
    )


def adam_update(weight, moments, grad, factor, rate, decay, step_float):
    clipped = grad * factor
    first = BETA_ONE * moments[0] + (1.0 - BETA_ONE) * clipped
    second = BETA_TWO * moments[1] + (1.0 - BETA_TWO) * clipped * clipped
    fix_one = 1.0 - jnp.power(BETA_ONE, step_float)
    fix_two = 1.0 - jnp.power(BETA_TWO, step_float)
    updated = weight - rate * (
        first / fix_one / (jnp.sqrt(second / fix_two) + ADAM_EPS) + decay * weight
    )
    return (updated, first, second, updated.astype(bf16))


def square_sum(arrays):
    total = jnp.zeros((), f32)
    for member in arrays:
        total = total + jnp.sum(member * member)
    return total


def swap(x, axis, k):
    n = lax.axis_size(axis)
    return lax.ppermute(x, axis, [(i, i ^ k) for i in range(n)])


def exchange(x, axis):
    return lax.all_to_all(x, axis, split_axis=0, concat_axis=0, tiled=True)


def shards(
    tokens,
    cotangent,
    expert_ids,
    priority,
    step,
    attn_qkv,
    attn_out,
    router,
    norms,
    expert_in,
    expert_out,
    moments_qkv,
    moments_out,
    moments_router,
    moments_norms,
    moments_in,
    moments_exp,
):
    tok_dev = tokens.shape[0]
    groups = lax.axis_size("expert")
    n_dp = lax.axis_size("dp")
    assert expert_in.shape[0] == 1 and n_dp == 4 and tok_dev % SEQ == 0
    experts = groups
    per = experts // n_dp
    cap = (tok_dev + experts - 1) // experts
    pad = -(-(cap + 2) // 16) * 16
    n = tok_dev // SEQ
    devices = n_dp * groups
    me_dp = lax.axis_index("dp").astype(i32)
    me_e = lax.axis_index("expert").astype(i32)
    core = me_e % 2
    where = jnp.stack([me_dp, core, me_e])

    qkvT = attn_qkv.astype(bf16).T
    ob = attn_out.astype(bf16)
    misc = jnp.concatenate(
        [
            router.astype(bf16).T,
            norms.astype(bf16).reshape(1, D),
            jnp.zeros((16 - per - 1, D), bf16),
        ],
        axis=0,
    )
    own = jnp.stack(
        [jnp.concatenate([qkvT[:192], ob[:64], misc]), jnp.concatenate([qkvT[192:], ob[64:], misc])]
    )
    half = lax.dynamic_index_in_dim(own, core, 0, keepdims=False)
    got = [swap(half, "dp", k) for k in (1, 2, 3)]
    sib = [swap(g, "expert", 1) for g in got]
    wT, ow, rT, nm = assemble(where, own, got, sib, experts)

    own_in = expert_in[0].astype(bf16)
    own_exp = expert_out[0].astype(bf16)
    iw = jnp.stack([own_in] + [swap(own_in, "dp", k) for k in (1, 2, 3)])
    xw = jnp.stack([own_exp] + [swap(own_exp, "dp", k) for k in (1, 2, 3)])

    ids = expert_ids.reshape(n, SEQ, 2).transpose(0, 2, 1)
    prio = priority.reshape(n, SEQ, 2).transpose(0, 2, 1)
    pos, cols, up_slots = slots(ids, prio, cotangent, experts, cap, pad)
    up = exchange(up_slots, "expert")
    proj, ctxT, lse, mid, sec, gatesT = attend(tokens, wT, ow, rT, nm)
    rows = exchange(spread(pos, sec, pad), "expert")
    gb, dr, din, dexpT = run_experts(where, rows, up, iw, xw, rT, cap)
    dr = exchange(dr, "expert")
    gb = exchange(gb, "expert")
    dmid, dn_two, drT = combine(dr, cols, gatesT, sec, mid, cotangent, rT, nm, cap)
    grad_input, dqkv, dout, dn_one = attend_back(tokens, dmid, proj, ctxT, lse, wT, ow, nm)
    activations = finish(gb, cols, mid)

    share_in = din[0]
    share_expT = dexpT[0]
    for k in (1, 2, 3):
        share_in = share_in + swap(din[k].astype(bf16), "dp", k).astype(f32)
        share_expT = share_expT + swap(dexpT[k].astype(bf16), "dp", k).astype(f32)
    share_exp = share_expT.T

    dn = jnp.concatenate([dn_one, dn_two], axis=0)
    blocks = []
    for d in range(n_dp):
        rws = [dqkv[:, d * 384 + j * 128 : d * 384 + (j + 1) * 128] for j in range(3)]
        rws += [dout[d * 128 : (d + 1) * 128, j * 128 : (j + 1) * 128] for j in range(4)]
        rws += [drT[d * per : (d + 1) * per, j * 128 : (j + 1) * 128] for j in range(4)]
        rws += [dn[:, d * 128 : (d + 1) * 128]]
        blocks.append(jnp.concatenate(rws, axis=0))
    used = blocks[0].shape[0]
    piece = -(-used // (groups * 16)) * 16
    packed = jnp.stack(blocks).astype(bf16)
    packed = jnp.pad(packed, ((0, 0), (0, groups * piece - used), (0, 0)))
    packed = packed.reshape(n_dp, groups, piece, 128).transpose(1, 0, 2, 3)
    packed = exchange(packed, "expert").astype(f32).sum(0).astype(bf16)
    packed = exchange(packed, "dp").astype(f32).sum(0)
    term = square_sum((packed, share_in, share_expT))
    packed = exchange(
        jnp.broadcast_to(packed.astype(bf16)[None], (groups, piece, 128)), "expert"
    )
    packed = packed.reshape(groups * piece, 128).astype(f32)
    share_qkv = jnp.concatenate([packed[j * 512 : (j + 1) * 512] for j in range(3)], axis=1)
    at = 1536
    share_out = jnp.concatenate(
        [packed[at + j * 128 : at + (j + 1) * 128] for j in range(4)], axis=1
    )
    at += 512
    share_router = jnp.concatenate(
        [packed[at + j * per : at + (j + 1) * per] for j in range(4)], axis=1
    ).T
    at += 4 * per
    share_norms = packed[at : at + 4]

    terms = exchange(jnp.full((devices, 1, 128), term, f32), ("dp", "expert"))
    grad_norm = jnp.sqrt(jnp.sum(terms[:, 0, 0]))
    factor = MAX_NORM / grad_norm
    rates = step_rates(experts)
    step_float = step.astype(f32)
    outs = [activations, grad_input, grad_norm]
    outs += adam_update(
        attn_qkv, moments_qkv, share_qkv, factor, rates[0], DECAY_RATE, step_float
    )
    outs += adam_update(
        attn_out, moments_out, share_out, factor, rates[1], DECAY_RATE, step_float
    )
    outs += adam_update(
        router, moments_router, share_router, factor, rates[2], DECAY_RATE, step_float
    )
    outs += adam_update(norms, moments_norms, share_norms, factor, rates[3], 0.0, step_float)
    outs += adam_update(
        expert_in, moments_in, share_in[None], factor, rates[4], DECAY_RATE, step_float
    )
    outs += adam_update(
        expert_out, moments_exp, share_exp[None], factor, rates[5], DECAY_RATE, step_float
    )
    return tuple(outs)


def solution(mesh):
    tok = P(("dp", "expert"), None)
    cols = P(None, "dp")
    rows = P("dp", None)
    e_in = P("expert", None, "dp")
    e_out = P("expert", "dp", None)
    in_specs = (
        tok,
        tok,
        tok,
        tok,
        P(),
        cols,
        rows,
        cols,
        cols,
        e_in,
        e_out,
        P(None, None, "dp"),
        P(None, "dp", None),
        P(None, None, "dp"),
        P(None, None, "dp"),
        P(None, "expert", None, "dp"),
        P(None, "expert", "dp", None),
    )
    out_specs = (
        (tok, tok, P())
        + (cols,) * 4
        + (rows,) * 4
        + (cols,) * 4
        + (cols,) * 4
        + (e_in,) * 4
        + (e_out,) * 4
    )
    return jax.shard_map(shards, mesh=mesh, in_specs=in_specs, out_specs=out_specs, check_vma=False)
```

time: 1340 us -> 662 us (0.49)
  matrix products: 475 us -> 0 us
  local copies, waits for them, and re-layouts: 340 us -> 43.8 us
  Pallas kernels: 0 us -> 267 us
  other arithmetic: 224 us -> 38.9 us
  starting transfers between devices: 18.8 us -> 58.7 us
  blocking collectives: 124 us -> 93.4 us
  waiting for transfers between devices: 126 us -> 147 us
  between operations: 21.5 us -> 6.25 us
    dot_general x61 -> x0, matrix products: 475 us -> none  [the longest x4 59.9 us: attend_backward(): jnp.einsum('qhd,khd->hqk', grad_context, values_all, preferred_element_ty...]
    pallas_call x0 -> x8, Pallas kernels: none -> 267 us  [the longest x1 79.8 us: run_experts(): call(functools.partial(experts_kernel, cap), 'experts', (70000000000.0, 2...]
    ppermute x0 -> x18, waiting for transfers between devices: none -> 147 us  [swap(): return lax.ppermute(x, axis, [(i, i ^ k) for i in range(n)])]
    gather x7 -> x0, local copies, waits for them, and re-layouts: 132 us -> none  [the longest x1 30 us: rank_in_expert(): return ordered_rank[pair_rank]]
    reduce_sum x21 -> x3, other arithmetic: 133 us -> 1.02 us  [the longest x1 0.63 us: shards(): grad_norm = jnp.sqrt(jnp.sum(terms[:, 0, 0]))]
    all_to_all x0 -> x3, blocking collectives: none -> 93.4 us  [exchange(): return lax.all_to_all(x, axis, split_axis=0, concat_axis=0, tiled=True)]
    psum x2 -> x0, blocking collectives: 78.5 us -> none  [the longest x1 39.3 us: shards(): lax.psum((grad_qkv, grad_out, grad_router, grad_norms), ('dp', 'expert'))]
    psum x2 -> x0, waiting for transfers between devices: 78 us -> none  [the longest x1 78 us: shards(): lax.psum((grad_qkv, grad_out, grad_router, grad_norms), ('dp', 'expert'))]
  transfers between devices with their start and end apart: 9 -> 23, of which waited for: 3 -> 10; matrix products, arithmetic and copies ran while one was open for 64% -> 10% of each run, Pallas kernels for 0% -> 13%
where the time goes in v1:
time: 662 us; the launch traced here: 656 us
  Pallas kernels  267 us (40%)
  waiting for transfers between devices  147 us (22%)
  blocking collectives  93.4 us (14%)
  starting transfers between devices  58.7 us (9%)
  local copies, waits for them, and re-layouts  43.8 us (7%)
  other arithmetic  38.9 us (6%)
    ppermute x18, waiting for transfers between devices, swap(): return lax.ppermute(x, axis, [(i, i ^ k) for i in range(n)])  147 us
    all_to_all x3, blocking collectives, exchange(): return lax.all_to_all(x, axis, split_axis=0, concat_axis=0, tiled=True)  93.4 us
    pallas_call x1, Pallas kernels, run_experts(): call(functools.partial(experts_kernel, cap), 'experts', (70000000000.0, 2...  79.8 us
    pallas_call x1, Pallas kernels, attend_back(): call(attend_back_kernel, 'attend_back', (80000000000.0, 40000000.0), grid...  69.5 us
    pallas_call x1, Pallas kernels, attend(): call(attend_kernel, 'attend', (45000000000.0, 30000000.0), grid=(n,), in_...  40.6 us
    all_to_all x5, starting transfers between devices, exchange(): return lax.all_to_all(x, axis, split_axis=0, concat_axis=0, tiled=True)  32.1 us
    pallas_call x1, Pallas kernels, combine(): call(functools.partial(combine_kernel, cap, experts), 'combine', (2000000...  30.1 us
    unnamed x76, local copies, waits for them, and re-layouts  27.9 us
  transfers between devices with their start and end apart: 23, of which 10 were waited for; matrix products, arithmetic and copies ran while one was open for 10% of the time, Pallas kernels for 13%

profile of v1, /device:TPU:0, one launch (start us, length us, event | category | flops | bytes accessed | tf_op | source)
XLA Modules:
  0.0 655.7 jit_solution(12540779465099686851)
XLA Ops:
  12.8 5.9 collective-permute-done.r1
  18.7 10.6 %collective-permute-done.1.r2 = bf16[272,512]{1,0:T(8,128)(2,1)S(1)} collective-permute-done((bf16[272,512]{1,0:T(8,128)(2,1)S(1)}, bf16[272,512]{1,0:T(8,128)(2,1)S(1)}, u32[]{:S(2)}, u32[]{:S(2)}) %collective-permute-start.1) | collective-permute-done | bytes 278560 | tf_op jit(solution)/shard_map/ppermute | solution.py:601
  29.8 16.6 %slots.1 = (s32[4,8,720]{2,1,0:T(8,128)}, s32[2880,8]{1,0:T(8,128)}, bf16[8,368,512]{2,1,0:T(8,128)(2,1)}) custom-call(s32[4,2,720]{2,1,0:T(2,128)} %bitcast.189, s32[4,2,720]{2,1,0:T(2,128)} %bitcast.190, bf16[2880,512]{1,0:T(8,128)(2,1)} %cot.3), custom_call_target="tpu_custom_call" | custom-call | flops 12000000000 | bytes 8000000 | tf_op jit(solution)/shard_map/slots/pallas_call | solution.py:202
  57.2 40.6 %attend.1 = (bf16[2880,1536]{1,0:T(8,128)(2,1)}, bf16[4,512,720]{2,1,0:T(8,128)(2,1)}, f32[4,8,720]{2,1,0:T(8,128)}, f32[2880,512]{1,0:T(8,128)}, bf16[2880,512]{1,0:T(8,128)(2,1)}, /*index=5*/f32[4,8,720]{2,1,0:T(8,128)}) custom-call(bf16[2880,512]{1,0:T(8,128)(2,1)} %tok.3, bf16[1536,512]{1,0:T(8,128)(2,1)} %get-tuple-element.52.wT, ...), custom_call_target="tpu_custom_call" | custom-call | flops 44999999488 | bytes 30000000 | tf_op jit(solution)/shard_map/attend/pallas_call | solution.py:276
  97.8 13.4 %spread.1 = bf16[8,368,512]{2,1,0:T(8,128)(2,1)} custom-call(s32[4,8,720]{2,1,0:T(8,128)} %get-tuple-element.51.pos, bf16[2880,512]{1,0:T(8,128)(2,1)} %get-tuple-element.56.x.sec), custom_call_target="tpu_custom_call" | custom-call | flops 8999999488 | bytes 6000000 | tf_op jit(solution)/shard_map/spread/pallas_call | solution.py:227
  111.2 5.0 all-to-all-start
  116.4 4.8 collective-permute-start.6
  126.8 17.9 %collective-permute-done.6 = bf16[512,512]{1,0:T(8,128)(2,1)S(1)} collective-permute-done((bf16[512,512]{1,0:T(8,128)(2,1)S(1)}, bf16[512,512]{1,0:T(8,128)(2,1)S(1)}, u32[]{:S(2)}, u32[]{:S(2)}) %collective-permute-start.6) | collective-permute-done | bytes 524320 | tf_op jit(solution)/shard_map/ppermute | solution.py:601
  146.5 12.8 %collective-permute-done.7 = bf16[512,512]{1,0:T(8,128)(2,1)S(1)} collective-permute-done((bf16[512,512]{1,0:T(8,128)(2,1)S(1)}, bf16[512,512]{1,0:T(8,128)(2,1)S(1)}, u32[]{:S(2)}, u32[]{:S(2)}) %collective-permute-start.7) | collective-permute-done | bytes 524320 | tf_op jit(solution)/shard_map/ppermute | solution.py:601
  161.0 6.4 collective-permute-done.9
  167.4 36.9 %collective-permute-done.10 = bf16[512,512]{1,0:T(8,128)(2,1)S(1)} collective-permute-done((bf16[512,512]{1,0:T(8,128)(2,1)S(1)}, bf16[512,512]{1,0:T(8,128)(2,1)S(1)}, u32[]{:S(2)}, u32[]{:S(2)}) %collective-permute-start.10) | collective-permute-done | bytes 524320 | tf_op jit(solution)/shard_map/ppermute | solution.py:601
  205.9 79.8 %experts.1 = (bf16[8,368,512]{2,1,0:T(8,128)(2,1)}, bf16[8,368,512]{2,1,0:T(8,128)(2,1)}, f32[4,512,512]{2,1,0:T(8,128)}, f32[4,512,512]{2,1,0:T(8,128)}) custom-call(s32[3]{0:T(128)} %pad_add_fusion.where, bf16[8,368,512]{2,1,0:T(8,128)(2,1)} %all-to-all-done.rows, bf16[8,368,512]{2,1,0:T(8,128)(2,1)} %all-to-all-done.1.u, ...), custom_call_target="tpu_custom_call" | custom-call | flops 70000001024 | bytes 25000000 | tf_op jit(solution)/shard_map/experts/pallas_call | solution.py:375
  285.7 40.9 %all_to_all.40 = bf16[8,368,512]{2,1,0:T(8,128)(2,1)} all-to-all(bf16[8,368,512]{2,1,0:T(8,128)(2,1)} %get-tuple-element.61), channel_id=1, replica_groups=mesh['dp'=4,'expert'=8] {'expert'}, dimensions={0} | all-to-all | bytes 6029312 | tf_op jit(solution)/shard_map/all_to_all | solution.py:605
  326.6 30.1 %combine.1 = (f32[2880,512]{1,0:T(8,128)}, f32[2,512]{1,0:T(2,128)}, f32[8,512]{1,0:T(8,128)}) custom-call(bf16[2944,512]{1,0:T(8,128)(2,1)} %bitcast.173, s32[2880,8]{1,0:T(8,128)} %get-tuple-element.59.cols, f32[4,8,720]{2,1,0:T(8,128)} %get-tuple-element.62.gatesT, bf16[2880,512]{1,0:T(8,128)(2,1)} %get-tuple-element.56.x.sec, ...), custom_call_target="tpu_custom_call" | custom-call | flops 20000000000 | bytes 25000000 | tf_op jit(solution)/shard_map/combine/pallas_call | solution.py:435
  356.6 69.5 %attend_back.1 = (f32[2880,512]{1,0:T(8,128)}, f32[512,1536]{1,0:T(8,128)}, f32[512,512]{1,0:T(8,128)}, f32[2,512]{1,0:T(2,128)}) custom-call(bf16[2880,512]{1,0:T(8,128)(2,1)} %tok.3, f32[2880,512]{1,0:T(8,128)} %get-tuple-element.63.dmid, bf16[2880,1536]{1,0:T(8,128)(2,1)} %get-tuple-element.64.proj, bf16[4,512,720]{2,1,0:T(8,128)(2,1)} %get-tuple-element.65.ctxT, ...), custom_call_target="tpu_custom_call" | custom-call | flops 80000000000 | bytes 40000000 | tf_op jit(solution)/shard_map/attend_back/pallas_call | solution.py:539
  432.6 30.4 %all_to_all.41 = bf16[8,4,272,128]{3,2,1,0:T(8,128)(2,1)S(1)} all-to-all(bf16[8,4,272,128]{3,2,1,0:T(8,128)(2,1)S(1)} %bitcast.172), channel_id=1, replica_groups=mesh['dp'=4,'expert'=8] {'expert'}, dimensions={0} | all-to-all | bytes 4456448 | tf_op jit(solution)/shard_map/all_to_all | solution.py:605
  463.4 22.1 %all_to_all.42 = bf16[4,272,128]{2,1,0:T(8,128)(2,1)S(1)} all-to-all(bf16[4,272,128]{2,1,0:T(8,128)(2,1)S(1)} %reduce_sum.57), channel_id=1, replica_groups=mesh['dp'=4,'expert'=8] {'dp'}, dimensions={0} | all-to-all | bytes 557056 | tf_op jit(solution)/shard_map/all_to_all | solution.py:605
  501.8 5.2 copy.136
  512.7 7.3 %collective-permute-done.15 = bf16[512,512]{1,0:T(8,128)(2,1)} collective-permute-done((bf16[512,512]{1,0:T(8,128)(2,1)}, bf16[512,512]{1,0:T(8,128)(2,1)}, u32[]{:S(2)}, u32[]{:S(2)}) %collective-permute-start.15) | collective-permute-done | bytes 524320 | tf_op jit(solution)/shard_map/ppermute | solution.py:601
  528.7 8.2 %collective-permute-done.16 = bf16[512,512]{1,0:T(8,128)(2,1)} collective-permute-done((bf16[512,512]{1,0:T(8,128)(2,1)}, bf16[512,512]{1,0:T(8,128)(2,1)}, u32[]{:S(2)}, u32[]{:S(2)}) %collective-permute-start.16) | collective-permute-done | bytes 524320 | tf_op jit(solution)/shard_map/ppermute | solution.py:601
  544.6 37.2 %collective-permute-done.13 = bf16[512,512]{0,1:T(8,128)(2,1)} collective-permute-done((bf16[512,512]{0,1:T(8,128)(2,1)}, bf16[512,512]{0,1:T(8,128)(2,1)}, u32[]{:S(2)}, u32[]{:S(2)}) %collective-permute-start.13) | collective-permute-done | bytes 524320 | tf_op jit(solution)/shard_map/ppermute | solution.py:601
  588.6 13.6 %all-to-all-start.6 = ((f32[32,1,128]{2,1,0:T(1,128)}), f32[32,1,128]{2,1,0:T(1,128)S(1)}, u32[]{:S(2)}, u32[]{:S(2)}) async-start(f32[32,1,128]{2,1,0:T(1,128)} %broadcast_in_dim.7), calls=%async_computation.6 | async-start | bytes 32768 | tf_op jit(solution)/shard_map/all_to_all | solution.py:605
  602.3 13.8 %finish.1 = bf16[2880,512]{1,0:T(8,128)(2,1)} custom-call(bf16[2944,512]{1,0:T(8,128)(2,1)} %bitcast.18.gb, s32[2880,8]{1,0:T(8,128)} %get-tuple-element.59.cols, f32[2880,512]{1,0:T(8,128)} %get-tuple-element.60.mid), custom_call_target="tpu_custom_call" | custom-call | flops 10000000000 | bytes 12000000 | tf_op jit(solution)/shard_map/finish/pallas_call | solution.py:463
  637.3 5.3 fusion.30
  (170 shorter events, 115.1 us)
Async XLA Ops:
  3.8 14.9 %collective-permute-start = (bf16[272,512]{1,0:T(8,128)(2,1)S(1)}, bf16[272,512]{1,0:T(8,128)(2,1)S(1)}, u32[]{:S(2)}, u32[]{:S(2)}) collective-permute-start(bf16[272,512]{1,0:T(8,128)(2,1)S(1)} %fusion.21), channel_id=1, source_target_pairs={{0,8},{8,0},{16,24},{24,16},{1,9},{9,1},{17,25},{25,17},{2,10},{10... | collective-permute-start | bytes 835592 | tf_op jit(solution)/shard_map/ppermute | solution.py:601
  6.9 22.4 %collective-permute-start.1 = (bf16[272,512]{1,0:T(8,128)(2,1)S(1)}, bf16[272,512]{1,0:T(8,128)(2,1)S(1)}, u32[]{:S(2)}, u32[]{:S(2)}) collective-permute-start(bf16[272,512]{1,0:T(8,128)(2,1)S(1)} %fusion.21), channel_id=1, source_target_pairs={{0,16},{8,24},{16,0},{24,8},{1,17},{9,25},{17,1},{25,9},{2,18},{10... | collective-permute-start | bytes 835592 | tf_op jit(solution)/shard_map/ppermute | solution.py:601
  9.5 19.8 %collective-permute-start.2 = (bf16[272,512]{1,0:T(8,128)(2,1)S(1)}, bf16[272,512]{1,0:T(8,128)(2,1)S(1)}, u32[]{:S(2)}, u32[]{:S(2)}) collective-permute-start(bf16[272,512]{1,0:T(8,128)(2,1)S(1)} %fusion.21), channel_id=1, source_target_pairs={{0,24},{8,16},{16,8},{24,0},{1,25},{9,17},{17,9},{25,1},{2,26},{10... | collective-permute-start | bytes 835592 | tf_op jit(solution)/shard_map/ppermute | solution.py:601
  18.7 33.6 %collective-permute-start.3 = (bf16[272,512]{1,0:T(8,128)(2,1)S(1)}, bf16[272,512]{1,0:T(8,128)(2,1)S(1)}, u32[]{:S(2)}, u32[]{:S(2)}) collective-permute-start(bf16[272,512]{1,0:T(8,128)(2,1)S(1)} %collective-permute-done.r1), channel_id=1, source_target_pairs={{0,1},{1,0},{2,3},{3,2},{4,5},{5,4},{6,7},{7,6},{8,9},{9,8},{10,11... | collective-permute-start | bytes 835592 | tf_op jit(solution)/shard_map/ppermute | solution.py:601
  29.3 23.1 %collective-permute-start.4 = (bf16[272,512]{1,0:T(8,128)(2,1)S(1)}, bf16[272,512]{1,0:T(8,128)(2,1)S(1)}, u32[]{:S(2)}, u32[]{:S(2)}) collective-permute-start(bf16[272,512]{1,0:T(8,128)(2,1)S(1)} %collective-permute-done.1.r2), channel_id=1, source_target_pairs={{0,1},{1,0},{2,3},{3,2},{4,5},{5,4},{6,7},{7,6},{8,9},{9,8},{10,11... | collective-permute-start | bytes 835592 | tf_op jit(solution)/shard_map/ppermute | solution.py:601
  29.3 23.1 %collective-permute-start.5 = (bf16[272,512]{1,0:T(8,128)(2,1)S(1)}, bf16[272,512]{1,0:T(8,128)(2,1)S(1)}, u32[]{:S(2)}, u32[]{:S(2)}) collective-permute-start(bf16[272,512]{1,0:T(8,128)(2,1)S(1)} %collective-permute-done.2.r3), channel_id=1, source_target_pairs={{0,1},{1,0},{2,3},{3,2},{4,5},{5,4},{6,7},{7,6},{8,9},{9,8},{10,11... | collective-permute-start | bytes 835592 | tf_op jit(solution)/shard_map/ppermute | solution.py:601
  46.5 64.8 %all-to-all-start.1 = ((bf16[8,368,512]{2,1,0:T(8,128)(2,1)}), bf16[8,368,512]{2,1,0:T(8,128)(2,1)}, u32[]{:S(2)}, u32[]{:S(2)}) async-start(bf16[8,368,512]{2,1,0:T(8,128)(2,1)} %get-tuple-element.57), calls=%async_computation.1 | async-start | bytes 6029312 | tf_op jit(solution)/shard_map/all_to_all | solution.py:605
  111.2 94.7 %all-to-all-start = ((bf16[8,368,512]{2,1,0:T(8,128)(2,1)}), bf16[8,368,512]{2,1,0:T(8,128)(2,1)}, u32[]{:S(2)}, u32[]{:S(2)}) async-start(bf16[8,368,512]{2,1,0:T(8,128)(2,1)} %spread.1), calls=%async_computation | async-start | bytes 6029312 | tf_op jit(solution)/shard_map/all_to_all | solution.py:605
  116.4 28.3 %collective-permute-start.6 = (bf16[512,512]{1,0:T(8,128)(2,1)S(1)}, bf16[512,512]{1,0:T(8,128)(2,1)S(1)}, u32[]{:S(2)}, u32[]{:S(2)}) collective-permute-start(bf16[512,512]{1,0:T(8,128)(2,1)S(1)} %convert_bitcast_fusion.4), channel_id=1, source_target_pairs={{0,8},{8,0},{16,24},{24,16},{1,9},{9,1},{17,25},{25,17},{2,10},{10... | collective-permute-start | bytes 1572872 | tf_op jit(solution)/shard_map/ppermute | solution.py:601
  121.2 38.2 %collective-permute-start.7 = (bf16[512,512]{1,0:T(8,128)(2,1)S(1)}, bf16[512,512]{1,0:T(8,128)(2,1)S(1)}, u32[]{:S(2)}, u32[]{:S(2)}) collective-permute-start(bf16[512,512]{1,0:T(8,128)(2,1)S(1)} %convert_bitcast_fusion.4), channel_id=1, source_target_pairs={{0,16},{8,24},{16,0},{24,8},{1,17},{9,25},{17,1},{25,9},{2,18},{10... | collective-permute-start | bytes 1572872 | tf_op jit(solution)/shard_map/ppermute | solution.py:601
  122.3 37.1 %collective-permute-start.8 = (bf16[512,512]{1,0:T(8,128)(2,1)S(1)}, bf16[512,512]{1,0:T(8,128)(2,1)S(1)}, u32[]{:S(2)}, u32[]{:S(2)}) collective-permute-start(bf16[512,512]{1,0:T(8,128)(2,1)S(1)} %convert_bitcast_fusion.4), channel_id=1, source_target_pairs={{0,24},{8,16},{16,8},{24,0},{1,25},{9,17},{17,9},{25,1},{2,26},{10... | collective-permute-start | bytes 1572872 | tf_op jit(solution)/shard_map/ppermute | solution.py:601
  123.7 43.7 %collective-permute-start.9 = (bf16[512,512]{1,0:T(8,128)(2,1)S(1)}, bf16[512,512]{1,0:T(8,128)(2,1)S(1)}, u32[]{:S(2)}, u32[]{:S(2)}) collective-permute-start(bf16[512,512]{1,0:T(8,128)(2,1)S(1)} %convert_bitcast_fusion.3), channel_id=1, source_target_pairs={{0,8},{8,0},{16,24},{24,16},{1,9},{9,1},{17,25},{25,17},{2,10},{10... | collective-permute-start | bytes 1572872 | tf_op jit(solution)/shard_map/ppermute | solution.py:601
  124.8 79.5 %collective-permute-start.10 = (bf16[512,512]{1,0:T(8,128)(2,1)S(1)}, bf16[512,512]{1,0:T(8,128)(2,1)S(1)}, u32[]{:S(2)}, u32[]{:S(2)}) collective-permute-start(bf16[512,512]{1,0:T(8,128)(2,1)S(1)} %convert_bitcast_fusion.3), channel_id=1, source_target_pairs={{0,16},{8,24},{16,0},{24,8},{1,17},{9,25},{17,1},{25,9},{2,18},{10... | collective-permute-start | bytes 1572872 | tf_op jit(solution)/shard_map/ppermute | solution.py:601
  144.7 59.6 %collective-permute-start.11 = (bf16[512,512]{1,0:T(8,128)(2,1)S(1)}, bf16[512,512]{1,0:T(8,128)(2,1)S(1)}, u32[]{:S(2)}, u32[]{:S(2)}) collective-permute-start(bf16[512,512]{1,0:T(8,128)(2,1)S(1)} %convert_bitcast_fusion.3), channel_id=1, source_target_pairs={{0,24},{8,16},{16,8},{24,0},{1,25},{9,17},{17,9},{25,1},{2,26},{10... | collective-permute-start | bytes 1572872 | tf_op jit(solution)/shard_map/ppermute | solution.py:601
  356.6 69.5 %copy-start.28 = (f32[2,512]{1,0:T(2,128)S(1)}, f32[2,512]{1,0:T(2,128)}, u32[]{:S(2)}) copy-start(f32[2,512]{1,0:T(2,128)} %get-tuple-element.72) | copy-start | bytes 12292
  485.5 102.5 %all-to-all-start.2 = ((bf16[8,368,512]{2,1,0:T(8,128)(2,1)}), bf16[8,368,512]{2,1,0:T(8,128)(2,1)}, u32[]{:S(2)}, u32[]{:S(2)}) async-start(bf16[8,368,512]{2,1,0:T(8,128)(2,1)} %get-tuple-element.58), calls=%async_computation.2 | async-start | bytes 6029312 | tf_op jit(solution)/shard_map/all_to_all | solution.py:605
  496.4 23.5 %collective-permute-start.15 = (bf16[512,512]{1,0:T(8,128)(2,1)}, bf16[512,512]{1,0:T(8,128)(2,1)}, u32[]{:S(2)}, u32[]{:S(2)}) collective-permute-start(bf16[512,512]{1,0:T(8,128)(2,1)} %get-tuple-element.238), channel_id=1, source_target_pairs={{0,8},{8,0},{16,24},{24,16},{1,9},{9,1},{17,25},{25,17},{2,10},{10... | collective-permute-start | bytes 1572872 | tf_op jit(solution)/shard_map/ppermute | solution.py:601
  498.3 38.6 %collective-permute-start.16 = (bf16[512,512]{1,0:T(8,128)(2,1)}, bf16[512,512]{1,0:T(8,128)(2,1)}, u32[]{:S(2)}, u32[]{:S(2)}) collective-permute-start(bf16[512,512]{1,0:T(8,128)(2,1)} %get-tuple-element.240), channel_id=1, source_target_pairs={{0,16},{8,24},{16,0},{24,8},{1,17},{9,25},{17,1},{25,9},{2,18},{10... | collective-permute-start | bytes 1572872 | tf_op jit(solution)/shard_map/ppermute | solution.py:601
  499.4 37.5 %collective-permute-start.17 = (bf16[512,512]{1,0:T(8,128)(2,1)}, bf16[512,512]{1,0:T(8,128)(2,1)}, u32[]{:S(2)}, u32[]{:S(2)}) collective-permute-start(bf16[512,512]{1,0:T(8,128)(2,1)} %get-tuple-element.239), channel_id=1, source_target_pairs={{0,24},{8,16},{16,8},{24,0},{1,25},{9,17},{17,9},{25,1},{2,26},{10... | collective-permute-start | bytes 1572872 | tf_op jit(solution)/shard_map/ppermute | solution.py:601
  510.6 34.0 %collective-permute-start.12 = (bf16[512,512]{0,1:T(8,128)(2,1)}, bf16[512,512]{0,1:T(8,128)(2,1)}, u32[]{:S(2)}, u32[]{:S(2)}) collective-permute-start(bf16[512,512]{0,1:T(8,128)(2,1)} %get-tuple-element.241), channel_id=1, source_target_pairs={{0,8},{8,0},{16,24},{24,16},{1,9},{9,1},{17,25},{25,17},{2,10},{10... | collective-permute-start | bytes 1572872 | tf_op jit(solution)/shard_map/ppermute | solution.py:601
  510.7 71.1 %collective-permute-start.13 = (bf16[512,512]{0,1:T(8,128)(2,1)}, bf16[512,512]{0,1:T(8,128)(2,1)}, u32[]{:S(2)}, u32[]{:S(2)}) collective-permute-start(bf16[512,512]{0,1:T(8,128)(2,1)} %get-tuple-element.243), channel_id=1, source_target_pairs={{0,16},{8,24},{16,0},{24,8},{1,17},{9,25},{17,1},{25,9},{2,18},{10... | collective-permute-start | bytes 1572872 | tf_op jit(solution)/shard_map/ppermute | solution.py:601
  520.0 61.8 %collective-permute-start.14 = (bf16[512,512]{0,1:T(8,128)(2,1)}, bf16[512,512]{0,1:T(8,128)(2,1)}, u32[]{:S(2)}, u32[]{:S(2)}) collective-permute-start(bf16[512,512]{0,1:T(8,128)(2,1)} %get-tuple-element.242), channel_id=1, source_target_pairs={{0,24},{8,16},{16,8},{24,0},{1,25},{9,17},{17,9},{25,1},{2,26},{10... | collective-permute-start | bytes 1572872 | tf_op jit(solution)/shard_map/ppermute | solution.py:601
  588.6 27.4 %all-to-all-start.6 = ((f32[32,1,128]{2,1,0:T(1,128)}), f32[32,1,128]{2,1,0:T(1,128)S(1)}, u32[]{:S(2)}, u32[]{:S(2)}) async-start(f32[32,1,128]{2,1,0:T(1,128)} %broadcast_in_dim.7), calls=%async_computation.6 | async-start | bytes 32768 | tf_op jit(solution)/shard_map/all_to_all | solution.py:605
  616.9 31.7 %all-to-all-start.7 = ((bf16[8,272,128]{2,1,0:T(8,128)(2,1)}), bf16[8,272,128]{2,1,0:T(8,128)(2,1)}, u32[]{:S(2)}, u32[]{:S(2)}) async-start(bf16[8,272,128]{2,1,0:T(8,128)(2,1)} %broadcast_in_dim.16), calls=%async_computation.7 | async-start | bytes 1114112 | tf_op jit(solution)/shard_map/all_to_all | solution.py:605
  (29 other events, 153.7 us)

commit v2 on v1

v2 whole, which is shorter than its diff:
```python
import functools

import jax
import jax.numpy as jnp
from jax import lax
from jax.experimental import pallas as pl
from jax.experimental.pallas import tpu as pltpu
from jax.sharding import PartitionSpec as P

D = 512
HEADS = 8
HEAD = 64
FF = 2048
SEQ = 720

EPS_NORM = 1e-06
BETA_ONE = 0.9
BETA_TWO = 0.999
ADAM_EPS = 1e-08
DECAY_RATE = 0.1
MAX_NORM = 1.0

f32, bf16, i32 = jnp.float32, jnp.bfloat16, jnp.int32
NN = (((1,), (0,)), ((), ()))
NT = (((1,), (1,)), ((), ()))
TN = (((0,), (0,)), ((), ()))
LOG2E = 1.4426950408889634
SCALE = HEAD**-0.5
FAR = 1 << 20
VMEM_LIMIT = 60 * 2**20


def mm(a, b, dims=NN):
    return lax.dot_general(a, b, dims, preferred_element_type=f32)


def full(a):
    return pl.BlockSpec(a.shape, lambda *i: (0,) * a.ndim)


def whole(*shape):
    return pl.BlockSpec(shape, lambda *i: (0,) * len(shape))


def per_image(cols):
    return pl.BlockSpec((SEQ, cols), lambda i: (i, 0))


def per_image_t(rows):
    return pl.BlockSpec((1, rows, SEQ), lambda i: (i, 0, 0))


def sds(shape, dtype):
    return jax.ShapeDtypeStruct(shape, dtype)


SMEM = pl.BlockSpec(memory_space=pltpu.SMEM)


def call(body, name, us=0.1, **kw):
    return pl.pallas_call(
        body,
        name=name,
        compiler_params=pltpu.CompilerParams(vmem_limit_bytes=VMEM_LIMIT),
        cost_estimate=pl.CostEstimate(flops=int(us * 10**9), bytes_accessed=10**5, transcendentals=0),
        **kw,
    )


def normalize(v):
    c = v - jnp.mean(v, axis=-1, keepdims=True)
    r = lax.rsqrt(jnp.mean(c * c, axis=-1, keepdims=True) + EPS_NORM)
    return c * r, r


def assemble_kernel(experts, where, got, misc, near, far, wT, ow, rT, nm):
    me, slot = where[0], where[2] % 8
    per = experts // 4
    for c in range(4):
        for b in range(2):
            s = slot ^ (2 * c + b)
            for k in range(4):
                d = me ^ k
                if b == 0:
                    piece = got[k] if c == 0 else near[c - 1, k]
                else:
                    piece = far[c, k]
                lo = pl.multiple_of(d * 384 + s * 48, 16)
                wT[pl.ds(lo, 48), :] = piece[:48, :]
                lo = pl.multiple_of(d * 128 + s * 16, 16)
                ow[pl.ds(lo, 16), :] = piece[48:64, :]
    for d in range(4):
        for k in range(4):

            @pl.when((me ^ k) == d)
            def _(d=d, k=k):
                rest = misc[k].astype(f32)
                rT[d * per : (d + 1) * per, :] = rest[:per, :]
                for j in range(4):
                    nm[j : j + 1, d * 128 : (d + 1) * 128] = rest[
                        per : per + 1, j * 128 : (j + 1) * 128
                    ]


def assemble(where, got, misc, near, far, experts):
    args = (got, misc, near, far)
    return call(
        functools.partial(assemble_kernel, experts),
        "assemble",
        in_specs=[SMEM] + [whole(*a.shape) for a in args],
        out_specs=[whole(3 * D, D), whole(D, D), whole(experts, D), whole(4, D)],
        out_shape=[
            sds((3 * D, D), bf16),
            sds((D, D), bf16),
            sds((experts, D), f32),
            sds((4, D), f32),
        ],
    )(where, *args)


def dispatch(pos, x, pad, step):
    io = lax.broadcasted_iota(i32, (pad, SEQ), 0)
    acc = None
    for i in range(pos.shape[0]):
        hit = jnp.where(io == pos[i, pl.ds(step, 1), :], 1.0, 0.0).astype(bf16)
        part = mm(hit, x[i * SEQ : (i + 1) * SEQ, :])
        acc = part if acc is None else acc + part
    return acc.astype(bf16)


def slots_kernel(cap, pad, where, ids, prio, cot, pos, cols, u):
    step = pl.program_id(0)
    me = where[2]
    n = ids.shape[0]
    experts = pos.shape[1]
    nh = -(-(2 * n * SEQ) // 2048) * 16

    @pl.when(step == 0)
    def _():
        hi_io = lax.broadcasted_iota(i32, (nh, SEQ), 0)
        lo_io = lax.broadcasted_iota(i32, (128, SEQ), 0)

        def hot(i, k):
            q = prio[i, k : k + 1, :]
            return hi_io == (q >> 7), lo_io == (q & 127)

        table = jnp.zeros((nh, 128), f32)
        for i in range(n):
            for k in range(2):
                a, b = hot(i, k)
                ex = ((ids[i, k : k + 1, :] ^ me) + 1).astype(f32)
                table += mm(
                    jnp.where(a, 1.0, 0.0).astype(bf16), jnp.where(b, ex, 0.0).astype(bf16), NT
                )
        upper = (
            lax.broadcasted_iota(i32, (128, 128), 0) < lax.broadcasted_iota(i32, (128, 128), 1)
        ).astype(bf16)
        lower = (
            lax.broadcasted_iota(i32, (nh, nh), 1) < lax.broadcasted_iota(i32, (nh, nh), 0)
        ).astype(bf16)
        ones = jnp.ones((128, 128), bf16)
        rank = jnp.zeros((nh, 128), f32)
        for e in range(experts):
            m = (table == float(e + 1)).astype(f32)
            mb = m.astype(bf16)
            rank += m * (mm(mb, upper) + mm(mm(lower, mb).astype(bf16), ones))
        ri = jnp.minimum(rank.astype(i32), 16383)
        rlo = (ri & 127).astype(bf16)
        rhi = (ri >> 7).astype(bf16)
        eio = lax.broadcasted_iota(i32, (experts, SEQ), 0)
        for i in range(n):
            out = jnp.full((experts, SEQ), FAR, i32)
            flat = []
            for k in range(2):
                a, b = hot(i, k)
                bb = jnp.where(b, 1.0, 0.0).astype(bf16)
                x = mm(rlo, bb) + 128.0 * mm(rhi, bb)
                r = jnp.sum(jnp.where(a, x, 0.0), axis=0, keepdims=True).astype(i32)
                ex = ids[i, k : k + 1, :] ^ me
                keep = r < cap
                out = jnp.where((eio == ex) & keep, r, out)
                flat.append(jnp.where(keep, ex * pad + r, FAR))
            pos[i] = out
            fl = jnp.concatenate(flat + [jnp.zeros((6, SEQ), i32)], axis=0).astype(f32)
            cols[i * SEQ : (i + 1) * SEQ, :] = fl.T.astype(i32)

    u[pl.ds(step ^ me, 1)] = dispatch(pos, cot, pad, step)[None]


def slots(where, ids, prio, cot, experts, cap, pad):
    n = ids.shape[0]
    t = n * SEQ
    return call(
        functools.partial(slots_kernel, cap, pad),
        "slots",
        grid=(experts,),
        in_specs=[SMEM, full(ids), full(prio), full(cot)],
        out_specs=[whole(n, experts, SEQ), whole(t, 8), whole(experts, pad, D)],
        out_shape=[
            sds((n, experts, SEQ), i32),
            sds((t, 8), i32),
            sds((experts, pad, D), bf16),
        ],
    )(where, ids, prio, cot)


def spread_kernel(pad, pos, x, *outs):
    step = pl.program_id(0)
    block = dispatch(pos, x, pad, step)
    for j, out in enumerate(outs):

        @pl.when(step == j)
        def _(out=out):
            out[...] = block


def spread(pos, x, pad):
    experts = pos.shape[1]
    return call(
        functools.partial(spread_kernel, pad),
        "spread",
        grid=(experts,),
        in_specs=[full(pos), full(x)],
        out_specs=[whole(pad, D)] * experts,
        out_shape=[sds((pad, D), bf16)] * experts,
    )(pos, x)


def head_masks():
    lane = lax.broadcasted_iota(i32, (1, 128), 1)
    return (lane < 64).astype(bf16), (lane >= 64).astype(bf16)


def attend_kernel(tok, wT, ow, rT, nm, proj, ctxT, lse, mid, sec, gatesT, vT, ct):
    x = tok[...].astype(f32)
    xh, _ = normalize(x)
    fb = (xh * nm[0:1, :] + nm[1:2, :]).astype(bf16)
    proj[...] = mm(fb, wT[...], NT).astype(bf16)
    vT[...] = proj[:, 2 * D :].T
    masks = head_masks()
    for h in range(HEADS):
        p = h // 2
        qm = proj[:, p * 128 : (p + 1) * 128] * masks[h % 2]
        kk = proj[:, D + p * 128 : D + (p + 1) * 128]
        s = mm(kk, qm, NT)
        m = jnp.max(s, axis=0, keepdims=True)
        e = jnp.exp2((s - m) * (SCALE * LOG2E))
        total = jnp.sum(e, axis=0, keepdims=True)
        c = mm(vT[h * 64 : (h + 1) * 64, :], e.astype(bf16))
        ct[h * 64 : (h + 1) * 64, :] = (c * (1.0 / total)).astype(bf16)
        lse[0, h : h + 1, :] = m * (SCALE * LOG2E) + jnp.log2(total)
    ctxT[0] = ct[...]
    middle = x + mm(ct[...], ow[...], TN)
    mid[...] = middle
    xh2, _ = normalize(middle)
    s2 = (xh2 * nm[2:3, :] + nm[3:4, :]).astype(bf16)
    sec[...] = s2
    logits = mm(rT[...].astype(bf16), s2, NT)
    ex = jnp.exp(logits - jnp.max(logits, axis=0, keepdims=True))
    gatesT[0] = ex / jnp.sum(ex, axis=0, keepdims=True)


def attend(tok, wT, ow, rT, nm):
    t = tok.shape[0]
    n = t // SEQ
    experts = rT.shape[0]
    return call(
        attend_kernel,
        "attend",
        grid=(n,),
        in_specs=[per_image(D), full(wT), full(ow), full(rT), full(nm)],
        out_specs=[
            per_image(3 * D),
            per_image_t(D),
            per_image_t(HEADS),
            per_image(D),
            per_image(D),
            per_image_t(experts),
        ],
        out_shape=[
            sds((t, 3 * D), bf16),
            sds((n, D, SEQ), bf16),
            sds((n, HEADS, SEQ), f32),
            sds((t, D), f32),
            sds((t, D), bf16),
            sds((n, experts, SEQ), f32),
        ],
        scratch_shapes=[pltpu.VMEM((D, SEQ), bf16), pltpu.VMEM((D, SEQ), bf16)],
    )(tok, wT, ow, rT, nm)


def normal_cdf(h):
    t = 1.0 / (1.0 + (0.3275911 * 0.7071067811865476) * jnp.abs(h))
    g = jnp.exp2((-0.5 * LOG2E) * h * h)
    poly = t * (
        0.5 * 0.254829592
        + t
        * (
            0.5 * -0.284496736
            + t * (0.5 * 1.421413741 + t * (0.5 * -1.453152027 + t * (0.5 * 1.061405429)))
        )
    )
    q = poly * g
    return jnp.where(h >= 0, 1.0 - q, q), g


def experts_kernel(cap, ks, where, *refs):
    nb = len(ks)
    rows, (u, gw, rT) = refs[:nb], refs[nb : nb + 3]
    gb, dr = refs[nb + 3 : 2 * nb + 3], refs[2 * nb + 3 : 3 * nb + 3]
    xs, db, act, dh = refs[3 * nb + 3 : 3 * nb + 7]
    s = pl.program_id(0)
    pad = rows[0].shape[0]
    me = where[2]
    chunks, _, cols = gw.shape
    iw = [gw.at[j, :D] for j in range(chunks)]
    xw = [gw.at[j, D:] for j in range(chunks)]
    for i in range(nb // 2):

        @pl.when(s == i)
        def _(i=i):
            xs[:pad, :] = rows[2 * i][...]
            xs[pad:, :] = rows[2 * i + 1][...]
            db[:pad, :] = u[me ^ ks[2 * i]]
            db[pad:, :] = u[me ^ ks[2 * i + 1]]

    x = xs[...]
    upf = db[...].astype(f32)
    logits = mm(x, rT[...].astype(bf16), NT)
    ex = jnp.exp(logits - jnp.max(logits, axis=1, keepdims=True))
    mine = lax.broadcasted_iota(i32, ex.shape, 1) == me
    gate = jnp.sum(jnp.where(mine, ex, 0.0), axis=1, keepdims=True) / jnp.sum(
        ex, axis=1, keepdims=True
    )
    d = (gate * upf).astype(bf16)
    db[...] = d
    back = None
    drow = None
    for j in range(chunks):
        h = mm(x, iw[j][...])
        cdf, g = normal_cdf(h)
        a = (h * cdf).astype(bf16)
        act[:, j * cols : (j + 1) * cols] = a
        part = mm(a, xw[j][...])
        back = part if back is None else back + part
        dact = mm(d, xw[j][...], NT)
        dj = (dact * (cdf + h * g * 0.3989422804014327)).astype(bf16)
        dh[:, j * cols : (j + 1) * cols] = dj
        part = mm(dj, iw[j][...], NT)
        drow = part if drow is None else drow + part
    b = back.astype(bf16).astype(f32)
    gback = (gate * b).astype(bf16)
    prod = upf * b
    first = prod.astype(bf16)
    rest = (prod - first.astype(f32)).astype(bf16)
    ones = jnp.ones((8, D), bf16)
    dgs = (mm(ones, first, NT) + mm(ones, rest, NT))[0:1, :]
    line = lax.broadcasted_iota(i32, (pad, D), 0)
    for o in range(2):
        dg = dgs[:, o * pad : (o + 1) * pad]
        dg = jnp.concatenate([dg, jnp.zeros((1, D - pad), f32)], axis=1)
        top = dg.astype(bf16).astype(f32)
        part = drow[o * pad : (o + 1) * pad, :]
        part = jnp.where(line == cap, top, jnp.where(line == cap + 1, dg - top, part))
        part = part.astype(bf16)
        for i in range(nb // 2):

            @pl.when(s == i)
            def _(i=i, o=o, part=part):
                dr[2 * i + o][...] = part
                gb[2 * i + o][...] = gback[o * pad : (o + 1) * pad, :]


def run_experts(where, ks, rows, u, gw, rT, cap):
    nb = len(ks)
    pad = rows[0].shape[0]
    chunks, _, cols = gw.shape
    pair = lambda c: pl.BlockSpec((2 * pad, c), lambda i: (i, 0))
    blk = sds((pad, D), bf16)
    out = call(
        functools.partial(experts_kernel, cap, ks),
        "experts",
        us=8 * nb,
        grid=(nb // 2,),
        in_specs=[SMEM] + [whole(pad, D)] * nb + [full(u), full(gw), full(rT)],
        out_specs=[whole(pad, D)] * (2 * nb) + [pair(D), pair(D), pair(FF), pair(FF)],
        out_shape=[blk] * (2 * nb)
        + [sds((nb * pad, D), bf16)] * 2
        + [sds((nb * pad, chunks * cols), bf16)] * 2,
    )(where, *rows, u, gw, rT)
    return out[:nb], out[nb : 2 * nb], out[2 * nb :]


def weights_kernel(groups, *refs):
    xs, dbs, acts, dhs = (refs[i * groups : (i + 1) * groups] for i in range(4))
    out, xT, dT = refs[4 * groups :]
    pieces = []
    at = 0
    for g in range(groups):
        step = xT.shape[2]
        for r in range(xs[g].shape[0] // step):
            pieces.append((g, r * step, at))
            at += 1

    @pl.when(pl.program_id(0) == 0)
    def _():
        for g, r, p in pieces:
            xT[p] = xs[g][r : r + xT.shape[2], :].T
            dT[p] = dbs[g][r : r + xT.shape[2], :].T

    di = None
    de = None
    for g, r, p in pieces:
        part = mm(xT[p], dhs[g][r : r + xT.shape[2], :])
        di = part if di is None else di + part
        part = mm(dT[p], acts[g][r : r + xT.shape[2], :])
        de = part if de is None else de + part
    out[0, :D, :] = di.astype(bf16)
    out[0, D:, :] = de.astype(bf16)


def weight_grads(kept, pad):
    groups = len(kept)
    ins = [k[i] for i in range(4) for k in kept]
    total = sum(k[0].shape[0] for k in kept) // (2 * pad)
    col = lambda a: pl.BlockSpec((a.shape[0], D), lambda j: (0, j))
    return call(
        functools.partial(weights_kernel, groups),
        "weight_grads",
        grid=(FF // D,),
        in_specs=[full(a) for a in ins[: 2 * groups]] + [col(a) for a in ins[2 * groups :]],
        out_specs=pl.BlockSpec((1, 2 * D, D), lambda j: (j, 0, 0)),
        out_shape=sds((FF // D, 2 * D, D), bf16),
        scratch_shapes=[pltpu.VMEM((total, D, 2 * pad), bf16)] * 2,
    )(*ins)


def pick(cols, count):
    io = lax.broadcasted_iota(i32, (SEQ, count), 1)
    return jnp.where((io == cols[:, 0:1]) | (io == cols[:, 1:2]), 1.0, 0.0).astype(bf16)


def stack_once(blocks, scratch):
    pad = blocks[0].shape[0]

    @pl.when(pl.program_id(0) == 0)
    def _():
        for j, block in enumerate(blocks):
            scratch[j * pad : (j + 1) * pad, :] = block[...]


def combine_kernel(cap, experts, where, *refs):
    cols, gatesT, sec, mid, cot, rT, nm, dmid, dn, drT, dr, dgs = refs[experts:]
    stack_once(refs[:experts], dr)
    i = pl.program_id(0)
    me = where[2]
    pad = dr.shape[0] // experts
    hits = pick(cols[...], dr.shape[0])
    ds = mm(hits, dr[...])
    base = cap // 16 * 16
    off = cap - base
    for e in range(experts):
        two = dr[e * pad + base : (e + 1) * pad, :pad]
        x = mm(two, hits[:, e * pad : (e + 1) * pad], NT)
        dgs[pl.ds(e ^ me, 1), :] = x[off : off + 1, :] + x[off + 1 : off + 2, :]
    dg = dgs[...]
    g = gatesT[0]
    dl = (g * (dg - jnp.sum(g * dg, axis=0, keepdims=True))).astype(bf16)
    ds = ds + mm(dl, rT[...].astype(bf16), TN)
    xh, r = normalize(mid[...])
    y = ds * nm[2:3, :]
    dmid[...] = cot[...].astype(f32) + r * (
        y - jnp.mean(y, axis=-1, keepdims=True) - xh * jnp.mean(y * xh, axis=-1, keepdims=True)
    )
    gg = jnp.sum(ds * xh, axis=0, keepdims=True)
    gs = jnp.sum(ds, axis=0, keepdims=True)
    dR = mm(dl, sec[...])

    @pl.when(i == 0)
    def _():
        dn[0:1, :] = gg
        dn[1:2, :] = gs
        drT[...] = dR

    @pl.when(i > 0)
    def _():
        dn[0:1, :] += gg
        dn[1:2, :] += gs
        drT[...] += dR


def combine(where, blocks, cols, gatesT, sec, mid, cot, rT, nm, cap):
    experts = len(blocks)
    pad = blocks[0].shape[0]
    t = cols.shape[0]
    return call(
        functools.partial(combine_kernel, cap, experts),
        "combine",
        grid=(t // SEQ,),
        in_specs=[SMEM]
        + [whole(pad, D)] * experts
        + [
            per_image(8),
            per_image_t(experts),
            per_image(D),
            per_image(D),
            per_image(D),
            full(rT),
            full(nm),
        ],
        out_specs=[per_image(D), whole(2, D), whole(experts, D)],
        out_shape=[sds((t, D), f32), sds((2, D), f32), sds((experts, D), f32)],
        scratch_shapes=[pltpu.VMEM((experts * pad, D), bf16), pltpu.VMEM((experts, SEQ), f32)],
    )(where, *blocks, cols, gatesT, sec, mid, cot, rT, nm)


def finish_kernel(experts, *refs):
    cols, mid, out, gb = refs[experts:]
    stack_once(refs[:experts], gb)
    out[...] = (mid[...] + mm(pick(cols[...], gb.shape[0]), gb[...])).astype(bf16)


def finish(blocks, cols, mid):
    experts = len(blocks)
    pad = blocks[0].shape[0]
    t = cols.shape[0]
    return call(
        functools.partial(finish_kernel, experts),
        "finish",
        grid=(t // SEQ,),
        in_specs=[whole(pad, D)] * experts + [per_image(8), per_image(D)],
        out_specs=per_image(D),
        out_shape=sds((t, D), bf16),
        scratch_shapes=[pltpu.VMEM((experts * pad, D), bf16)],
    )(*blocks, cols, mid)


TILES = (
    (((0, 0), (0, 1)), ((0, 4), (0, 5)), ((0, 8), (1, 2)), ((0, 9), (1, 3))),
    (((0, 2), (1, 0)), ((0, 3), (1, 1)), ((0, 6), (0, 7)), ((0, 10), (0, 11))),
)


def attend_back_kernel(part, tok, dmid, proj, ctxT, lse, ow, nm, dproj, packed, kT, dqT, gq, go):
    i = pl.program_id(0)
    half = D // 2
    base = part * half
    da = dmid[...].astype(bf16)
    owp = ow[base : base + half, :]
    do = mm(da, owp, NT).astype(bf16)
    doT = mm(owp, da, NT).astype(bf16)
    prod = doT.astype(f32) * ctxT[0, base : base + half, :].astype(f32)
    kT[...] = proj[:, D + base : D + base + half].T
    masks = head_masks()
    low = lax.broadcasted_iota(i32, (SEQ, 128), 1) < 64
    for p in range(HEADS // 4):
        dv = []
        dk = []
        lo = base + p * 128
        qq = proj[:, lo : lo + 128]
        kk = proj[:, D + lo : D + lo + 128]
        vv = proj[:, 2 * D + lo : 2 * D + lo + 128]
        dd = do[:, p * 128 : (p + 1) * 128]
        for j in range(2):
            hl = 2 * p + j
            h = part * (HEADS // 2) + hl
            s = mm(kk, qq * masks[j], NT)
            prob = jnp.exp2(s * (SCALE * LOG2E) - lse[0, h : h + 1, :])
            dprob = mm(vv, dd * masks[j], NT)
            dv.append(mm(prob.astype(bf16), dd))
            inner = jnp.sum(prod[hl * 64 : (hl + 1) * 64, :], axis=0, keepdims=True)
            ds = (prob * (dprob - inner)).astype(bf16)
            dk.append(mm(ds, qq))
            dqT[hl * 64 : (hl + 1) * 64, :] = (
                mm(kT[hl * 64 : (hl + 1) * 64, :], ds) * SCALE
            ).astype(bf16)
        at = p * 128
        dproj[:, 2 * half + at : 2 * half + at + 128] = jnp.where(low, dv[0], dv[1]).astype(bf16)
        dproj[:, half + at : half + at + 128] = (jnp.where(low, dk[0], dk[1]) * SCALE).astype(bf16)
    dproj[:, :half] = dqT[...].T
    xh, _ = normalize(tok[...].astype(f32))
    fb = (xh * nm[0:1, :] + nm[1:2, :]).astype(bf16)
    dq = mm(fb, dproj[...], TN)
    other = (1 - part) * half
    do_ = mm(ctxT[0, other : other + half, :], da)

    @pl.when(i == 0)
    def _():
        gq[...] = dq
        go[...] = do_

    @pl.when(i > 0)
    def _():
        gq[...] += dq
        go[...] += do_

    @pl.when(i == pl.num_programs(0) - 1)
    def _():
        groups, _, r, _ = packed.shape
        for d in range(4):
            for t in range(2):
                kind, c = TILES[part][d][t]
                if kind == 0:
                    third, at = c // 4, c % 4 - 2 * part
                    tile = gq[:, third * half + at * 128 : third * half + (at + 1) * 128]
                else:
                    row = (c - (2 - 2 * part)) * 128
                    tile = jnp.concatenate(
                        [go[row : row + 128, j * 128 : (j + 1) * 128] for j in range(4)], axis=0
                    )
                tile = tile.astype(bf16)
                for m in range(512 // r):
                    packed[t * (512 // r) + m, d] = tile[m * r : (m + 1) * r, :]


def attend_back(part, groups, tok, dmid, proj, ctxT, lse, ow, nm):
    t = tok.shape[0]
    r = 1024 // groups
    return call(
        functools.partial(attend_back_kernel, part),
        "attend_back",
        grid=(t // SEQ,),
        in_specs=[
            per_image(D),
            per_image(D),
            per_image(3 * D),
            per_image_t(D),
            per_image_t(HEADS),
            full(ow),
            full(nm),
        ],
        out_specs=[per_image(3 * D // 2), whole(groups, 4, r, 128)],
        out_shape=[sds((t, 3 * D // 2), bf16), sds((groups, 4, r, 128), bf16)],
        scratch_shapes=[
            pltpu.VMEM((D // 2, SEQ), bf16),
            pltpu.VMEM((D // 2, SEQ), bf16),
            pltpu.VMEM((D, 3 * D // 2), f32),
            pltpu.VMEM((D // 2, D), f32),
        ],
    )(tok, dmid, proj, ctxT, lse, ow, nm)


def enter_kernel(tok, dmid, dp0, dp1, wT, nm, gin, dn):
    i = pl.program_id(0)
    half = D // 2
    df = None
    for part, dp in enumerate((dp0, dp1)):
        for third in range(3):
            lo = third * D + part * half
            term = mm(dp[:, third * half : (third + 1) * half], wT[lo : lo + half, :])
            df = term if df is None else df + term
    xh, r = normalize(tok[...].astype(f32))
    y = df * nm[0:1, :]
    gin[...] = dmid[...] + r * (
        y - jnp.mean(y, axis=-1, keepdims=True) - xh * jnp.mean(y * xh, axis=-1, keepdims=True)
    )
    gg = jnp.sum(df * xh, axis=0, keepdims=True)
    gs = jnp.sum(df, axis=0, keepdims=True)

    @pl.when(i == 0)
    def _():
        dn[0:1, :] = gg
        dn[1:2, :] = gs

    @pl.when(i > 0)
    def _():
        dn[0:1, :] += gg
        dn[1:2, :] += gs


def enter(tok, dmid, dp0, dp1, wT, nm):
    t = tok.shape[0]
    return call(
        enter_kernel,
        "enter",
        grid=(t // SEQ,),
        in_specs=[
            per_image(D),
            per_image(D),
            per_image(3 * D // 2),
            per_image(3 * D // 2),
            full(wT),
            full(nm),
        ],
        out_specs=[per_image(D), whole(2, D)],
        out_shape=[sds((t, D), f32), sds((2, D), f32)],
    )(tok, dmid, dp0, dp1, wT, nm)


def step_rates(experts):
    return (
        D ** (-0.5),
        2.0 ** (-0.5),
        (2 * D) ** (-0.5),
        0.1,
        D ** (-0.5),
        2.0 * experts / (1.2 * FF**0.5),
    )


def adam_update(weight, moments, grad, factor, rate, decay, fixes):
    clipped = grad * factor
    first = BETA_ONE * moments[0] + (1.0 - BETA_ONE) * clipped
    second = BETA_TWO * moments[1] + (1.0 - BETA_TWO) * clipped * clipped
    updated = weight - rate * (
        first / fixes[0] / (jnp.sqrt(second / fixes[1]) + ADAM_EPS) + decay * weight
    )
    return (updated, first, second, updated.astype(bf16))


def adam_kernel(rates, where, nums, *refs):
    parts, owned = refs[:2], refs[2]
    weights, moments, outs = refs[3:7], refs[7:11], refs[11:27]
    gq, go = refs[27:]
    i = pl.program_id(0)

    @pl.when(i == 0)
    def _():
        for d in range(4):

            @pl.when(where[0] == d)
            def _(d=d):
                for part in range(2):
                    for t in range(2):
                        kind, c = TILES[part][d][t]
                        if kind == 0:
                            at = (c - 3 * d) * 128
                            gq[:, at : at + 128] = parts[part][t * 512 : (t + 1) * 512, :]
                        else:
                            for j in range(4):
                                lo = t * 512 + j * 128
                                go[:, j * 128 : (j + 1) * 128] = parts[part][lo : lo + 128, :]

    rows_q, rows_o = weights[0].shape[0], weights[1].shape[0]
    rows_e = weights[2].shape[1]
    grads = (
        gq[pl.ds(i * rows_q, rows_q), :].astype(f32),
        go[pl.ds(i * rows_o, rows_o), :].astype(f32),
        owned[pl.ds(i * rows_e, rows_e), :],
        owned[D:, pl.ds(pl.multiple_of(i * rows_e, 128), rows_e)].T,
    )
    factor = nums[0]
    fixes = (nums[1], nums[2])
    for j in range(4):
        lead = j >= 2
        w = weights[j][0] if lead else weights[j][...]
        m = (moments[j][0, 0], moments[j][1, 0]) if lead else (moments[j][0], moments[j][1])
        new = adam_update(w, m, grads[j], factor, rates[j], DECAY_RATE, fixes)
        for o in range(4):
            if lead:
                outs[4 * j + o][0] = new[o]
            else:
                outs[4 * j + o][...] = new[o]


def adam(rates, where, nums, part0, part1, owned, weights, moments):
    steps = 4
    specs = []
    mspecs = []
    for w in weights:
        if w.ndim == 2:
            specs.append(pl.BlockSpec((w.shape[0] // steps, w.shape[1]), lambda i: (i, 0)))
            mspecs.append(pl.BlockSpec((2, w.shape[0] // steps, w.shape[1]), lambda i: (0, i, 0)))
        else:
            specs.append(
                pl.BlockSpec((1, w.shape[1] // steps, w.shape[2]), lambda i: (0, i, 0))
            )
            mspecs.append(
                pl.BlockSpec((2, 1, w.shape[1] // steps, w.shape[2]), lambda i: (0, 0, i, 0))
            )
    return call(
        functools.partial(adam_kernel, rates),
        "adam",
        grid=(steps,),
        in_specs=[SMEM, SMEM, full(part0), full(part1), full(owned)] + specs + mspecs,
        out_specs=[sp for sp in specs for _ in range(4)],
        out_shape=[sds(w.shape, dt) for w in weights for dt in (f32, f32, f32, bf16)],
        scratch_shapes=[pltpu.VMEM((D, 384), bf16), pltpu.VMEM((128, D), bf16)],
    )(where, nums, part0, part1, owned, *weights, *moments)


def swap(x, axis, k):
    n = lax.axis_size(axis)
    return lax.ppermute(x, axis, [(i, i ^ k) for i in range(n)])


def exchange(x, axis):
    return lax.all_to_all(x, axis, split_axis=0, concat_axis=0, tiled=True)


def total(blocks):
    return functools.reduce(lambda a, b: a + b, [b.astype(f32) for b in blocks])


def at(x, i):
    return lax.dynamic_index_in_dim(x, i, 0, keepdims=False)


def fence(*groups):
    flat, tree = jax.tree.flatten(groups)
    return jax.tree.unflatten(tree, lax.optimization_barrier(tuple(flat)))


class Sums:
    def __init__(self, me_dp, me_e, groups):
        self.d, self.core, self.chip = me_dp, me_e % 2, me_e // 2
        self.chips = groups // 2

    def send_core(self, packed):
        groups, n_dp, r, c = packed.shape
        x = packed.reshape(2, self.chips, n_dp, r, c)
        self.own = at(x, self.core)
        return [swap(at(x, 1 - self.core), "expert", 1)]

    def take_core(self, got):
        self.own = total([self.own] + got).astype(bf16)

    def send_chip(self):
        return [swap(at(self.own, self.chip ^ k), "expert", 2 * k) for k in range(1, self.chips)]

    def take_chip(self, got):
        self.own = total([at(self.own, self.chip)] + got).astype(bf16)

    def send_dp(self):
        return [swap(at(self.own, self.d ^ k), "dp", k) for k in range(1, 4)]

    def take_dp(self, got):
        self.piece = total([at(self.own, self.d)] + got)
        self.own = self.piece.astype(bf16)

    def spread_chip(self):
        return [swap(self.own, "expert", 2 * k) for k in range(1, self.chips)]

    def join_chip(self, got):
        got = jnp.stack([self.own] + got)
        self.own = jnp.concatenate(
            [lax.dynamic_slice_in_dim(got, self.chip ^ k, 1, 0) for k in range(self.chips)]
        )

    def spread_core(self):
        return [swap(self.own, "expert", 1)]

    def join_core(self, got):
        own, other = self.own, got[0]
        x = jnp.stack(
            [jnp.where(self.core == 0, own, other), jnp.where(self.core == 0, other, own)]
        )
        return x.reshape(-1, 128)


def shards(
    tokens,
    cotangent,
    expert_ids,
    priority,
    step,
    attn_qkv,
    attn_out,
    router,
    norms,
    expert_in,
    expert_out,
    moments_qkv,
    moments_out,
    moments_router,
    moments_norms,
    moments_in,
    moments_exp,
):
    tok_dev = tokens.shape[0]
    groups = lax.axis_size("expert")
    n_dp = lax.axis_size("dp")
    assert expert_in.shape[0] == 1 and n_dp == 4 and tok_dev % SEQ == 0
    experts = groups
    per = experts // n_dp
    cap = (tok_dev + experts - 1) // experts
    pad = -(-(cap + 2) // 16) * 16
    n = tok_dev // SEQ
    devices = n_dp * groups
    me_dp = lax.axis_index("dp").astype(i32)
    me_e = lax.axis_index("expert").astype(i32)
    core = me_e % 2
    where = jnp.stack([me_dp, core, me_e])

    qkvT = attn_qkv.astype(bf16).T
    misc = jnp.concatenate(
        [
            router.astype(bf16).T,
            norms.astype(bf16).reshape(1, D),
            jnp.zeros((16 - per - 1, D), bf16),
        ],
        axis=0,
    )
    eighth = me_e % 8
    own = jnp.concatenate(
        [
            lax.dynamic_slice_in_dim(qkvT, eighth * 48, 48, 0),
            lax.dynamic_slice_in_dim(attn_out.astype(bf16), eighth * 16, 16, 0),
            misc,
        ],
        axis=0,
    )
    own_e = jnp.concatenate([expert_in[0].astype(bf16), expert_out[0].astype(bf16)], axis=0)
    ids = expert_ids.reshape(n, SEQ, 2).transpose(0, 2, 1)
    prio = priority.reshape(n, SEQ, 2).transpose(0, 2, 1)
    got = [own] + [swap(own, "dp", k) for k in (1, 2, 3)]
    got, own_e, ids, prio = fence(got, own_e, ids, prio)
    gathered = lax.all_gather(own_e, "dp", axis=0)
    got = jnp.stack(got)
    got, misc = got[:, :64], got[:, 64:]
    near = [swap(got, "expert", 2 * k) for k in (1, 2, 3)]
    pos, cols, up_slots = slots(where, ids, prio, cotangent, experts, cap, pad)
    near, pos, cols, up_slots = fence(near, pos, cols, up_slots)
    far = swap(jnp.stack([got] + near), "expert", 1)
    up = exchange(up_slots, "expert")
    wT, ow, rT, nm = assemble(where, got, misc, jnp.stack(near), far, experts)
    proj, ctxT, lse, mid, sec, gatesT = attend(tokens, wT, ow, rT, nm)

    blocks = spread(pos, sec, pad)
    near = [k for k in range(2, groups) if (k >> 1) & ((k >> 1) - 1) == 0]
    distant = [k for k in range(2, groups) if (k >> 1) & ((k >> 1) - 1)]
    gb, dr, kept = {}, {}, []

    def experts_on(ks, rows):
        g, d, keep = run_experts(where, tuple(ks), rows, up, gathered, rT, cap)
        kept.append(keep)
        for k, gk, dk in zip(ks, g, d):
            gb[k], dr[k] = gk, dk

    send = lambda ks: [swap(blocks[k], "expert", k) for k in ks]
    here, there = [blocks[0]] + send([1]), send(near)
    experts_on([0, 1], here)
    there, kept[0] = fence(there, kept[0])
    ends = [blocks[k] for k in distant]
    ends, there = fence(ends, there)
    last = [swap(b, "expert", k) for k, b in zip(distant, ends)]
    dr[1] = swap(dr[1], "expert", 1)
    experts_on(near, there)
    last, kept[1], dr[1] = fence(last, kept[1], dr[1])
    for k in near:
        dr[k] = swap(dr[k], "expert", k)
    experts_on(distant, last)
    for k in distant:
        dr[k] = swap(dr[k], "expert", k)
    partial = weight_grads(kept, pad)
    dr, gb, partial = fence([dr[k] for k in range(groups)], [gb[k] for k in range(groups)], partial)
    owned = exchange(partial, "dp")
    dmid, dn_two, drT = combine(where, dr, cols, gatesT, sec, mid, cotangent, rT, nm, cap)

    back = functools.partial(attend_back, groups=groups, proj=proj, ctxT=ctxT, lse=lse, ow=ow, nm=nm)
    dmid, gb = fence(dmid, gb)
    split = 1 + 5 * groups // 8
    early = [gb[0]] + [swap(gb[k], "expert", k) for k in range(1, split)]
    late = gb[split:]
    dp0, packed0 = back(0, tok=tokens, dmid=dmid)
    early, late, dmid, dp0, packed0 = fence(early, late, dmid, dp0, packed0)
    sum0, sum1 = Sums(me_dp, me_e, groups), Sums(me_dp, me_e, groups)
    sum0.take_core(sum0.send_core(packed0))
    sum0.own, dmid = fence(sum0.own, dmid)
    late = [swap(b, "expert", k) for k, b in enumerate(late, split)]
    got = sum0.send_chip()
    dp1, packed1 = back(1, tok=tokens, dmid=dmid)
    got, late, dp1, packed1, owned, dmid = fence(got, late, dp1, packed1, owned, dmid)
    sum0.take_chip(got)
    got0, got1 = sum0.send_dp(), sum1.send_core(packed1)
    grad_input, dn_one = enter(tokens, dmid, dp0, dp1, wT, nm)
    got0, got1, grad_input, dn_one, mid = fence(got0, got1, grad_input, dn_one, mid)
    sum0.take_dp(got0)
    sum1.take_core(got1)
    got0, got1 = sum0.spread_chip(), sum1.send_chip()

    dn = jnp.concatenate([dn_one, dn_two], axis=0)
    small = jnp.stack(
        [
            jnp.concatenate(
                [drT[d * per : (d + 1) * per, j * 128 : (j + 1) * 128] for j in range(4)]
                + [dn[:, d * 128 : (d + 1) * 128]],
                axis=0,
            )
            for d in range(n_dp)
        ]
    )
    lines = small.shape[1]
    small = jnp.broadcast_to(small[:, None], (n_dp, groups, lines, 128))
    small = exchange(small.reshape(devices, lines, 128), ("dp", "expert"))
    activations = finish(early + late, cols, mid)
    got0, got1, small, activations = fence(got0, got1, small, activations)
    sum0.join_chip(got0)
    sum1.take_chip(got1)
    got0, got1 = sum0.spread_core(), sum1.send_dp()
    owned = total([owned[d] for d in range(n_dp)])
    small = small.sum(0)
    term = jnp.sum(sum0.piece * sum0.piece) + jnp.sum(owned * owned)
    term = term + jnp.sum(small * small) / groups
    got0, got1, term, owned, small = fence(got0, got1, term, owned, small)
    part0 = sum0.join_core(got0)
    sum1.take_dp(got1)
    term = term + jnp.sum(sum1.piece * sum1.piece)
    terms = exchange(jnp.full((devices, 1, 128), term, f32), ("dp", "expert"))
    sum1.join_chip(sum1.spread_chip())
    part1 = sum1.join_core(sum1.spread_core())
    share_router = jnp.concatenate(
        [small[j * per : (j + 1) * per] for j in range(4)], axis=1
    ).T
    share_norms = small[4 * per :]
    grad_norm = jnp.sqrt(jnp.sum(terms[:, 0, 0]))
    factor = MAX_NORM / grad_norm
    rates = step_rates(experts)
    step_float = step.astype(f32)
    fixes = (1.0 - jnp.power(BETA_ONE, step_float), 1.0 - jnp.power(BETA_TWO, step_float))
    new = adam(
        (rates[0], rates[1], rates[4], rates[5]),
        where,
        jnp.stack([factor, *fixes]),
        part0,
        part1,
        owned,
        (attn_qkv, attn_out, expert_in, expert_out),
        (moments_qkv, moments_out, moments_in, moments_exp),
    )
    new_router = adam_update(
        router, moments_router, share_router, factor, rates[2], DECAY_RATE, fixes
    )
    new_norms = adam_update(norms, moments_norms, share_norms, factor, rates[3], 0.0, fixes)
    return (
        activations,
        grad_input,
        grad_norm,
        *new[:8],
        *new_router,
        *new_norms,
        *new[8:],
    )


def solution(mesh):
    tok = P(("dp", "expert"), None)
    cols = P(None, "dp")
    rows = P("dp", None)
    e_in = P("expert", None, "dp")
    e_out = P("expert", "dp", None)
    in_specs = (
        tok,
        tok,
        tok,
        tok,
        P(),
        cols,
        rows,
        cols,
        cols,
        e_in,
        e_out,
        P(None, None, "dp"),
        P(None, "dp", None),
        P(None, None, "dp"),
        P(None, None, "dp"),
        P(None, "expert", None, "dp"),
        P(None, "expert", "dp", None),
    )
    out_specs = (
        (tok, tok, P())
        + (cols,) * 4
        + (rows,) * 4
        + (cols,) * 4
        + (cols,) * 4
        + (e_in,) * 4
        + (e_out,) * 4
    )
    return jax.shard_map(shards, mesh=mesh, in_specs=in_specs, out_specs=out_specs, check_vma=False)
```

time: 662 us -> 440 us (0.66)
  waiting for transfers between devices: 147 us -> 11.4 us
  blocking collectives: 93.4 us -> 0 us
  local copies, waits for them, and re-layouts: 43.8 us -> 15.2 us
  Pallas kernels: 267 us -> 293 us
  other arithmetic: 38.9 us -> 23 us
  between operations: 6.25 us -> 20.7 us
  starting transfers between devices: 58.7 us -> 70.6 us
    ppermute x18 -> x50, waiting for transfers between devices: 147 us -> 5.07 us  [swap(): return lax.ppermute(x, axis, [(i, i ^ k) for i in range(n)])]
    all_to_all x3 -> x0, blocking collectives: 93.4 us -> none  [exchange(): return lax.all_to_all(x, axis, split_axis=0, concat_axis=0, tiled=True)]
    ppermute x18 -> x50, starting transfers between devices: 26.6 us -> 53.3 us  [swap(): return lax.ppermute(x, axis, [(i, i ^ k) for i in range(n)])]
    pallas_call x8 -> x14, Pallas kernels: 267 us -> 293 us  [the longest x2 68 us: attend_back(): call(functools.partial(attend_back_kernel, part), 'attend_back', grid=(t...]
    unnamed x76 -> x80, local copies, waits for them, and re-layouts: 27.9 us -> 5.94 us
    all_to_all x5 -> x4, starting transfers between devices: 32.1 us -> 17.3 us  [exchange(): return lax.all_to_all(x, axis, split_axis=0, concat_axis=0, tiled=True)]
    convert_element_type x5 -> x2, other arithmetic: 9.49 us -> 1.24 us  [adam_update(): return (updated, first, second, updated.astype(bf16))]
    another operation x10 -> x11, other arithmetic: 13 us -> 5.58 us  [the longest x1 2.08 us: shards(): wT, ow, rT, nm = assemble(where, got, misc, jnp.stack(near), far, experts)]
  transfers between devices with their start and end apart: 23 -> 55, of which waited for: 10 -> 6; matrix products, arithmetic and copies ran while one was open for 10% -> 6% of each run, Pallas kernels for 13% -> 65%
where the time goes in v2:
time: 440 us; the launch traced here: 434 us
  Pallas kernels  293 us (67%)
  starting transfers between devices  70.6 us (16%)
  other arithmetic  23 us (5%)
  between operations  20.7 us (5%)
  local copies, waits for them, and re-layouts  15.2 us (3%)
  waiting for transfers between devices  11.4 us (3%)
    pallas_call x2, Pallas kernels, attend_back(): call(functools.partial(attend_back_kernel, part), 'attend_back', grid=(t...  68 us
    pallas_call x3, Pallas kernels, run_experts(): call(functools.partial(experts_kernel, cap, ks), 'experts', us=8 * nb, gr...  59 us
    ppermute x50, starting transfers between devices, swap(): return lax.ppermute(x, axis, [(i, i ^ k) for i in range(n)])  53.3 us
    pallas_call x1, Pallas kernels, attend(): call(attend_kernel, 'attend', grid=(n,), in_specs=[per_image(D), full(wT)...  40.6 us
    pallas_call x1, Pallas kernels, combine(): call(functools.partial(combine_kernel, cap, experts), 'combine', grid=(t...  30.8 us
    pallas_call x1, Pallas kernels, weight_grads(): call(functools.partial(weights_kernel, groups), 'weight_grads', grid=(FF...  21.9 us
    pallas_call x1, Pallas kernels, slots(): call(functools.partial(slots_kernel, cap, pad), 'slots', grid=(experts,),...  17.6 us
    all_to_all x4, starting transfers between devices, exchange(): return lax.all_to_all(x, axis, split_axis=0, concat_axis=0, tiled=True)  17.3 us
  transfers between devices with their start and end apart: 55, of which 6 were waited for; matrix products, arithmetic and copies ran while one was open for 6% of the time, Pallas kernels for 65%

profile of v2, /device:TPU:0, one launch (start us, length us, event | category | flops | bytes accessed | tf_op | source)
XLA Modules:
  0.0 434.3 jit_solution(15711350016004490487)
XLA Ops:
  11.0 3.1 collective-permute-start
  14.0 2.6 collective-permute-start.1
  27.6 17.6 %slots.1 = (s32[4,8,720]{2,1,0:T(8,128)}, s32[2880,8]{1,0:T(8,128)}, bf16[8,368,512]{2,1,0:T(8,128)(2,1)}) custom-call(s32[3]{0:T(128)} %pad_add_fusion.where, s32[4,2,720]{2,1,0:T(2,128)} %bitcast.162, s32[4,2,720]{2,1,0:T(2,128)} %bitcast.163, bf16[2880,512]{1,0:T(8,128)(2,1)} %refs_12_.1), custom_call_target="tpu_custom_call" | custom-call | flops 100000000 | bytes 100000 | tf_op jit(solution)/shard_map/slots/pallas_call | solution.py:193
  46.1 3.8 all-to-all-start
  55.1 3.8 assemble.1
  58.9 40.6 %attend.1 = (bf16[2880,1536]{1,0:T(8,128)(2,1)}, bf16[4,512,720]{2,1,0:T(8,128)(2,1)}, f32[4,8,720]{2,1,0:T(8,128)}, f32[2880,512]{1,0:T(8,128)}, bf16[2880,512]{1,0:T(8,128)(2,1)}, /*index=5*/f32[4,8,720]{2,1,0:T(8,128)}) custom-call(bf16[2880,512]{1,0:T(8,128)(2,1)} %tok.7, bf16[1536,512]{1,0:T(8,128)(2,1)} %get-tuple-element.218.wT, ...), custom_call_target="tpu_custom_call" | custom-call | flops 100000000 | bytes 100000 | tf_op jit(solution)/shard_map/attend/pallas_call | solution.py:267
  99.5 15.0 %spread.1 = (bf16[368,512]{1,0:T(8,128)(2,1)}, bf16[368,512]{1,0:T(8,128)(2,1)}, bf16[368,512]{1,0:T(8,128)(2,1)}, bf16[368,512]{1,0:T(8,128)(2,1)}, bf16[368,51...) custom-call(s32[4,8,720]{2,1,0:T(8,128)} %get-tuple-element.214.pos, ...), custom_call_target="tpu_custom_call" | custom-call | flops 100000000 | bytes 100000 | tf_op jit(solution)/shard_map/spread/pallas_call | solution.py:219
  120.0 15.1 %experts.3 = (bf16[368,512]{1,0:T(8,128)(2,1)}, bf16[368,512]{1,0:T(8,128)(2,1)}, bf16[368,512]{1,0:T(8,128)(2,1)}, bf16[368,512]{1,0:T(8,128)(2,1)}, bf16[736,5...) custom-call(s32[3]{0:T(128)} %pad_add_fusion.where, ...), custom_call_target="tpu_custom_call" | custom-call | flops 16000000000 | bytes 100000 | tf_op jit(solution)/shard_map/experts/pallas_call | solution.py:380
  135.6 2.8 collective-permute-start.12
  138.6 28.9 %experts.4 = (bf16[368,512]{1,0:T(8,128)(2,1)}, bf16[368,512]{1,0:T(8,128)(2,1)}, bf16[368,512]{1,0:T(8,128)(2,1)}, bf16[368,512]{1,0:T(8,128)(2,1)}, bf16[368,5...) custom-call(s32[3]{0:T(128)} %pad_add_fusion.where, ...), custom_call_target="tpu_custom_call" | custom-call | flops 32000000000 | bytes 100000 | tf_op jit(solution)/shard_map/experts/pallas_call | solution.py:380
  171.8 15.0 %experts.5 = (bf16[368,512]{1,0:T(8,128)(2,1)}, bf16[368,512]{1,0:T(8,128)(2,1)}, bf16[368,512]{1,0:T(8,128)(2,1)}, bf16[368,512]{1,0:T(8,128)(2,1)}, bf16[736,5...) custom-call(s32[3]{0:T(128)} %pad_add_fusion.where, ...), custom_call_target="tpu_custom_call" | custom-call | flops 16000000000 | bytes 100000 | tf_op jit(solution)/shard_map/experts/pallas_call | solution.py:380
  189.5 21.9 %weight_grads.1 = bf16[4,1024,512]{2,1,0:T(8,128)(2,1)} custom-call(bf16[736,512]{1,0:T(8,128)(2,1)} %get-tuple-element.270.refs_0_, bf16[1472,512]{1,0:T(8,128)(2,1)} %get-tuple-element.271.refs_1_, bf16[736,512]{1,0:T(8,128)(2,1)} %get-tuple-element.272.refs_2_, bf16[736,512]{1,0:T(8,128)(2,1)} %get-tuple-element.273.refs_3_, ...), custom_call_target="tpu_custom_call" | custom-call | flops 100000000 | bytes 100000 | tf_op jit(solution)/shard_map/weight_grads/pallas_call | solution.py:427
  212.7 4.9 %all-to-all-start.1 = ((bf16[4,1024,512]{2,1,0:T(8,128)(2,1)}), bf16[4,1024,512]{2,1,0:T(8,128)(2,1)}, u32[]{:S(2)}, u32[]{:S(2)}) async-start(bf16[4,1024,512]{2,1,0:T(8,128)(2,1)} %weight_grads.1), calls=%async_computation.1 | async-start | bytes 8388608 | tf_op jit(solution)/shard_map/all_to_all | solution.py:788
  217.6 30.8 %combine.1 = (f32[2880,512]{1,0:T(8,128)}, f32[2,512]{1,0:T(2,128)}, f32[8,512]{1,0:T(8,128)}) custom-call(s32[3]{0:T(128)} %pad_add_fusion.where, bf16[368,512]{1,0:T(8,128)(2,1)} %get-tuple-element.282.refs_0_, bf16[368,512]{1,0:T(8,128)(2,1)} %copy-done.15, bf16[368,512]{1,0:T(8,128)(2,1)} %copy-done.16, bf16[368,512]{1,0:T(8,128)(2,1)} %copy-done.17, ...), custom_call_target="tpu_custom_call" | custom-call | flops 100000000 | bytes 100000 | tf_op jit(solution)/shard_map/combine/pallas_call | solution.py:496
  252.4 34.0 %attend_back.2 = (bf16[2880,768]{1,0:T(8,128)(2,1)}, bf16[8,4,128,128]{3,2,1,0:T(8,128)(2,1)}) custom-call(bf16[2880,512]{1,0:T(8,128)(2,1)} %tok.7, f32[2880,512]{1,0:T(8,128)} %get-tuple-element.329.dmid, bf16[2880,1536]{1,0:T(8,128)(2,1)} %get-tuple-element.311.proj, bf16[4,512,720]{2,1,0:T(8,128)(2,1)} %get-tuple-element.312.ctxT, ...), custom_call_target="tpu_custom_call" | custom-call | flops 100000000 | bytes 100000 | tf_op jit(solution)/shard_map/attend_back/pallas_call | solution.py:619
  296.9 34.1 %attend_back.3 = (bf16[2880,768]{1,0:T(8,128)(2,1)}, bf16[8,4,128,128]{3,2,1,0:T(8,128)(2,1)}) custom-call(bf16[2880,512]{1,0:T(8,128)(2,1)} %tok.7, f32[2880,512]{1,0:T(8,128)} %get-tuple-element.329.dmid, bf16[2880,1536]{1,0:T(8,128)(2,1)} %get-tuple-element.311.proj, bf16[4,512,720]{2,1,0:T(8,128)(2,1)} %get-tuple-element.312.ctxT, ...), custom_call_target="tpu_custom_call" | custom-call | flops 100000000 | bytes 100000 | tf_op jit(solution)/shard_map/attend_back/pallas_call | solution.py:619
  337.6 13.1 %enter.1 = (f32[2880,512]{1,0:T(8,128)}, f32[2,512]{1,0:T(2,128)}) custom-call(bf16[2880,512]{1,0:T(8,128)(2,1)} %tok.7, f32[2880,512]{1,0:T(8,128)} %get-tuple-element.329.dmid, bf16[2880,768]{1,0:T(8,128)(2,1)} %get-tuple-element.330.dp0, bf16[2880,768]{1,0:T(8,128)(2,1)} %get-tuple-element.331.dp1, bf16[1536,512]{1,0:T(8,128)(2,1)} %get-tuple-element.218.wT, ...), custom_call_target="tpu_custom_call" | custom-call | flops 100000000 | bytes 100000 | tf_op jit(solution)/shard_map/enter/pallas_call | solution.py:673
  356.5 5.9 %all-to-all-start.2 = ((f32[32,12,128]{2,1,0:T(8,128)}), f32[32,12,128]{2,1,0:T(8,128)S(1)}, u32[]{:S(2)}, u32[]{:S(2)}) async-start(f32[32,12,128]{2,1,0:T(8,128)} %bitcast.39), calls=%async_computation.2 | async-start | bytes 524288 | tf_op jit(solution)/shard_map/all_to_all | solution.py:788
  366.2 4.7 %multiply_reduce_fusion = (f32[]{:T(128)}, f32[1024,512]{1,0:T(8,128)}) fusion(bf16[4,1024,512]{2,1,0:T(8,128)(2,1)} %all-to-all-done.1), kind=kLoop, calls=%fused_computation | loop fusion | flops 4718591 | bytes 6291460 | tf_op jit(solution)/shard_map/reduce_sum | solution.py:993
  372.2 13.9 %finish.1 = bf16[2880,512]{1,0:T(8,128)(2,1)} custom-call(bf16[368,512]{1,0:T(8,128)(2,1)} %get-tuple-element.341.refs_0_, bf16[368,512]{1,0:T(8,128)(2,1)} %copy-done.8, bf16[368,512]{1,0:T(8,128)(2,1)} %copy-done.9, bf16[368,512]{1,0:T(8,128)(2,1)} %copy-done.10, bf16[368,512]{1,0:T(8,128)(2,1)} %copy-done.11, bf16[368,512]{1,0:T(8,128)(2,1)} %copy-done.12, ...), custom_call_target="tpu_custom_call" | custom-call | flops 100000000 | bytes 100000 | tf_op jit(solution)/shard_map/finish/pallas_call | solution.py:527
  393.8 2.7 collective-permute-done.45
  401.9 2.8 all-to-all-start.3
  405.4 6.3 %all-to-all-done.3 = f32[32,1,128]{2,1,0:T(1,128)S(1)} async-done(((f32[32,1,128]{2,1,0:T(1,128)}), f32[32,1,128]{2,1,0:T(1,128)S(1)}, u32[]{:S(2)}, u32[]{:S(2)}) %all-to-all-start.3) | async-done | bytes 16416 | tf_op jit(solution)/shard_map/all_to_all | solution.py:788
  416.0 9.8 %adam.1 = (f32[512,384]{1,0:T(8,128)}, f32[512,384]{1,0:T(8,128)}, f32[512,384]{1,0:T(8,128)}, bf16[512,384]{1,0:T(8,128)(2,1)}, f32[128,512]{1,0:T(8,128)}, /*i...) custom-call(s32[3]{0:T(128)} %pad_add_fusion.where, ...), custom_call_target="tpu_custom_call" | custom-call | flops 100000000 | bytes 100000 | tf_op jit(solution)/shard_map/adam/pallas_call | solution.py:771
  (239 shorter events, 80.7 us)
Async XLA Ops:
  7.2 111.2 %all-gather.3.cloned.1.call-start = ((), (), s32[]{:S(2)}) async-start(), calls=%async_computation.4 | async-start | bytes 5242880 | tf_op jit(solution)/shard_map/all_gather | solution.py:908
  46.1 72.3 %all-to-all-start = ((bf16[8,368,512]{2,1,0:T(8,128)(2,1)}), bf16[8,368,512]{2,1,0:T(8,128)(2,1)S(1)}, u32[]{:S(2)}, u32[]{:S(2)}) async-start(bf16[8,368,512]{2,1,0:T(8,128)(2,1)} %get-tuple-element.225), calls=%async_computation | async-start | bytes 6029312 | tf_op jit(solution)/shard_map/all_to_all | solution.py:788
  135.6 34.0 %collective-permute-start.12 = (bf16[368,512]{1,0:T(8,128)(2,1)}, bf16[368,512]{1,0:T(8,128)(2,1)S(1)}, u32[]{:S(2)}, u32[]{:S(2)}) collective-permute-start(bf16[368,512]{1,0:T(8,128)(2,1)} %get-tuple-element.242), channel_id=1, source_target_pairs={{0,6},{1,7},{2,4},{3,5},{4,2},{5,3},{6,0},{7,1},{8,14},{9,15},{10,... | collective-permute-start | bytes 1130504 | tf_op jit(solution)/shard_map/ppermute | solution.py:784
  138.4 32.7 %collective-permute-start.13 = (bf16[368,512]{1,0:T(8,128)(2,1)S(1)}, bf16[368,512]{1,0:T(8,128)(2,1)S(1)}, u32[]{:S(2)}, u32[]{:S(2)}) collective-permute-start(bf16[368,512]{1,0:T(8,128)(2,1)S(1)} %copy-done.36), channel_id=1, source_target_pairs={{0,7},{1,6},{2,5},{3,4},{4,3},{5,2},{6,1},{7,0},{8,15},{9,14},{10,... | collective-permute-start | bytes 1130504 | tf_op jit(solution)/shard_map/ppermute | solution.py:784
  138.4 33.0 %collective-permute-start.14 = (bf16[368,512]{1,0:T(8,128)(2,1)}, bf16[368,512]{1,0:T(8,128)(2,1)S(1)}, u32[]{:S(2)}, u32[]{:S(2)}) collective-permute-start(bf16[368,512]{1,0:T(8,128)(2,1)} %get-tuple-element.252), channel_id=1, source_target_pairs={{0,1},{1,0},{2,3},{3,2},{4,5},{5,4},{6,7},{7,6},{8,9},{9,8},{10,11... | collective-permute-start | bytes 1130504 | tf_op jit(solution)/shard_map/ppermute | solution.py:784
  169.5 41.9 %collective-permute-start.16 = (bf16[368,512]{1,0:T(8,128)(2,1)}, bf16[368,512]{1,0:T(8,128)(2,1)S(1)}, u32[]{:S(2)}, u32[]{:S(2)}) collective-permute-start(bf16[368,512]{1,0:T(8,128)(2,1)} %get-tuple-element.255), channel_id=1, source_target_pairs={{0,3},{1,2},{2,1},{3,0},{4,7},{5,6},{6,5},{7,4},{8,11},{9,10},{10,... | collective-permute-start | bytes 1130504 | tf_op jit(solution)/shard_map/ppermute | solution.py:784
  169.6 41.9 %collective-permute-start.17 = (bf16[368,512]{1,0:T(8,128)(2,1)}, bf16[368,512]{1,0:T(8,128)(2,1)S(1)}, u32[]{:S(2)}, u32[]{:S(2)}) collective-permute-start(bf16[368,512]{1,0:T(8,128)(2,1)} %get-tuple-element.256), channel_id=1, source_target_pairs={{0,4},{1,5},{2,6},{3,7},{4,0},{5,1},{6,2},{7,3},{8,12},{9,13},{10,... | collective-permute-start | bytes 1130504 | tf_op jit(solution)/shard_map/ppermute | solution.py:784
  171.1 40.4 %collective-permute-start.18 = (bf16[368,512]{1,0:T(8,128)(2,1)}, bf16[368,512]{1,0:T(8,128)(2,1)S(1)}, u32[]{:S(2)}, u32[]{:S(2)}) collective-permute-start(bf16[368,512]{1,0:T(8,128)(2,1)} %get-tuple-element.257), channel_id=1, source_target_pairs={{0,5},{1,4},{2,7},{3,6},{4,1},{5,0},{6,3},{7,2},{8,13},{9,12},{10,... | collective-permute-start | bytes 1130504 | tf_op jit(solution)/shard_map/ppermute | solution.py:784
  186.9 24.6 %collective-permute-start.19 = (bf16[368,512]{1,0:T(8,128)(2,1)}, bf16[368,512]{1,0:T(8,128)(2,1)S(1)}, u32[]{:S(2)}, u32[]{:S(2)}) collective-permute-start(bf16[368,512]{1,0:T(8,128)(2,1)} %get-tuple-element.260), channel_id=1, source_target_pairs={{0,6},{1,7},{2,4},{3,5},{4,2},{5,3},{6,0},{7,1},{8,14},{9,15},{10,... | collective-permute-start | bytes 1130504 | tf_op jit(solution)/shard_map/ppermute | solution.py:784
  212.7 118.4 %all-to-all-start.1 = ((bf16[4,1024,512]{2,1,0:T(8,128)(2,1)}), bf16[4,1024,512]{2,1,0:T(8,128)(2,1)}, u32[]{:S(2)}, u32[]{:S(2)}) async-start(bf16[4,1024,512]{2,1,0:T(8,128)(2,1)} %weight_grads.1), calls=%async_computation.1 | async-start | bytes 8388608 | tf_op jit(solution)/shard_map/all_to_all | solution.py:788
  248.4 38.0 %collective-permute-start.21 = (bf16[368,512]{1,0:T(8,128)(2,1)S(1)}, bf16[368,512]{1,0:T(8,128)(2,1)S(1)}, u32[]{:S(2)}, u32[]{:S(2)}) collective-permute-start(bf16[368,512]{1,0:T(8,128)(2,1)S(1)} %copy-done.32), channel_id=1, source_target_pairs={{0,1},{1,0},{2,3},{3,2},{4,5},{5,4},{6,7},{7,6},{8,9},{9,8},{10,11... | collective-permute-start | bytes 1130504 | tf_op jit(solution)/shard_map/ppermute | solution.py:784
  248.9 37.5 %collective-permute-start.22 = (bf16[368,512]{1,0:T(8,128)(2,1)}, bf16[368,512]{1,0:T(8,128)(2,1)S(1)}, u32[]{:S(2)}, u32[]{:S(2)}) collective-permute-start(bf16[368,512]{1,0:T(8,128)(2,1)} %get-tuple-element.304), channel_id=1, source_target_pairs={{0,2},{1,3},{2,0},{3,1},{4,6},{5,7},{6,4},{7,5},{8,10},{9,11},{10,... | collective-permute-start | bytes 1130504 | tf_op jit(solution)/shard_map/ppermute | solution.py:784
  250.3 36.2 %collective-permute-start.23 = (bf16[368,512]{1,0:T(8,128)(2,1)S(1)}, bf16[368,512]{1,0:T(8,128)(2,1)S(1)}, u32[]{:S(2)}, u32[]{:S(2)}) collective-permute-start(bf16[368,512]{1,0:T(8,128)(2,1)S(1)} %copy-done.35), channel_id=1, source_target_pairs={{0,3},{1,2},{2,1},{3,0},{4,7},{5,6},{6,5},{7,4},{8,11},{9,10},{10,... | collective-permute-start | bytes 1130504 | tf_op jit(solution)/shard_map/ppermute | solution.py:784
  250.4 36.1 %collective-permute-start.24 = (bf16[368,512]{1,0:T(8,128)(2,1)S(1)}, bf16[368,512]{1,0:T(8,128)(2,1)S(1)}, u32[]{:S(2)}, u32[]{:S(2)}) collective-permute-start(bf16[368,512]{1,0:T(8,128)(2,1)S(1)} %copy-done.34), channel_id=1, source_target_pairs={{0,4},{1,5},{2,6},{3,7},{4,0},{5,1},{6,2},{7,3},{8,12},{9,13},{10,... | collective-permute-start | bytes 1130504 | tf_op jit(solution)/shard_map/ppermute | solution.py:784
  251.8 34.7 %collective-permute-start.25 = (bf16[368,512]{1,0:T(8,128)(2,1)S(1)}, bf16[368,512]{1,0:T(8,128)(2,1)S(1)}, u32[]{:S(2)}, u32[]{:S(2)}) collective-permute-start(bf16[368,512]{1,0:T(8,128)(2,1)S(1)} %copy-done.33), channel_id=1, source_target_pairs={{0,5},{1,4},{2,7},{3,6},{4,1},{5,0},{6,3},{7,2},{8,13},{9,12},{10,... | collective-permute-start | bytes 1130504 | tf_op jit(solution)/shard_map/ppermute | solution.py:784
  288.6 42.4 %collective-permute-start.30 = (bf16[368,512]{1,0:T(8,128)(2,1)}, bf16[368,512]{1,0:T(8,128)(2,1)S(1)}, u32[]{:S(2)}, u32[]{:S(2)}) collective-permute-start(bf16[368,512]{1,0:T(8,128)(2,1)} %get-tuple-element.319), channel_id=1, source_target_pairs={{0,6},{1,7},{2,4},{3,5},{4,2},{5,3},{6,0},{7,1},{8,14},{9,15},{10,... | collective-permute-start | bytes 1130504 | tf_op jit(solution)/shard_map/ppermute | solution.py:784
  291.0 40.0 %collective-permute-start.31 = (bf16[368,512]{1,0:T(8,128)(2,1)}, bf16[368,512]{1,0:T(8,128)(2,1)S(1)}, u32[]{:S(2)}, u32[]{:S(2)}) collective-permute-start(bf16[368,512]{1,0:T(8,128)(2,1)} %get-tuple-element.320), channel_id=1, source_target_pairs={{0,7},{1,6},{2,5},{3,4},{4,3},{5,2},{6,1},{7,0},{8,15},{9,14},{10,... | collective-permute-start | bytes 1130504 | tf_op jit(solution)/shard_map/ppermute | solution.py:784
  292.6 38.5 %collective-permute-start.27 = (bf16[4,128,128]{2,1,0:T(8,128)(2,1)S(1)}, bf16[4,128,128]{2,1,0:T(8,128)(2,1)S(1)}, u32[]{:S(2)}, u32[]{:S(2)}) collective-permute-start(bf16[4,128,128]{2,1,0:T(8,128)(2,1)S(1)} %get-tuple-element.398), channel_id=1, source_target_pairs={{0,2},{1,3},{2,0},{3,1},{4,6},{5,7},{6,4},{7,5},{8,10},{9,11},{10,... | collective-permute-start | bytes 393224 | tf_op jit(solution)/shard_map/ppermute | solution.py:784
  294.0 37.1 %collective-permute-start.28 = (bf16[4,128,128]{2,1,0:T(8,128)(2,1)S(1)}, bf16[4,128,128]{2,1,0:T(8,128)(2,1)S(1)}, u32[]{:S(2)}, u32[]{:S(2)}) collective-permute-start(bf16[4,128,128]{2,1,0:T(8,128)(2,1)S(1)} %get-tuple-element.397), channel_id=1, source_target_pairs={{0,4},{1,5},{2,6},{3,7},{4,0},{5,1},{6,2},{7,3},{8,12},{9,13},{10,... | collective-permute-start | bytes 393224 | tf_op jit(solution)/shard_map/ppermute | solution.py:784
  295.5 35.6 %collective-permute-start.29 = (bf16[4,128,128]{2,1,0:T(8,128)(2,1)S(1)}, bf16[4,128,128]{2,1,0:T(8,128)(2,1)S(1)}, u32[]{:S(2)}, u32[]{:S(2)}) collective-permute-start(bf16[4,128,128]{2,1,0:T(8,128)(2,1)S(1)} %get-tuple-element.396), channel_id=1, source_target_pairs={{0,6},{1,7},{2,4},{3,5},{4,2},{5,3},{6,0},{7,1},{8,14},{9,15},{10,... | collective-permute-start | bytes 393224 | tf_op jit(solution)/shard_map/ppermute | solution.py:784
  352.7 33.3 %collective-permute-start.37 = (bf16[128,128]{1,0:T(8,128)(2,1)S(1)}, bf16[128,128]{1,0:T(8,128)(2,1)S(1)}, u32[]{:S(2)}, u32[]{:S(2)}) collective-permute-start(bf16[128,128]{1,0:T(8,128)(2,1)S(1)} %get-tuple-element.408), channel_id=1, source_target_pairs={{0,4},{1,5},{2,6},{3,7},{4,0},{5,1},{6,2},{7,3},{8,12},{9,13},{10,... | collective-permute-start | bytes 98312 | tf_op jit(solution)/shard_map/ppermute | solution.py:784
  354.2 31.9 %collective-permute-start.38 = (bf16[128,128]{1,0:T(8,128)(2,1)S(1)}, bf16[128,128]{1,0:T(8,128)(2,1)S(1)}, u32[]{:S(2)}, u32[]{:S(2)}) collective-permute-start(bf16[128,128]{1,0:T(8,128)(2,1)S(1)} %get-tuple-element.408), channel_id=1, source_target_pairs={{0,6},{1,7},{2,4},{3,5},{4,2},{5,3},{6,0},{7,1},{8,14},{9,15},{10,... | collective-permute-start | bytes 98312 | tf_op jit(solution)/shard_map/ppermute | solution.py:784
  356.5 29.6 %all-to-all-start.2 = ((f32[32,12,128]{2,1,0:T(8,128)}), f32[32,12,128]{2,1,0:T(8,128)S(1)}, u32[]{:S(2)}, u32[]{:S(2)}) async-start(f32[32,12,128]{2,1,0:T(8,128)} %bitcast.39), calls=%async_computation.2 | async-start | bytes 524288 | tf_op jit(solution)/shard_map/all_to_all | solution.py:788
  362.6 23.5 %collective-permute-start.39 = (bf16[4,128,128]{2,1,0:T(8,128)(2,1)S(1)}, bf16[4,128,128]{2,1,0:T(8,128)(2,1)S(1)}, u32[]{:S(2)}, u32[]{:S(2)}) collective-permute-start(bf16[4,128,128]{2,1,0:T(8,128)(2,1)S(1)} %get-tuple-element.395), channel_id=1, source_target_pairs={{0,2},{1,3},{2,0},{3,1},{4,6},{5,7},{6,4},{7,5},{8,10},{9,11},{10,... | collective-permute-start | bytes 393224 | tf_op jit(solution)/shard_map/ppermute | solution.py:784
  (70 other events, 1078.2 us)
Sparse Core Ops, SparseCore 0:
  23.4 82.0 all-gather.2

commit v3 on v2

--- a/solution.py
+++ b/solution.py
@@ -55,6 +55,7 @@
 
 
 SMEM = pl.BlockSpec(memory_space=pltpu.SMEM)
+ANY = pl.BlockSpec(memory_space=pl.ANY)
 
 
 def call(body, name, us=0.1, **kw):
@@ -118,112 +119,110 @@
     )(where, *args)
 
 
-def dispatch(pos, x, pad, step):
-    io = lax.broadcasted_iota(i32, (pad, SEQ), 0)
-    acc = None
-    for i in range(pos.shape[0]):
-        hit = jnp.where(io == pos[i, pl.ds(step, 1), :], 1.0, 0.0).astype(bf16)
-        part = mm(hit, x[i * SEQ : (i + 1) * SEQ, :])
-        acc = part if acc is None else acc + part
-    return acc.astype(bf16)
-
-
-def slots_kernel(cap, pad, where, ids, prio, cot, pos, cols, u):
-    step = pl.program_id(0)
+def route_kernel(cap, pad, where, ids, prio, pos, cols):
     me = where[2]
     n = ids.shape[0]
     experts = pos.shape[1]
     nh = -(-(2 * n * SEQ) // 2048) * 16
 
-    @pl.when(step == 0)
-    def _():
-        hi_io = lax.broadcasted_iota(i32, (nh, SEQ), 0)
-        lo_io = lax.broadcasted_iota(i32, (128, SEQ), 0)
-
-        def hot(i, k):
-            q = prio[i, k : k + 1, :]
-            return hi_io == (q >> 7), lo_io == (q & 127)
-
-        table = jnp.zeros((nh, 128), f32)
-        for i in range(n):
-            for k in range(2):
-                a, b = hot(i, k)
-                ex = ((ids[i, k : k + 1, :] ^ me) + 1).astype(f32)
-                table += mm(
-                    jnp.where(a, 1.0, 0.0).astype(bf16), jnp.where(b, ex, 0.0).astype(bf16), NT
-                )
-        upper = (
-            lax.broadcasted_iota(i32, (128, 128), 0) < lax.broadcasted_iota(i32, (128, 128), 1)
-        ).astype(bf16)
-        lower = (
-            lax.broadcasted_iota(i32, (nh, nh), 1) < lax.broadcasted_iota(i32, (nh, nh), 0)
-        ).astype(bf16)
-        ones = jnp.ones((128, 128), bf16)
-        rank = jnp.zeros((nh, 128), f32)
-        for e in range(experts):
-            m = (table == float(e + 1)).astype(f32)
-            mb = m.astype(bf16)
-            rank += m * (mm(mb, upper) + mm(mm(lower, mb).astype(bf16), ones))
-        ri = jnp.minimum(rank.astype(i32), 16383)
-        rlo = (ri & 127).astype(bf16)
-        rhi = (ri >> 7).astype(bf16)
-        eio = lax.broadcasted_iota(i32, (experts, SEQ), 0)
-        for i in range(n):
-            out = jnp.full((experts, SEQ), FAR, i32)
-            flat = []
-            for k in range(2):
-                a, b = hot(i, k)
-                bb = jnp.where(b, 1.0, 0.0).astype(bf16)
-                x = mm(rlo, bb) + 128.0 * mm(rhi, bb)
-                r = jnp.sum(jnp.where(a, x, 0.0), axis=0, keepdims=True).astype(i32)
-                ex = ids[i, k : k + 1, :] ^ me
-                keep = r < cap
-                out = jnp.where((eio == ex) & keep, r, out)
-                flat.append(jnp.where(keep, ex * pad + r, FAR))
-            pos[i] = out
-            fl = jnp.concatenate(flat + [jnp.zeros((6, SEQ), i32)], axis=0).astype(f32)
-            cols[i * SEQ : (i + 1) * SEQ, :] = fl.T.astype(i32)
-
-    u[pl.ds(step ^ me, 1)] = dispatch(pos, cot, pad, step)[None]
-
-
-def slots(where, ids, prio, cot, experts, cap, pad):
+    hi_io = lax.broadcasted_iota(i32, (nh, SEQ), 0)
+    lo_io = lax.broadcasted_iota(i32, (128, SEQ), 0)
+
+    def hot(i, k):
+        q = prio[i, k : k + 1, :]
+        return hi_io == (q >> 7), lo_io == (q & 127)
+
+    table = jnp.zeros((nh, 128), f32)
+    for i in range(n):
+        for k in range(2):
+            a, b = hot(i, k)
+            ex = ((ids[i, k : k + 1, :] ^ me) + 1).astype(f32)
+            table += mm(
+                jnp.where(a, 1.0, 0.0).astype(bf16), jnp.where(b, ex, 0.0).astype(bf16), NT
+            )
+    upper = (
+        lax.broadcasted_iota(i32, (128, 128), 0) < lax.broadcasted_iota(i32, (128, 128), 1)
+    ).astype(bf16)
+    lower = (
+        lax.broadcasted_iota(i32, (nh, nh), 1) < lax.broadcasted_iota(i32, (nh, nh), 0)
+    ).astype(bf16)
+    ones = jnp.ones((128, 128), bf16)
+    rank = jnp.zeros((nh, 128), f32)
+    for e in range(experts):
+        m = (table == float(e + 1)).astype(f32)
+        mb = m.astype(bf16)
+        rank += m * (mm(mb, upper) + mm(mm(lower, mb).astype(bf16), ones))
+    ri = jnp.minimum(rank.astype(i32), 16383)
+    rlo = (ri & 127).astype(bf16)
+    rhi = (ri >> 7).astype(bf16)
+    eio = lax.broadcasted_iota(i32, (experts, SEQ), 0)
+    for i in range(n):
+        out = jnp.full((experts, SEQ), FAR, i32)
+        flat = []
+        for k in range(2):
+            a, b = hot(i, k)
+            bb = jnp.where(b, 1.0, 0.0).astype(bf16)
+            x = mm(rlo, bb) + 128.0 * mm(rhi, bb)
+            r = jnp.sum(jnp.where(a, x, 0.0), axis=0, keepdims=True).astype(i32)
+            ex = ids[i, k : k + 1, :] ^ me
+            keep = r < cap
+            out = jnp.where((eio == ex) & keep, r, out)
+            flat.append(jnp.where(keep, ex * pad + r, FAR))
+        pos[i] = out
+        fl = jnp.concatenate(flat + [jnp.zeros((6, SEQ), i32)], axis=0).astype(f32)
+        cols[i * SEQ : (i + 1) * SEQ, :] = fl.T.astype(i32)
+
+
+def route(where, ids, prio, experts, cap, pad):
     n = ids.shape[0]
     t = n * SEQ
     return call(
-        functools.partial(slots_kernel, cap, pad),
-        "slots",
-        grid=(experts,),
-        in_specs=[SMEM, full(ids), full(prio), full(cot)],
-        out_specs=[whole(n, experts, SEQ), whole(t, 8), whole(experts, pad, D)],
-        out_shape=[
-            sds((n, experts, SEQ), i32),
-            sds((t, 8), i32),
-            sds((experts, pad, D), bf16),
-        ],
-    )(where, ids, prio, cot)
-
-
-def spread_kernel(pad, pos, x, *outs):
+        functools.partial(route_kernel, cap, pad),
+        "route",
+        in_specs=[SMEM, whole(*ids.shape), whole(*prio.shape)],
+        out_specs=[whole(n, experts, SEQ), whole(t, 8)],
+        out_shape=[sds((n, experts, SEQ), i32), sds((t, 8), i32)],
+    )(where, ids, prio)
+
+
+def spread_kernel(pad, together, where, pos, x, *outs):
     step = pl.program_id(0)
-    block = dispatch(pos, x, pad, step)
-    for j, out in enumerate(outs):
-
-        @pl.when(step == j)
-        def _(out=out):
-            out[...] = block
-
-
-def spread(pos, x, pad):
+    io = lax.broadcasted_iota(i32, (pad, SEQ), 0)
+    acc = None
+    for i in range(pos.shape[0]):
+        hit = [
+            jnp.where(io == pos[i, pl.ds(2 * step + o, 1), :], 1.0, 0.0).astype(bf16)
+            for o in range(2)
+        ]
+        part = mm(jnp.concatenate(hit, axis=0), x[i * SEQ : (i + 1) * SEQ, :])
+        acc = part if acc is None else acc + part
+    block = acc.astype(bf16)
+    for o in range(2):
+        half = block[o * pad : (o + 1) * pad, :]
+        if together:
+            outs[0][pl.ds((2 * step + o) ^ where[2], 1)] = half[None]
+            continue
+        for j in range(o, len(outs), 2):
+
+            @pl.when(2 * step + o == j)
+            def _(j=j, half=half):
+                outs[j][...] = half
+
+
+def spread(where, pos, x, pad, together):
     experts = pos.shape[1]
+    if together:
+        out_specs, out_shape = whole(experts, pad, D), sds((experts, pad, D), bf16)
+    else:
+        out_specs, out_shape = [whole(pad, D)] * experts, [sds((pad, D), bf16)] * experts
     return call(
-        functools.partial(spread_kernel, pad),
+        functools.partial(spread_kernel, pad, together),
         "spread",
-        grid=(experts,),
-        in_specs=[full(pos), full(x)],
-        out_specs=[whole(pad, D)] * experts,
-        out_shape=[sds((pad, D), bf16)] * experts,
-    )(pos, x)
+        grid=(experts // 2,),
+        in_specs=[SMEM, full(pos), full(x)],
+        out_specs=out_specs,
+        out_shape=out_shape,
+    )(where, pos, x)
 
 
 def head_masks():
@@ -290,42 +289,28 @@
 
 
 def normal_cdf(h):
-    t = 1.0 / (1.0 + (0.3275911 * 0.7071067811865476) * jnp.abs(h))
-    g = jnp.exp2((-0.5 * LOG2E) * h * h)
-    poly = t * (
-        0.5 * 0.254829592
-        + t
-        * (
-            0.5 * -0.284496736
-            + t * (0.5 * 1.421413741 + t * (0.5 * -1.453152027 + t * (0.5 * 1.061405429)))
-        )
-    )
-    q = poly * g
-    return jnp.where(h >= 0, 1.0 - q, q), g
-
-
-def experts_kernel(cap, ks, where, *refs):
-    nb = len(ks)
-    rows, (u, gw, rT) = refs[:nb], refs[nb : nb + 3]
-    gb, dr = refs[nb + 3 : 2 * nb + 3], refs[2 * nb + 3 : 3 * nb + 3]
-    xs, db, act, dh = refs[3 * nb + 3 : 3 * nb + 7]
+    return 0.5 + 0.5 * lax.erf(h * 0.7071067811865476), jnp.exp2((-0.5 * LOG2E) * h * h)
+
+
+def experts_kernel(cap, nb, first, sources, where, *refs):
+    rows, (u0, u1), gw, rT = refs[:nb], refs[nb : nb + 2], refs[nb + 2 : nb + 10], refs[nb + 10]
+    refs = refs[nb + 11 :] if first else refs[nb + 12 :]
+    dr = refs[:nb]
+    gated, xs, db, act, dh, gb, sems = refs[nb:]
     s = pl.program_id(0)
     pad = rows[0].shape[0]
     me = where[2]
-    chunks, _, cols = gw.shape
-    iw = [gw.at[j, :D] for j in range(chunks)]
-    xw = [gw.at[j, D:] for j in range(chunks)]
+    iw, xw = gw[:4], gw[4:]
+    chunks, cols = len(iw), iw[0].shape[1]
     for i in range(nb // 2):
 
         @pl.when(s == i)
         def _(i=i):
             xs[:pad, :] = rows[2 * i][...]
             xs[pad:, :] = rows[2 * i + 1][...]
-            db[:pad, :] = u[me ^ ks[2 * i]]
-            db[pad:, :] = u[me ^ ks[2 * i + 1]]
 
     x = xs[...]
-    upf = db[...].astype(f32)
+    upf = jnp.concatenate([u0[0], u1[0]], axis=0).astype(f32)
     logits = mm(x, rT[...].astype(bf16), NT)
     ex = jnp.exp(logits - jnp.max(logits, axis=1, keepdims=True))
     mine = lax.broadcasted_iota(i32, ex.shape, 1) == me
@@ -349,7 +334,15 @@
         part = mm(dj, iw[j][...], NT)
         drow = part if drow is None else drow + part
     b = back.astype(bf16).astype(f32)
-    gback = (gate * b).astype(bf16)
+    gb[...] = (gate * b).astype(bf16)
+    moves = [
+        pltpu.make_async_copy(
+            gb.at[pl.ds(o * pad, pad)], gated.at[sources[2 * s + o]], sems.at[o]
+        )
+        for o in range(2)
+    ]
+    for move in moves:
+        move.start()
     prod = upf * b
     first = prod.astype(bf16)
     rest = (prod - first.astype(f32)).astype(bf16)
@@ -368,70 +361,91 @@
             @pl.when(s == i)
             def _(i=i, o=o, part=part):
                 dr[2 * i + o][...] = part
-                gb[2 * i + o][...] = gback[o * pad : (o + 1) * pad, :]
-
-
-def run_experts(where, ks, rows, u, gw, rT, cap):
+
+    for move in moves:
+        move.wait()
+
+
+def run_experts(where, ks, rows, u, gw, rT, cap, gated):
     nb = len(ks)
     pad = rows[0].shape[0]
-    chunks, _, cols = gw.shape
-    pair = lambda c: pl.BlockSpec((2 * pad, c), lambda i: (i, 0))
+    hidden = len(gw) // 2 * gw[0].shape[1]
+    pair = lambda c: pl.BlockSpec((2 * pad, c), lambda i, src: (i, 0))
+    source = lambda o: pl.BlockSpec((1, pad, D), lambda i, src: (src[2 * i + o], 0, 0))
     blk = sds((pad, D), bf16)
+    prior = [] if gated is None else [gated]
     out = call(
-        functools.partial(experts_kernel, cap, ks),
+        functools.partial(experts_kernel, cap, nb, gated is None),
         "experts",
         us=8 * nb,
-        grid=(nb // 2,),
-        in_specs=[SMEM] + [whole(pad, D)] * nb + [full(u), full(gw), full(rT)],
-        out_specs=[whole(pad, D)] * (2 * nb) + [pair(D), pair(D), pair(FF), pair(FF)],
-        out_shape=[blk] * (2 * nb)
+        grid_spec=pltpu.PrefetchScalarGridSpec(
+            num_scalar_prefetch=1,
+            grid=(nb // 2,),
+            in_specs=[SMEM]
+            + [whole(pad, D)] * nb
+            + [source(0), source(1)]
+            + [full(w) for w in gw]
+            + [full(rT)]
+            + [ANY] * len(prior),
+            out_specs=[whole(pad, D)] * nb + [ANY, pair(D), pair(D), pair(FF), pair(FF)],
+            scratch_shapes=[pltpu.VMEM((2 * pad, D), bf16), pltpu.SemaphoreType.DMA((2,))],
+        ),
+        out_shape=[blk] * nb
+        + [sds(u.shape, bf16)]
         + [sds((nb * pad, D), bf16)] * 2
-        + [sds((nb * pad, chunks * cols), bf16)] * 2,
-    )(where, *rows, u, gw, rT)
-    return out[:nb], out[nb : 2 * nb], out[2 * nb :]
+        + [sds((nb * pad, hidden), bf16)] * 2,
+        input_output_aliases={nb + 13: nb} if prior else {},
+    )(where[2] ^ jnp.asarray(ks, i32), where, *rows, u, u, *gw, rT, *prior)
+    return out[:nb], out[nb], out[nb + 1 :]
 
 
 def weights_kernel(groups, *refs):
     xs, dbs, acts, dhs = (refs[i * groups : (i + 1) * groups] for i in range(4))
-    out, xT, dT = refs[4 * groups :]
-    pieces = []
-    at = 0
-    for g in range(groups):
-        step = xT.shape[2]
-        for r in range(xs[g].shape[0] // step):
-            pieces.append((g, r * step, at))
-            at += 1
-
-    @pl.when(pl.program_id(0) == 0)
+    *outs, xT, dT = refs[4 * groups :]
+    step = pl.program_id(0)
+
+    @pl.when(step == 0)
     def _():
-        for g, r, p in pieces:
-            xT[p] = xs[g][r : r + xT.shape[2], :].T
-            dT[p] = dbs[g][r : r + xT.shape[2], :].T
+        lo = 0
+        for x, db in zip(xs, dbs):
+            n = x.shape[0]
+            xT[:, lo : lo + n] = x[...].T
+            dT[:, lo : lo + n] = db[...].T
+            lo += n
 
     di = None
     de = None
-    for g, r, p in pieces:
-        part = mm(xT[p], dhs[g][r : r + xT.shape[2], :])
+    lo = 0
+    for act, dh in zip(acts, dhs):
+        n = act.shape[0]
+        part = mm(xT[:, lo : lo + n], dh[...])
         di = part if di is None else di + part
-        part = mm(dT[p], acts[g][r : r + xT.shape[2], :])
+        part = mm(dT[:, lo : lo + n], act[...])
         de = part if de is None else de + part
-    out[0, :D, :] = di.astype(bf16)
-    out[0, D:, :] = de.astype(bf16)
-
-
-def weight_grads(kept, pad):
+        lo += n
+    di = di.astype(bf16)
+    de = de.astype(bf16)
+    for j, out in enumerate(outs):
+
+        @pl.when(step == j)
+        def _(out=out):
+            out[:D, :] = di
+            out[D:, :] = de
+
+
+def weight_grads(kept):
     groups = len(kept)
     ins = [k[i] for i in range(4) for k in kept]
-    total = sum(k[0].shape[0] for k in kept) // (2 * pad)
+    rows = sum(k[0].shape[0] for k in kept)
     col = lambda a: pl.BlockSpec((a.shape[0], D), lambda j: (0, j))
     return call(
         functools.partial(weights_kernel, groups),
         "weight_grads",
         grid=(FF // D,),
         in_specs=[full(a) for a in ins[: 2 * groups]] + [col(a) for a in ins[2 * groups :]],
-        out_specs=pl.BlockSpec((1, 2 * D, D), lambda j: (j, 0, 0)),
-        out_shape=sds((FF // D, 2 * D, D), bf16),
-        scratch_shapes=[pltpu.VMEM((total, D, 2 * pad), bf16)] * 2,
+        out_specs=[whole(2 * D, D)] * (FF // D),
+        out_shape=[sds((2 * D, D), bf16)] * (FF // D),
+        scratch_shapes=[pltpu.VMEM((D, rows), bf16)] * 2,
     )(*ins)
 
 
@@ -514,25 +528,29 @@
     )(where, *blocks, cols, gatesT, sec, mid, cot, rT, nm)
 
 
-def finish_kernel(experts, *refs):
-    cols, mid, out, gb = refs[experts:]
-    stack_once(refs[:experts], gb)
+def finish_kernel(where, back, cols, mid, out, gb):
+    experts, pad, _ = back.shape
+
+    @pl.when(pl.program_id(0) == 0)
+    def _():
+        for j in range(experts):
+            gb[j * pad : (j + 1) * pad, :] = back[where[2] ^ j]
+
     out[...] = (mid[...] + mm(pick(cols[...], gb.shape[0]), gb[...])).astype(bf16)
 
 
-def finish(blocks, cols, mid):
-    experts = len(blocks)
-    pad = blocks[0].shape[0]
+def finish(where, back, cols, mid):
+    experts, pad, _ = back.shape
     t = cols.shape[0]
     return call(
-        functools.partial(finish_kernel, experts),
+        finish_kernel,
         "finish",
         grid=(t // SEQ,),
-        in_specs=[whole(pad, D)] * experts + [per_image(8), per_image(D)],
+        in_specs=[SMEM, full(back), per_image(8), per_image(D)],
         out_specs=per_image(D),
         out_shape=sds((t, D), bf16),
         scratch_shapes=[pltpu.VMEM((experts * pad, D), bf16)],
-    )(*blocks, cols, mid)
+    )(where, back, cols, mid)
 
 
 TILES = (
@@ -709,13 +727,25 @@
 
 
 def adam_kernel(rates, where, nums, *refs):
-    parts, owned = refs[:2], refs[2]
+    own, other, owned = refs[:3]
     weights, moments, outs = refs[3:7], refs[7:11], refs[11:27]
-    gq, go = refs[27:]
+    gq, go, pieces = refs[27:]
+    groups, _, r, _ = pieces.shape
     i = pl.program_id(0)
 
     @pl.when(i == 0)
     def _():
+        chip = where[2] // 2
+        for g in range(groups):
+
+            @pl.when(where[1] == g % 2)
+            def _(g=g):
+                pieces[g] = own[chip ^ (g // 2)]
+
+            @pl.when(where[1] != g % 2)
+            def _(g=g):
+                pieces[g] = other[chip ^ (g // 2)]
+
         for d in range(4):
 
             @pl.when(where[0] == d)
@@ -723,13 +753,14 @@
                 for part in range(2):
                     for t in range(2):
                         kind, c = TILES[part][d][t]
-                        if kind == 0:
-                            at = (c - 3 * d) * 128
-                            gq[:, at : at + 128] = parts[part][t * 512 : (t + 1) * 512, :]
-                        else:
-                            for j in range(4):
-                                lo = t * 512 + j * 128
-                                go[:, j * 128 : (j + 1) * 128] = parts[part][lo : lo + 128, :]
+                        for m in range(512 // r):
+                            tile = pieces[t * (512 // r) + m, part]
+                            if kind == 0:
+                                at = (c - 3 * d) * 128
+                                gq[m * r : (m + 1) * r, at : at + 128] = tile
+                            else:
+                                j, row = m * r // 128, m * r % 128
+                                go[row : row + r, j * 128 : (j + 1) * 128] = tile
 
     rows_q, rows_o = weights[0].shape[0], weights[1].shape[0]
     rows_e = weights[2].shape[1]
@@ -753,7 +784,7 @@
                 outs[4 * j + o][...] = new[o]
 
 
-def adam(rates, where, nums, part0, part1, owned, weights, moments):
+def adam(rates, where, nums, own, other, owned, weights, moments):
     steps = 4
     specs = []
     mspecs = []
@@ -772,11 +803,15 @@
         functools.partial(adam_kernel, rates),
         "adam",
         grid=(steps,),
-        in_specs=[SMEM, SMEM, full(part0), full(part1), full(owned)] + specs + mspecs,
+        in_specs=[SMEM, SMEM, full(own), full(other), full(owned)] + specs + mspecs,
         out_specs=[sp for sp in specs for _ in range(4)],
         out_shape=[sds(w.shape, dt) for w in weights for dt in (f32, f32, f32, bf16)],
-        scratch_shapes=[pltpu.VMEM((D, 384), bf16), pltpu.VMEM((128, D), bf16)],
-    )(where, nums, part0, part1, owned, *weights, *moments)
+        scratch_shapes=[
+            pltpu.VMEM((D, 384), bf16),
+            pltpu.VMEM((128, D), bf16),
+            pltpu.VMEM((2 * own.shape[0], *own.shape[1:]), bf16),
+        ],
+    )(where, nums, own, other, owned, *weights, *moments)
 
 
 def swap(x, axis, k):
@@ -788,64 +823,18 @@
     return lax.all_to_all(x, axis, split_axis=0, concat_axis=0, tiled=True)
 
 
-def total(blocks):
+def add_up(blocks):
     return functools.reduce(lambda a, b: a + b, [b.astype(f32) for b in blocks])
 
 
-def at(x, i):
-    return lax.dynamic_index_in_dim(x, i, 0, keepdims=False)
+def to_owners(x, axis, me):
+    part = lambda k: lax.dynamic_index_in_dim(x, me ^ k, 0, keepdims=False)
+    return [part(0)] + [swap(part(k), axis, k) for k in range(1, x.shape[0])]
 
 
 def fence(*groups):
     flat, tree = jax.tree.flatten(groups)
     return jax.tree.unflatten(tree, lax.optimization_barrier(tuple(flat)))
-
-
-class Sums:
-    def __init__(self, me_dp, me_e, groups):
-        self.d, self.core, self.chip = me_dp, me_e % 2, me_e // 2
-        self.chips = groups // 2
-
-    def send_core(self, packed):
-        groups, n_dp, r, c = packed.shape
-        x = packed.reshape(2, self.chips, n_dp, r, c)
-        self.own = at(x, self.core)
-        return [swap(at(x, 1 - self.core), "expert", 1)]
-
-    def take_core(self, got):
-        self.own = total([self.own] + got).astype(bf16)
-
-    def send_chip(self):
-        return [swap(at(self.own, self.chip ^ k), "expert", 2 * k) for k in range(1, self.chips)]
-
-    def take_chip(self, got):
-        self.own = total([at(self.own, self.chip)] + got).astype(bf16)
-
-    def send_dp(self):
-        return [swap(at(self.own, self.d ^ k), "dp", k) for k in range(1, 4)]
-
-    def take_dp(self, got):
-        self.piece = total([at(self.own, self.d)] + got)
-        self.own = self.piece.astype(bf16)
-
-    def spread_chip(self):
-        return [swap(self.own, "expert", 2 * k) for k in range(1, self.chips)]
-
-    def join_chip(self, got):
-        got = jnp.stack([self.own] + got)
-        self.own = jnp.concatenate(
-            [lax.dynamic_slice_in_dim(got, self.chip ^ k, 1, 0) for k in range(self.chips)]
-        )
-
-    def spread_core(self):
-        return [swap(self.own, "expert", 1)]
-
-    def join_core(self, got):
-        own, other = self.own, got[0]
-        x = jnp.stack(
-            [jnp.where(self.core == 0, own, other), jnp.where(self.core == 0, other, own)]
-        )
-        return x.reshape(-1, 128)
 
 
 def shards(
@@ -874,7 +863,7 @@
     experts = groups
     per = experts // n_dp
     cap = (tok_dev + experts - 1) // experts
-    pad = -(-(cap + 2) // 16) * 16
+    pad = -(-(cap + 2) // 128) * 128
     n = tok_dev // SEQ
     devices = n_dp * groups
     me_dp = lax.axis_index("dp").astype(i32)
@@ -900,74 +889,72 @@
         ],
         axis=0,
     )
-    own_e = jnp.concatenate([expert_in[0].astype(bf16), expert_out[0].astype(bf16)], axis=0)
+    got = [own] + [swap(own, "dp", k) for k in (1, 2, 3)]
     ids = expert_ids.reshape(n, SEQ, 2).transpose(0, 2, 1)
     prio = priority.reshape(n, SEQ, 2).transpose(0, 2, 1)
-    got = [own] + [swap(own, "dp", k) for k in (1, 2, 3)]
-    got, own_e, ids, prio = fence(got, own_e, ids, prio)
-    gathered = lax.all_gather(own_e, "dp", axis=0)
+    pos, cols = route(where, ids, prio, experts, cap, pad)
+    own_in, own_out = expert_in[0].astype(bf16), expert_out[0].astype(bf16)
+    in_w = [own_in, None, swap(own_in, "dp", 2), None]
+    got, pos, cols = fence(got, pos, cols)
     got = jnp.stack(got)
     got, misc = got[:, :64], got[:, 64:]
     near = [swap(got, "expert", 2 * k) for k in (1, 2, 3)]
-    pos, cols, up_slots = slots(where, ids, prio, cotangent, experts, cap, pad)
-    near, pos, cols, up_slots = fence(near, pos, cols, up_slots)
+    up_slots = spread(where, pos, cotangent, pad, True)
+    near, up_slots, in_w[2], own_in = fence(near, up_slots, in_w[2], own_in)
+    in_w[1], in_w[3] = swap(own_in, "dp", 1), swap(own_in, "dp", 3)
+    out_w = [own_out] + [swap(own_out, "dp", k) for k in (1, 2, 3)]
     far = swap(jnp.stack([got] + near), "expert", 1)
     up = exchange(up_slots, "expert")
     wT, ow, rT, nm = assemble(where, got, misc, jnp.stack(near), far, experts)
     proj, ctxT, lse, mid, sec, gatesT = attend(tokens, wT, ow, rT, nm)
 
-    blocks = spread(pos, sec, pad)
+    blocks = spread(where, pos, sec, pad, False)
     near = [k for k in range(2, groups) if (k >> 1) & ((k >> 1) - 1) == 0]
     distant = [k for k in range(2, groups) if (k >> 1) & ((k >> 1) - 1)]
-    gb, dr, kept = {}, {}, []
+    in_w, out_w, blocks = fence(in_w, out_w, blocks)
+    gated, dr, kept = None, {}, []
 
     def experts_on(ks, rows):
-        g, d, keep = run_experts(where, tuple(ks), rows, up, gathered, rT, cap)
+        d, gated_now, keep = run_experts(
+            where, tuple(ks), rows, up, in_w + out_w, rT, cap, gated
+        )
         kept.append(keep)
-        for k, gk, dk in zip(ks, g, d):
-            gb[k], dr[k] = gk, dk
+        dr.update(zip(ks, d))
+        return gated_now
 
     send = lambda ks: [swap(blocks[k], "expert", k) for k in ks]
     here, there = [blocks[0]] + send([1]), send(near)
-    experts_on([0, 1], here)
+    gated = experts_on([0, 1], here)
     there, kept[0] = fence(there, kept[0])
     ends = [blocks[k] for k in distant]
     ends, there = fence(ends, there)
     last = [swap(b, "expert", k) for k, b in zip(distant, ends)]
     dr[1] = swap(dr[1], "expert", 1)
-    experts_on(near, there)
+    gated = experts_on(near, there)
     last, kept[1], dr[1] = fence(last, kept[1], dr[1])
     for k in near:
         dr[k] = swap(dr[k], "expert", k)
-    experts_on(distant, last)
+    gated = experts_on(distant, last)
     for k in distant:
         dr[k] = swap(dr[k], "expert", k)
-    partial = weight_grads(kept, pad)
-    dr, gb, partial = fence([dr[k] for k in range(groups)], [gb[k] for k in range(groups)], partial)
-    owned = exchange(partial, "dp")
+    chunks = weight_grads(kept)
+    dr, chunks, gated = fence([dr[k] for k in range(groups)], chunks, gated)
+    owned = [chunks[0]] + [swap(chunks[k], "dp", k) for k in (1, 2, 3)]
+    gated = exchange(gated, "expert")
     dmid, dn_two, drT = combine(where, dr, cols, gatesT, sec, mid, cotangent, rT, nm, cap)
 
     back = functools.partial(attend_back, groups=groups, proj=proj, ctxT=ctxT, lse=lse, ow=ow, nm=nm)
-    dmid, gb = fence(dmid, gb)
-    split = 1 + 5 * groups // 8
-    early = [gb[0]] + [swap(gb[k], "expert", k) for k in range(1, split)]
-    late = gb[split:]
     dp0, packed0 = back(0, tok=tokens, dmid=dmid)
-    early, late, dmid, dp0, packed0 = fence(early, late, dmid, dp0, packed0)
-    sum0, sum1 = Sums(me_dp, me_e, groups), Sums(me_dp, me_e, groups)
-    sum0.take_core(sum0.send_core(packed0))
-    sum0.own, dmid = fence(sum0.own, dmid)
-    late = [swap(b, "expert", k) for k, b in enumerate(late, split)]
-    got = sum0.send_chip()
+    gated, dmid, dp0, packed0 = fence(gated, dmid, dp0, packed0)
+    got0 = exchange(packed0, "expert")
     dp1, packed1 = back(1, tok=tokens, dmid=dmid)
-    got, late, dp1, packed1, owned, dmid = fence(got, late, dp1, packed1, owned, dmid)
-    sum0.take_chip(got)
-    got0, got1 = sum0.send_dp(), sum1.send_core(packed1)
+    got0, dp1, packed1, owned, dmid = fence(got0, dp1, packed1, owned, dmid)
+
+    got0 = to_owners(add_up(got0).astype(bf16), "dp", me_dp)
+    got1 = exchange(packed1, "expert")
     grad_input, dn_one = enter(tokens, dmid, dp0, dp1, wT, nm)
     got0, got1, grad_input, dn_one, mid = fence(got0, got1, grad_input, dn_one, mid)
-    sum0.take_dp(got0)
-    sum1.take_core(got1)
-    got0, got1 = sum0.spread_chip(), sum1.send_chip()
+    got1 = to_owners(add_up(got1).astype(bf16), "dp", me_dp)
 
     dn = jnp.concatenate([dn_one, dn_two], axis=0)
     small = jnp.stack(
@@ -983,22 +970,20 @@
     lines = small.shape[1]
     small = jnp.broadcast_to(small[:, None], (n_dp, groups, lines, 128))
     small = exchange(small.reshape(devices, lines, 128), ("dp", "expert"))
-    activations = finish(early + late, cols, mid)
-    got0, got1, small, activations = fence(got0, got1, small, activations)
-    sum0.join_chip(got0)
-    sum1.take_chip(got1)
-    got0, got1 = sum0.spread_core(), sum1.send_dp()
-    owned = total([owned[d] for d in range(n_dp)])
+    activations = finish(where, gated, cols, mid)
+    piece0 = add_up(got0)
+    owned = add_up(owned)
+    term = jnp.sum(piece0 * piece0) + jnp.sum(owned * owned)
+    got1, small, activations, piece0, owned, term = fence(
+        got1, small, activations, piece0, owned, term
+    )
+    piece1 = add_up(got1)
     small = small.sum(0)
-    term = jnp.sum(sum0.piece * sum0.piece) + jnp.sum(owned * owned)
-    term = term + jnp.sum(small * small) / groups
-    got0, got1, term, owned, small = fence(got0, got1, term, owned, small)
-    part0 = sum0.join_core(got0)
-    sum1.take_dp(got1)
-    term = term + jnp.sum(sum1.piece * sum1.piece)
+    term = term + jnp.sum(piece1 * piece1) + jnp.sum(small * small) / groups
     terms = exchange(jnp.full((devices, 1, 128), term, f32), ("dp", "expert"))
-    sum1.join_chip(sum1.spread_chip())
-    part1 = sum1.join_core(sum1.spread_core())
+    pieces = jnp.stack([piece0, piece1]).astype(bf16)
+    mine = jnp.stack([pieces] + [swap(pieces, "expert", 2 * k) for k in range(1, groups // 2)])
+    other = swap(mine, "expert", 1)
     share_router = jnp.concatenate(
         [small[j * per : (j + 1) * per] for j in range(4)], axis=1
     ).T
@@ -1012,8 +997,8 @@
         (rates[0], rates[1], rates[4], rates[5]),
         where,
         jnp.stack([factor, *fixes]),
-        part0,
-        part1,
+        mine,
+        other,
         owned,
         (attn_qkv, attn_out, expert_in, expert_out),
         (moments_qkv, moments_out, moments_in, moments_exp),

time: 440 us -> 426 us (0.968)
  between operations: 20.7 us -> 6.92 us
  starting transfers between devices: 70.6 us -> 81 us
  Pallas kernels: 293 us -> 287 us
    all_to_all x4 -> x6, starting transfers between devices: 17.3 us -> 28.7 us  [exchange(): return lax.all_to_all(x, axis, split_axis=0, concat_axis=0, tiled=True)]
    pallas_call x6 -> x7, Pallas kernels: 105 us -> 102 us  [the longest x3 54.2 us: run_experts(): call(functools.partial(experts_kernel, cap, nb, gated is None), 'experts'...]
    ppermute x50 -> x40, starting transfers between devices: 53.3 us -> 52.3 us  [swap(): return lax.ppermute(x, axis, [(i, i ^ k) for i in range(n)])]
  transfers between devices with their start and end apart: 55 -> 46, of which waited for: 6 -> 5; matrix products, arithmetic and copies ran while one was open for 6% -> 5% of each run, Pallas kernels for 65% -> 66%
where the time goes in v3:
time: 426 us; the launch traced here: 419 us
  Pallas kernels  287 us (67%)
  starting transfers between devices  81 us (19%)
  other arithmetic  18.7 us (4%)
  waiting for transfers between devices  14.5 us (3%)
  local copies, waits for them, and re-layouts  11.2 us (3%)
  between operations  6.92 us (2%)
    pallas_call x2, Pallas kernels, attend_back(): call(functools.partial(attend_back_kernel, part), 'attend_back', grid=(t...  67.6 us
    pallas_call x3, Pallas kernels, run_experts(): call(functools.partial(experts_kernel, cap, nb, gated is None), 'experts'...  54.2 us
    ppermute x40, starting transfers between devices, swap(): return lax.ppermute(x, axis, [(i, i ^ k) for i in range(n)])  52.3 us
    pallas_call x1, Pallas kernels, attend(): call(attend_kernel, 'attend', grid=(n,), in_specs=[per_image(D), full(wT)...  40.6 us
    all_to_all x6, starting transfers between devices, exchange(): return lax.all_to_all(x, axis, split_axis=0, concat_axis=0, tiled=True)  28.7 us
    pallas_call x2, Pallas kernels, spread(): call(functools.partial(spread_kernel, pad, together), 'spread', grid=(exp...  28.7 us
    pallas_call x1, Pallas kernels, combine(): call(functools.partial(combine_kernel, cap, experts), 'combine', grid=(t...  26.4 us
    pallas_call x1, Pallas kernels, weight_grads(): call(functools.partial(weights_kernel, groups), 'weight_grads', grid=(FF...  23.4 us
  transfers between devices with their start and end apart: 46, of which 5 were waited for; matrix products, arithmetic and copies ran while one was open for 5% of the time, Pallas kernels for 66%

profile of v3, /device:TPU:0, one launch (start us, length us, event | category | flops | bytes accessed | tf_op | source)
XLA Modules:
  0.0 419.2 jit_solution(13405920568778794354)
XLA Ops:
  18.6 5.1 %route.1 = (s32[4,8,720]{2,1,0:T(8,128)}, s32[2880,8]{1,0:T(8,128)}) custom-call(s32[3]{0:T(128)} %pad_add_fusion.where, s32[4,2,720]{2,1,0:T(2,128)} %bitcast.110, s32[4,2,720]{2,1,0:T(2,128)} %bitcast.111), custom_call_target="tpu_custom_call" | custom-call | flops 100000000 | bytes 100000 | tf_op jit(solution)/shard_map/route/pallas_call | solution.py:179
  23.7 4.2 collective-permute-done.1
  31.6 14.1 %spread.2 = bf16[8,384,512]{2,1,0:T(8,128)(2,1)} custom-call(s32[3]{0:T(128)} %pad_add_fusion.where, s32[4,8,720]{2,1,0:T(8,128)} %get-tuple-element.196.pos, bf16[2880,512]{1,0:T(8,128)(2,1)} %refs_12_.1), custom_call_target="tpu_custom_call" | custom-call | flops 100000000 | bytes 100000 | tf_op jit(solution)/shard_map/spread/pallas_call | solution.py:218
  45.7 4.6 %all-to-all-start = ((bf16[8,384,512]{2,1,0:T(8,128)(2,1)}), bf16[8,384,512]{2,1,0:T(8,128)(2,1)}, u32[]{:S(2)}, u32[]{:S(2)}) async-start(bf16[8,384,512]{2,1,0:T(8,128)(2,1)} %spread.2), calls=%async_computation | async-start | bytes 6291456 | tf_op jit(solution)/shard_map/all_to_all | solution.py:823
  65.5 40.6 %attend.1 = (bf16[2880,1536]{1,0:T(8,128)(2,1)}, bf16[4,512,720]{2,1,0:T(8,128)(2,1)}, f32[4,8,720]{2,1,0:T(8,128)}, f32[2880,512]{1,0:T(8,128)}, bf16[2880,512]{1,0:T(8,128)(2,1)}, /*index=5*/f32[4,8,720]{2,1,0:T(8,128)}) custom-call(bf16[2880,512]{1,0:T(8,128)(2,1)} %tok.7, bf16[1536,512]{1,0:T(8,128)(2,1)} %get-tuple-element.202.wT, ...), custom_call_target="tpu_custom_call" | custom-call | flops 100000000 | bytes 100000 | tf_op jit(solution)/shard_map/attend/pallas_call | solution.py:266
  106.2 14.6 %spread.3 = (bf16[384,512]{1,0:T(8,128)(2,1)}, bf16[384,512]{1,0:T(8,128)(2,1)}, bf16[384,512]{1,0:T(8,128)(2,1)}, bf16[384,512]{1,0:T(8,128)(2,1)}, bf16[384,51...) custom-call(s32[3]{0:T(128)} %pad_add_fusion.where, ...), custom_call_target="tpu_custom_call" | custom-call | flops 100000000 | bytes 100000 | tf_op jit(solution)/shard_map/spread/pallas_call | solution.py:218
  125.7 14.9 %experts.3 = (bf16[384,512]{1,0:T(8,128)(2,1)}, bf16[384,512]{1,0:T(8,128)(2,1)}, bf16[8,384,512]{2,1,0:T(8,128)(2,1)}, bf16[768,512]{1,0:T(8,128)(2,1)}, bf16[7...) custom-call(s32[2]{0:T(128)} %iota_xor_fusion.sources, s32[3]{0:T(128)} %pad_add_fusion.where, ...), custom_call_target="tpu_custom_call" | custom-call | flops 16000000000 | bytes 100000 | tf_op jit(solution)/shard_map/experts/pallas_call | solution.py:377
  146.6 24.5 %experts.4 = (bf16[384,512]{1,0:T(8,128)(2,1)}, bf16[384,512]{1,0:T(8,128)(2,1)}, bf16[384,512]{1,0:T(8,128)(2,1)}, bf16[384,512]{1,0:T(8,128)(2,1)}, bf16[8,384...) custom-call(s32[4]{0:T(128)} %broadcast_xor_fusion.sources, ...), custom_call_target="tpu_custom_call", output_to_operand_aliasing={{4}: (17, {})} | custom-call | flops 32000000000 | bytes 100000 | tf_op jit(solution)/shard_map/experts/pallas_call | solution.py:377
  175.5 14.9 %experts.5 = (bf16[384,512]{1,0:T(8,128)(2,1)}, bf16[384,512]{1,0:T(8,128)(2,1)}, bf16[8,384,512]{2,1,0:T(8,128)(2,1)}, bf16[768,512]{1,0:T(8,128)(2,1)}, bf16[7...) custom-call(s32[2]{0:T(128)} %broadcast_xor_fusion.1.sources, ...), custom_call_target="tpu_custom_call", output_to_operand_aliasing={{2}: (15, {})} | custom-call | flops 16000000000 | bytes 100000 | tf_op jit(solution)/shard_map/experts/pallas_call | solution.py:377
  193.1 23.4 %weight_grads.1 = (bf16[1024,512]{1,0:T(8,128)(2,1)}, bf16[1024,512]{1,0:T(8,128)(2,1)}, bf16[1024,512]{1,0:T(8,128)(2,1)}, bf16[1024,512]{1,0:T(8,128)(2,1)}) custom-call(bf16[768,512]{1,0:T(8,128)(2,1)} %get-tuple-element.263.refs_0_, bf16[1536,512]{1,0:T(8,128)(2,1)} %get-tuple-element.264.refs_1_, bf16[768,512]{1,0:T(8,128)(2,1)} %get-tuple-element.265.refs_2_, ...), custom_call_target="tpu_custom_call" | custom-call | flops 100000000 | bytes 100000 | tf_op jit(solution)/shard_map/weight_grads/pallas_call | solution.py:441
  218.5 4.0 all-to-all-start.1
  222.5 3.9 collective-permute-start.27
  229.0 26.4 %combine.1 = (f32[2880,512]{1,0:T(8,128)}, f32[2,512]{1,0:T(2,128)}, f32[8,512]{1,0:T(8,128)}) custom-call(s32[3]{0:T(128)} %pad_add_fusion.where, bf16[384,512]{1,0:T(8,128)(2,1)} %get-tuple-element.281.refs_0_, bf16[384,512]{1,0:T(8,128)(2,1)} %copy-done.8, bf16[384,512]{1,0:T(8,128)(2,1)} %copy-done.9, bf16[384,512]{1,0:T(8,128)(2,1)} %copy-done.10, ...), custom_call_target="tpu_custom_call" | custom-call | flops 100000000 | bytes 100000 | tf_op jit(solution)/shard_map/combine/pallas_call | solution.py:510
  255.4 33.8 %attend_back.2 = (bf16[2880,768]{1,0:T(8,128)(2,1)}, bf16[8,4,128,128]{3,2,1,0:T(8,128)(2,1)}) custom-call(bf16[2880,512]{1,0:T(8,128)(2,1)} %tok.7, f32[2880,512]{1,0:T(8,128)} %get-tuple-element.308.dmid, bf16[2880,1536]{1,0:T(8,128)(2,1)} %get-tuple-element.293.proj, bf16[4,512,720]{2,1,0:T(8,128)(2,1)} %get-tuple-element.294.ctxT, ...), custom_call_target="tpu_custom_call" | custom-call | flops 100000000 | bytes 100000 | tf_op jit(solution)/shard_map/attend_back/pallas_call | solution.py:637
  289.2 4.5 %all-to-all-start.2 = ((bf16[8,4,128,128]{3,2,1,0:T(8,128)(2,1)}), bf16[8,4,128,128]{3,2,1,0:T(8,128)(2,1)}, u32[]{:S(2)}, u32[]{:S(2)}) async-start(bf16[8,4,128,128]{3,2,1,0:T(8,128)(2,1)} %get-tuple-element.298), calls=%async_computation.2 | async-start | bytes 2097152 | tf_op jit(solution)/shard_map/all_to_all | solution.py:823
  294.5 33.8 %attend_back.3 = (bf16[2880,768]{1,0:T(8,128)(2,1)}, bf16[8,4,128,128]{3,2,1,0:T(8,128)(2,1)}) custom-call(bf16[2880,512]{1,0:T(8,128)(2,1)} %tok.7, f32[2880,512]{1,0:T(8,128)} %get-tuple-element.308.dmid, bf16[2880,1536]{1,0:T(8,128)(2,1)} %get-tuple-element.293.proj, bf16[4,512,720]{2,1,0:T(8,128)(2,1)} %get-tuple-element.294.ctxT, ...), custom_call_target="tpu_custom_call" | custom-call | flops 100000000 | bytes 100000 | tf_op jit(solution)/shard_map/attend_back/pallas_call | solution.py:637
  328.3 4.3 %all-to-all-start.3 = ((bf16[8,4,128,128]{3,2,1,0:T(8,128)(2,1)}), bf16[8,4,128,128]{3,2,1,0:T(8,128)(2,1)S(1)}, u32[]{:S(2)}, u32[]{:S(2)}) async-start(bf16[8,4,128,128]{3,2,1,0:T(8,128)(2,1)} %get-tuple-element.307), calls=%async_computation.3 | async-start | bytes 2097152 | tf_op jit(solution)/shard_map/all_to_all | solution.py:823
  338.6 4.4 %multiply_reduce_fusion = (f32[]{:T(128)}, f32[1024,512]{1,0:T(8,128)}) fusion(bf16[1024,512]{1,0:T(8,128)(2,1)} %collective-permute-done.29, bf16[1024,512]{1,0:T(8,128)(2,1)} %collective-permute-done.28, bf16[1024,512]{1,0:T(8,128)(2,1)} %collective-permute-done.27, bf16[1024,512]{1,0:T(8,128)(2,1)S(1)} %copy-done.2), kind=kLoop, calls=%fused_computation | loop fusion | flops 4718591 | bytes 6291460 | tf_op jit(solution)/shard_map/reduce_sum | solution.py:976
  343.0 13.0 %enter.1 = (f32[2880,512]{1,0:T(8,128)}, f32[2,512]{1,0:T(2,128)}) custom-call(bf16[2880,512]{1,0:T(8,128)(2,1)} %tok.7, f32[2880,512]{1,0:T(8,128)} %get-tuple-element.308.dmid, bf16[2880,768]{1,0:T(8,128)(2,1)} %get-tuple-element.309.dp0, bf16[2880,768]{1,0:T(8,128)(2,1)} %get-tuple-element.310.dp1, bf16[1536,512]{1,0:T(8,128)(2,1)} %get-tuple-element.202.wT, ...), custom_call_target="tpu_custom_call" | custom-call | flops 100000000 | bytes 100000 | tf_op jit(solution)/shard_map/enter/pallas_call | solution.py:691
  357.7 5.4 %all-to-all-start.4 = ((f32[32,12,128]{2,1,0:T(8,128)}), f32[32,12,128]{2,1,0:T(8,128)S(1)}, u32[]{:S(2)}, u32[]{:S(2)}) async-start(f32[32,12,128]{2,1,0:T(8,128)} %bitcast.29), calls=%async_computation.4 | async-start | bytes 524288 | tf_op jit(solution)/shard_map/all_to_all | solution.py:823
  369.8 14.0 %finish.1 = bf16[2880,512]{1,0:T(8,128)(2,1)} custom-call(s32[3]{0:T(128)} %pad_add_fusion.where, bf16[8,384,512]{2,1,0:T(8,128)(2,1)} %copy-done, s32[2880,8]{1,0:T(8,128)} %get-tuple-element.289.refs_8_.cols, f32[2880,512]{1,0:T(8,128)} %get-tuple-element.318.refs_11_.mid), custom_call_target="tpu_custom_call" | custom-call | flops 100000000 | bytes 100000 | tf_op jit(solution)/shard_map/finish/pallas_call | solution.py:545
  390.5 5.9 %all-to-all-start.5 = ((f32[32,1,128]{2,1,0:T(1,128)}), f32[32,1,128]{2,1,0:T(1,128)S(1)}, u32[]{:S(2)}, u32[]{:S(2)}) async-start(f32[32,1,128]{2,1,0:T(1,128)} %broadcast_in_dim.14), calls=%async_computation.5 | async-start | bytes 32768 | tf_op jit(solution)/shard_map/all_to_all | solution.py:823
  396.4 7.1 %all-to-all-done.5 = f32[32,1,128]{2,1,0:T(1,128)S(1)} async-done(((f32[32,1,128]{2,1,0:T(1,128)}), f32[32,1,128]{2,1,0:T(1,128)S(1)}, u32[]{:S(2)}, u32[]{:S(2)}) %all-to-all-start.5) | async-done | bytes 16416 | tf_op jit(solution)/shard_map/all_to_all | solution.py:823
  407.9 10.0 %adam.1 = (f32[512,384]{1,0:T(8,128)}, f32[512,384]{1,0:T(8,128)}, f32[512,384]{1,0:T(8,128)}, bf16[512,384]{1,0:T(8,128)(2,1)}, f32[128,512]{1,0:T(8,128)}, /*i...) custom-call(s32[3]{0:T(128)} %pad_add_fusion.where, ...), custom_call_target="tpu_custom_call" | custom-call | flops 100000000 | bytes 100000 | tf_op jit(solution)/shard_map/adam/pallas_call | solution.py:802
  (213 shorter events, 80.9 us)
Async XLA Ops:
  11.3 34.4 %collective-permute-start.6 = (bf16[512,512]{1,0:T(8,128)(2,1)S(1)}, bf16[512,512]{1,0:T(8,128)(2,1)}, u32[]{:S(2)}, u32[]{:S(2)}) collective-permute-start(bf16[512,512]{1,0:T(8,128)(2,1)S(1)} %convert_bitcast_fusion.1.refs_4_.refs_6_), channel_id=1, source_target_pairs={{0,16},{8,24},{16,0},{24,8},{1,17},{9,25},{17,1},{25,9},{2,18},{10... | collective-permute-start | bytes 1572872 | tf_op jit(solution)/shard_map/ppermute | solution.py:819
  45.7 80.0 %all-to-all-start = ((bf16[8,384,512]{2,1,0:T(8,128)(2,1)}), bf16[8,384,512]{2,1,0:T(8,128)(2,1)}, u32[]{:S(2)}, u32[]{:S(2)}) async-start(bf16[8,384,512]{2,1,0:T(8,128)(2,1)} %spread.2), calls=%async_computation | async-start | bytes 6291456 | tf_op jit(solution)/shard_map/all_to_all | solution.py:823
  51.0 69.8 %collective-permute-start.9 = (bf16[512,512]{1,0:T(8,128)(2,1)S(1)}, bf16[512,512]{1,0:T(8,128)(2,1)S(1)}, u32[]{:S(2)}, u32[]{:S(2)}) collective-permute-start(bf16[512,512]{1,0:T(8,128)(2,1)S(1)} %convert_bitcast_fusion.refs_8_.refs_10_), channel_id=1, source_target_pairs={{0,8},{8,0},{16,24},{24,16},{1,9},{9,1},{17,25},{25,17},{2,10},{10... | collective-permute-start | bytes 1572872 | tf_op jit(solution)/shard_map/ppermute | solution.py:819
  53.4 67.5 %collective-permute-start.10 = (bf16[512,512]{1,0:T(8,128)(2,1)S(1)}, bf16[512,512]{1,0:T(8,128)(2,1)S(1)}, u32[]{:S(2)}, u32[]{:S(2)}) collective-permute-start(bf16[512,512]{1,0:T(8,128)(2,1)S(1)} %convert_bitcast_fusion.refs_8_.refs_10_), channel_id=1, source_target_pairs={{0,16},{8,24},{16,0},{24,8},{1,17},{9,25},{17,1},{25,9},{2,18},{10... | collective-permute-start | bytes 1572872 | tf_op jit(solution)/shard_map/ppermute | solution.py:819
  54.7 66.2 %collective-permute-start.11 = (bf16[512,512]{1,0:T(8,128)(2,1)S(1)}, bf16[512,512]{1,0:T(8,128)(2,1)}, u32[]{:S(2)}, u32[]{:S(2)}) collective-permute-start(bf16[512,512]{1,0:T(8,128)(2,1)S(1)} %convert_bitcast_fusion.refs_8_.refs_10_), channel_id=1, source_target_pairs={{0,24},{8,16},{16,8},{24,0},{1,25},{9,17},{17,9},{25,1},{2,26},{10... | collective-permute-start | bytes 1572872 | tf_op jit(solution)/shard_map/ppermute | solution.py:819
  56.0 64.8 %collective-permute-start.7 = (bf16[512,512]{1,0:T(8,128)(2,1)S(1)}, bf16[512,512]{1,0:T(8,128)(2,1)}, u32[]{:S(2)}, u32[]{:S(2)}) collective-permute-start(bf16[512,512]{1,0:T(8,128)(2,1)S(1)} %convert_bitcast_fusion.1.refs_4_.refs_6_), channel_id=1, source_target_pairs={{0,8},{8,0},{16,24},{24,16},{1,9},{9,1},{17,25},{25,17},{2,10},{10... | collective-permute-start | bytes 1572872 | tf_op jit(solution)/shard_map/ppermute | solution.py:819
  56.9 64.0 %collective-permute-start.8 = (bf16[512,512]{1,0:T(8,128)(2,1)S(1)}, bf16[512,512]{1,0:T(8,128)(2,1)}, u32[]{:S(2)}, u32[]{:S(2)}) collective-permute-start(bf16[512,512]{1,0:T(8,128)(2,1)S(1)} %convert_bitcast_fusion.1.refs_4_.refs_6_), channel_id=1, source_target_pairs={{0,24},{8,16},{16,8},{24,0},{1,25},{9,17},{17,9},{25,1},{2,26},{10... | collective-permute-start | bytes 1572872 | tf_op jit(solution)/shard_map/ppermute | solution.py:819
  143.5 29.4 %collective-permute-start.18 = (bf16[384,512]{1,0:T(8,128)(2,1)S(1)}, bf16[384,512]{1,0:T(8,128)(2,1)S(1)}, u32[]{:S(2)}, u32[]{:S(2)}) collective-permute-start(bf16[384,512]{1,0:T(8,128)(2,1)S(1)} %copy-done.31), channel_id=1, source_target_pairs={{0,6},{1,7},{2,4},{3,5},{4,2},{5,3},{6,0},{7,1},{8,14},{9,15},{10,... | collective-permute-start | bytes 1179656 | tf_op jit(solution)/shard_map/ppermute | solution.py:819
  146.2 28.3 %collective-permute-start.19 = (bf16[384,512]{1,0:T(8,128)(2,1)S(1)}, bf16[384,512]{1,0:T(8,128)(2,1)S(1)}, u32[]{:S(2)}, u32[]{:S(2)}) collective-permute-start(bf16[384,512]{1,0:T(8,128)(2,1)S(1)} %copy-done.30), channel_id=1, source_target_pairs={{0,7},{1,6},{2,5},{3,4},{4,3},{5,2},{6,1},{7,0},{8,15},{9,14},{10,... | collective-permute-start | bytes 1179656 | tf_op jit(solution)/shard_map/ppermute | solution.py:819
  146.2 29.3 %collective-permute-start.20 = (bf16[384,512]{1,0:T(8,128)(2,1)}, bf16[384,512]{1,0:T(8,128)(2,1)S(1)}, u32[]{:S(2)}, u32[]{:S(2)}) collective-permute-start(bf16[384,512]{1,0:T(8,128)(2,1)} %get-tuple-element.252), channel_id=1, source_target_pairs={{0,1},{1,0},{2,3},{3,2},{4,5},{5,4},{6,7},{7,6},{8,9},{9,8},{10,11... | collective-permute-start | bytes 1179656 | tf_op jit(solution)/shard_map/ppermute | solution.py:819
  171.1 21.9 %collective-permute-start.21 = (bf16[384,512]{1,0:T(8,128)(2,1)}, bf16[384,512]{1,0:T(8,128)(2,1)S(1)}, u32[]{:S(2)}, u32[]{:S(2)}) collective-permute-start(bf16[384,512]{1,0:T(8,128)(2,1)} %get-tuple-element.254), channel_id=1, source_target_pairs={{0,2},{1,3},{2,0},{3,1},{4,6},{5,7},{6,4},{7,5},{8,10},{9,11},{10,... | collective-permute-start | bytes 1179656 | tf_op jit(solution)/shard_map/ppermute | solution.py:819
  172.9 43.6 %collective-permute-start.22 = (bf16[384,512]{1,0:T(8,128)(2,1)}, bf16[384,512]{1,0:T(8,128)(2,1)S(1)}, u32[]{:S(2)}, u32[]{:S(2)}) collective-permute-start(bf16[384,512]{1,0:T(8,128)(2,1)} %get-tuple-element.255), channel_id=1, source_target_pairs={{0,3},{1,2},{2,1},{3,0},{4,7},{5,6},{6,5},{7,4},{8,11},{9,10},{10,... | collective-permute-start | bytes 1179656 | tf_op jit(solution)/shard_map/ppermute | solution.py:819
  173.0 44.4 %collective-permute-start.23 = (bf16[384,512]{1,0:T(8,128)(2,1)}, bf16[384,512]{1,0:T(8,128)(2,1)S(1)}, u32[]{:S(2)}, u32[]{:S(2)}) collective-permute-start(bf16[384,512]{1,0:T(8,128)(2,1)} %get-tuple-element.256), channel_id=1, source_target_pairs={{0,4},{1,5},{2,6},{3,7},{4,0},{5,1},{6,2},{7,3},{8,12},{9,13},{10,... | collective-permute-start | bytes 1179656 | tf_op jit(solution)/shard_map/ppermute | solution.py:819
  175.2 42.2 %collective-permute-start.24 = (bf16[384,512]{1,0:T(8,128)(2,1)}, bf16[384,512]{1,0:T(8,128)(2,1)S(1)}, u32[]{:S(2)}, u32[]{:S(2)}) collective-permute-start(bf16[384,512]{1,0:T(8,128)(2,1)} %get-tuple-element.257), channel_id=1, source_target_pairs={{0,5},{1,4},{2,7},{3,6},{4,1},{5,0},{6,3},{7,2},{8,13},{9,12},{10,... | collective-permute-start | bytes 1179656 | tf_op jit(solution)/shard_map/ppermute | solution.py:819
  190.4 27.0 %collective-permute-start.25 = (bf16[384,512]{1,0:T(8,128)(2,1)}, bf16[384,512]{1,0:T(8,128)(2,1)S(1)}, u32[]{:S(2)}, u32[]{:S(2)}) collective-permute-start(bf16[384,512]{1,0:T(8,128)(2,1)} %get-tuple-element.261), channel_id=1, source_target_pairs={{0,6},{1,7},{2,4},{3,5},{4,2},{5,3},{6,0},{7,1},{8,14},{9,15},{10,... | collective-permute-start | bytes 1179656 | tf_op jit(solution)/shard_map/ppermute | solution.py:819
  193.0 24.4 %collective-permute-start.26 = (bf16[384,512]{1,0:T(8,128)(2,1)}, bf16[384,512]{1,0:T(8,128)(2,1)S(1)}, u32[]{:S(2)}, u32[]{:S(2)}) collective-permute-start(bf16[384,512]{1,0:T(8,128)(2,1)} %get-tuple-element.262), channel_id=1, source_target_pairs={{0,7},{1,6},{2,5},{3,4},{4,3},{5,2},{6,1},{7,0},{8,15},{9,14},{10,... | collective-permute-start | bytes 1179656 | tf_op jit(solution)/shard_map/ppermute | solution.py:819
  218.5 70.7 %all-to-all-start.1 = ((bf16[8,384,512]{2,1,0:T(8,128)(2,1)}), bf16[8,384,512]{2,1,0:T(8,128)(2,1)S(1)}, u32[]{:S(2)}, u32[]{:S(2)}) async-start(bf16[8,384,512]{2,1,0:T(8,128)(2,1)} %get-tuple-element.280), calls=%async_computation.1 | async-start | bytes 6291456 | tf_op jit(solution)/shard_map/all_to_all | solution.py:823
  222.5 105.8 %collective-permute-start.27 = (bf16[1024,512]{1,0:T(8,128)(2,1)}, bf16[1024,512]{1,0:T(8,128)(2,1)}, u32[]{:S(2)}, u32[]{:S(2)}) collective-permute-start(bf16[1024,512]{1,0:T(8,128)(2,1)} %get-tuple-element.303), channel_id=1, source_target_pairs={{0,8},{8,0},{16,24},{24,16},{1,9},{9,1},{17,25},{25,17},{2,10},{10... | collective-permute-start | bytes 3145736 | tf_op jit(solution)/shard_map/ppermute | solution.py:819
  226.4 102.0 %collective-permute-start.28 = (bf16[1024,512]{1,0:T(8,128)(2,1)}, bf16[1024,512]{1,0:T(8,128)(2,1)}, u32[]{:S(2)}, u32[]{:S(2)}) collective-permute-start(bf16[1024,512]{1,0:T(8,128)(2,1)} %get-tuple-element.304), channel_id=1, source_target_pairs={{0,16},{8,24},{16,0},{24,8},{1,17},{9,25},{17,1},{25,9},{2,18},{10... | collective-permute-start | bytes 3145736 | tf_op jit(solution)/shard_map/ppermute | solution.py:819
  227.6 100.7 %collective-permute-start.29 = (bf16[1024,512]{1,0:T(8,128)(2,1)}, bf16[1024,512]{1,0:T(8,128)(2,1)}, u32[]{:S(2)}, u32[]{:S(2)}) collective-permute-start(bf16[1024,512]{1,0:T(8,128)(2,1)} %get-tuple-element.305), channel_id=1, source_target_pairs={{0,24},{8,16},{16,8},{24,0},{1,25},{9,17},{17,9},{25,1},{2,26},{10... | collective-permute-start | bytes 3145736 | tf_op jit(solution)/shard_map/ppermute | solution.py:819
  289.2 39.1 %all-to-all-start.2 = ((bf16[8,4,128,128]{3,2,1,0:T(8,128)(2,1)}), bf16[8,4,128,128]{3,2,1,0:T(8,128)(2,1)}, u32[]{:S(2)}, u32[]{:S(2)}) async-start(bf16[8,4,128,128]{3,2,1,0:T(8,128)(2,1)} %get-tuple-element.298), calls=%async_computation.2 | async-start | bytes 2097152 | tf_op jit(solution)/shard_map/all_to_all | solution.py:823
  328.3 27.8 %all-to-all-start.3 = ((bf16[8,4,128,128]{3,2,1,0:T(8,128)(2,1)}), bf16[8,4,128,128]{3,2,1,0:T(8,128)(2,1)S(1)}, u32[]{:S(2)}, u32[]{:S(2)}) async-start(bf16[8,4,128,128]{3,2,1,0:T(8,128)(2,1)} %get-tuple-element.307), calls=%async_computation.3 | async-start | bytes 2097152 | tf_op jit(solution)/shard_map/all_to_all | solution.py:823
  334.2 21.9 %collective-permute-start.30 = (bf16[128,128]{1,0:T(8,128)(2,1)S(1)}, bf16[128,128]{1,0:T(8,128)(2,1)S(1)}, u32[]{:S(2)}, u32[]{:S(2)}) collective-permute-start(bf16[128,128]{1,0:T(8,128)(2,1)S(1)} %get-tuple-element.375), channel_id=1, source_target_pairs={{0,8},{8,0},{16,24},{24,16},{1,9},{9,1},{17,25},{25,17},{2,10},{10... | collective-permute-start | bytes 98312 | tf_op jit(solution)/shard_map/ppermute | solution.py:819
  357.7 26.0 %all-to-all-start.4 = ((f32[32,12,128]{2,1,0:T(8,128)}), f32[32,12,128]{2,1,0:T(8,128)S(1)}, u32[]{:S(2)}, u32[]{:S(2)}) async-start(f32[32,12,128]{2,1,0:T(8,128)} %bitcast.29), calls=%async_computation.4 | async-start | bytes 524288 | tf_op jit(solution)/shard_map/all_to_all | solution.py:823
  (62 other events, 1046.4 us)

commit v4 on v3

--- a/solution.py
+++ b/solution.py
@@ -74,7 +74,7 @@
     return c * r, r
 
 
-def assemble_kernel(experts, where, got, misc, near, far, wT, ow, rT, nm):
+def assemble_kernel(experts, where, got, n1, n2, n3, far, wT, ow, rT, nm):
     me, slot = where[0], where[2] % 8
     per = experts // 4
     for c in range(4):
@@ -83,7 +83,7 @@
             for k in range(4):
                 d = me ^ k
                 if b == 0:
-                    piece = got[k] if c == 0 else near[c - 1, k]
+                    piece = got[k] if c == 0 else (n1, n2, n3)[c - 1][k]
                 else:
                     piece = far[c, k]
                 lo = pl.multiple_of(d * 384 + s * 48, 16)
@@ -95,7 +95,7 @@
 
             @pl.when((me ^ k) == d)
             def _(d=d, k=k):
-                rest = misc[k].astype(f32)
+                rest = got[k, 64:, :].astype(f32)
                 rT[d * per : (d + 1) * per, :] = rest[:per, :]
                 for j in range(4):
                     nm[j : j + 1, d * 128 : (d + 1) * 128] = rest[
@@ -103,8 +103,8 @@
                     ]
 
 
-def assemble(where, got, misc, near, far, experts):
-    args = (got, misc, near, far)
+def assemble(where, got, near, far, experts):
+    args = (got, *near, far)
     return call(
         functools.partial(assemble_kernel, experts),
         "assemble",
@@ -293,14 +293,15 @@
 
 
 def experts_kernel(cap, nb, first, sources, where, *refs):
-    rows, (u0, u1), gw, rT = refs[:nb], refs[nb : nb + 2], refs[nb + 2 : nb + 10], refs[nb + 10]
-    refs = refs[nb + 11 :] if first else refs[nb + 12 :]
+    rows, (u0, u1), gw, rT = refs[:nb], refs[nb : nb + 2], refs[nb + 2 : nb + 8], refs[nb + 8]
+    refs = refs[nb + 9 :] if first else refs[nb + 10 :]
     dr = refs[:nb]
     gated, xs, db, act, dh, gb, sems = refs[nb:]
     s = pl.program_id(0)
     pad = rows[0].shape[0]
     me = where[2]
-    iw, xw = gw[:4], gw[4:]
+    iw = [gw[0], gw[4].at[:D], gw[1], gw[5].at[:D]]
+    xw = [gw[2], gw[4].at[D:], gw[3], gw[5].at[D:]]
     chunks, cols = len(iw), iw[0].shape[1]
     for i in range(nb // 2):
 
@@ -369,7 +370,7 @@
 def run_experts(where, ks, rows, u, gw, rT, cap, gated):
     nb = len(ks)
     pad = rows[0].shape[0]
-    hidden = len(gw) // 2 * gw[0].shape[1]
+    hidden = 4 * gw[0].shape[1]
     pair = lambda c: pl.BlockSpec((2 * pad, c), lambda i, src: (i, 0))
     source = lambda o: pl.BlockSpec((1, pad, D), lambda i, src: (src[2 * i + o], 0, 0))
     blk = sds((pad, D), bf16)
@@ -394,7 +395,7 @@
         + [sds(u.shape, bf16)]
         + [sds((nb * pad, D), bf16)] * 2
         + [sds((nb * pad, hidden), bf16)] * 2,
-        input_output_aliases={nb + 13: nb} if prior else {},
+        input_output_aliases={nb + 11: nb} if prior else {},
     )(where[2] ^ jnp.asarray(ks, i32), where, *rows, u, u, *gw, rT, *prior)
     return out[:nb], out[nb], out[nb + 1 :]
 
@@ -566,7 +567,7 @@
     da = dmid[...].astype(bf16)
     owp = ow[base : base + half, :]
     do = mm(da, owp, NT).astype(bf16)
-    doT = mm(owp, da, NT).astype(bf16)
+    doT = do.T
     prod = doT.astype(f32) * ctxT[0, base : base + half, :].astype(f32)
     kT[...] = proj[:, D + base : D + base + half].T
     masks = head_masks()
@@ -658,8 +659,11 @@
     )(tok, dmid, proj, ctxT, lse, ow, nm)
 
 
-def enter_kernel(tok, dmid, dp0, dp1, wT, nm, gin, dn):
+def enter_kernel(tok, dmid, dp0, dp1, wT, nm, o0, o1, o2, o3, gin, dn, owned, squares):
     i = pl.program_id(0)
+    own = (o0[...].astype(f32) + o1[...].astype(f32)) + (o2[...].astype(f32) + o3[...].astype(f32))
+    owned[...] = own
+    sq = jnp.sum(own * own, axis=0, keepdims=True)
     half = D // 2
     df = None
     for part, dp in enumerate((dp0, dp1)):
@@ -679,15 +683,18 @@
     def _():
         dn[0:1, :] = gg
         dn[1:2, :] = gs
+        squares[...] = sq
 
     @pl.when(i > 0)
     def _():
         dn[0:1, :] += gg
         dn[1:2, :] += gs
-
-
-def enter(tok, dmid, dp0, dp1, wT, nm):
+        squares[...] += sq
+
+
+def enter(tok, dmid, dp0, dp1, wT, nm, chunks):
     t = tok.shape[0]
+    part = pl.BlockSpec((2 * D * SEQ // t, D), lambda i: (i, 0))
     return call(
         enter_kernel,
         "enter",
@@ -699,10 +706,11 @@
             per_image(3 * D // 2),
             full(wT),
             full(nm),
-        ],
-        out_specs=[per_image(D), whole(2, D)],
-        out_shape=[sds((t, D), f32), sds((2, D), f32)],
-    )(tok, dmid, dp0, dp1, wT, nm)
+        ]
+        + [part] * 4,
+        out_specs=[per_image(D), whole(2, D), part, whole(1, D)],
+        out_shape=[sds((t, D), f32), sds((2, D), f32), sds((2 * D, D), f32), sds((1, D), f32)],
+    )(tok, dmid, dp0, dp1, wT, nm, *chunks)
 
 
 def step_rates(experts):
@@ -727,9 +735,9 @@
 
 
 def adam_kernel(rates, where, nums, *refs):
-    own, other, owned = refs[:3]
-    weights, moments, outs = refs[3:7], refs[7:11], refs[11:27]
-    gq, go, pieces = refs[27:]
+    own, other, owned_in, owned_out = refs[:4]
+    weights, moments, outs = refs[4:8], refs[8:12], refs[12:28]
+    gq, go, pieces = refs[28:]
     groups, _, r, _ = pieces.shape
     i = pl.program_id(0)
 
@@ -763,12 +771,11 @@
                                 go[row : row + r, j * 128 : (j + 1) * 128] = tile
 
     rows_q, rows_o = weights[0].shape[0], weights[1].shape[0]
-    rows_e = weights[2].shape[1]
     grads = (
         gq[pl.ds(i * rows_q, rows_q), :].astype(f32),
         go[pl.ds(i * rows_o, rows_o), :].astype(f32),
-        owned[pl.ds(i * rows_e, rows_e), :],
-        owned[D:, pl.ds(pl.multiple_of(i * rows_e, 128), rows_e)].T,
+        owned_in[...],
+        owned_out[...].T,
     )
     factor = nums[0]
     fixes = (nums[1], nums[2])
@@ -803,7 +810,11 @@
         functools.partial(adam_kernel, rates),
         "adam",
         grid=(steps,),
-        in_specs=[SMEM, SMEM, full(own), full(other), full(owned)] + specs + mspecs,
+        in_specs=[SMEM, SMEM, full(own), full(other)]
+        + [
+            pl.BlockSpec((D // steps, D), lambda i: (i, 0)),
+            pl.BlockSpec((D, D // steps), lambda i: (1, i)),
+        ] + specs + mspecs,
         out_specs=[sp for sp in specs for _ in range(4)],
         out_shape=[sds(w.shape, dt) for w in weights for dt in (f32, f32, f32, bf16)],
         scratch_shapes=[
@@ -811,7 +822,37 @@
             pltpu.VMEM((128, D), bf16),
             pltpu.VMEM((2 * own.shape[0], *own.shape[1:]), bf16),
         ],
-    )(where, nums, own, other, owned, *weights, *moments)
+    )(where, nums, own, other, owned, owned, *weights, *moments)
+
+
+def settle_kernel(groups, small, squares, *refs):
+    got, (pieces, rest, terms) = refs[:4], refs[4:]
+    piece = got[0][...].astype(f32)
+    for g in got[1:]:
+        piece = piece + g[...].astype(f32)
+    pieces[...] = piece.astype(bf16)
+    own = jnp.sum(small[...], axis=0)
+    rest[...] = own
+    r = piece.shape[1]
+    flat = piece[0] * piece[0] + piece[1] * piece[1]
+    term = (
+        jnp.sum(flat, axis=(0, 1), keepdims=True)
+        + jnp.sum(squares[...], axis=(0, 1), keepdims=True)
+        + jnp.sum(own * own, axis=(0, 1), keepdims=True) / groups
+    )
+    terms[...] = jnp.broadcast_to(term[None], terms.shape)
+
+
+def settle(groups, small, squares, got):
+    args = (small, squares, *got)
+    devices, lines, _ = small.shape
+    return call(
+        functools.partial(settle_kernel, groups),
+        "settle",
+        in_specs=[whole(*a.shape) for a in args],
+        out_specs=[whole(*got[0].shape), whole(lines, 128), whole(devices, 1, 128)],
+        out_shape=[sds(got[0].shape, bf16), sds((lines, 128), f32), sds((devices, 1, 128), f32)],
+    )(*args)
 
 
 def swap(x, axis, k):
@@ -897,26 +938,28 @@
     in_w = [own_in, None, swap(own_in, "dp", 2), None]
     got, pos, cols = fence(got, pos, cols)
     got = jnp.stack(got)
-    got, misc = got[:, :64], got[:, 64:]
-    near = [swap(got, "expert", 2 * k) for k in (1, 2, 3)]
+    mine = got[:, :64]
+    near = [swap(mine, "expert", 2 * k) for k in (1, 2, 3)]
     up_slots = spread(where, pos, cotangent, pad, True)
     near, up_slots, in_w[2], own_in = fence(near, up_slots, in_w[2], own_in)
-    in_w[1], in_w[3] = swap(own_in, "dp", 1), swap(own_in, "dp", 3)
-    out_w = [own_out] + [swap(own_out, "dp", k) for k in (1, 2, 3)]
-    far = swap(jnp.stack([got] + near), "expert", 1)
+    own_e = jnp.concatenate([own_in, own_out], axis=0)
+    others = [swap(own_e, "dp", k) for k in (1, 3)]
+    out_w = [own_out, None, swap(own_out, "dp", 2), None]
+    far = swap(jnp.stack([mine] + near), "expert", 1)
     up = exchange(up_slots, "expert")
-    wT, ow, rT, nm = assemble(where, got, misc, jnp.stack(near), far, experts)
+    wT, ow, rT, nm = assemble(where, got, near, far, experts)
     proj, ctxT, lse, mid, sec, gatesT = attend(tokens, wT, ow, rT, nm)
 
     blocks = spread(where, pos, sec, pad, False)
     near = [k for k in range(2, groups) if (k >> 1) & ((k >> 1) - 1) == 0]
     distant = [k for k in range(2, groups) if (k >> 1) & ((k >> 1) - 1)]
-    in_w, out_w, blocks = fence(in_w, out_w, blocks)
+    in_w, out_w, others, blocks = fence(in_w, out_w, others, blocks)
+    weights = [in_w[0], in_w[2], out_w[0], out_w[2], *others]
     gated, dr, kept = None, {}, []
 
     def experts_on(ks, rows):
         d, gated_now, keep = run_experts(
-            where, tuple(ks), rows, up, in_w + out_w, rT, cap, gated
+            where, tuple(ks), rows, up, weights, rT, cap, gated
         )
         kept.append(keep)
         dr.update(zip(ks, d))
@@ -950,11 +993,13 @@
     dp1, packed1 = back(1, tok=tokens, dmid=dmid)
     got0, dp1, packed1, owned, dmid = fence(got0, dp1, packed1, owned, dmid)
 
-    got0 = to_owners(add_up(got0).astype(bf16), "dp", me_dp)
     got1 = exchange(packed1, "expert")
-    grad_input, dn_one = enter(tokens, dmid, dp0, dp1, wT, nm)
-    got0, got1, grad_input, dn_one, mid = fence(got0, got1, grad_input, dn_one, mid)
-    got1 = to_owners(add_up(got1).astype(bf16), "dp", me_dp)
+    grad_input, dn_one, owned, squares = enter(tokens, dmid, dp0, dp1, wT, nm, owned)
+    got1, grad_input, dn_one, mid, owned, squares, got0 = fence(
+        got1, grad_input, dn_one, mid, owned, squares, got0
+    )
+    both = jnp.stack([add_up(got0), add_up(got1)], axis=1).astype(bf16)
+    got = to_owners(both, "dp", me_dp)
 
     dn = jnp.concatenate([dn_one, dn_two], axis=0)
     small = jnp.stack(
@@ -971,17 +1016,9 @@
     small = jnp.broadcast_to(small[:, None], (n_dp, groups, lines, 128))
     small = exchange(small.reshape(devices, lines, 128), ("dp", "expert"))
     activations = finish(where, gated, cols, mid)
-    piece0 = add_up(got0)
-    owned = add_up(owned)
-    term = jnp.sum(piece0 * piece0) + jnp.sum(owned * owned)
-    got1, small, activations, piece0, owned, term = fence(
-        got1, small, activations, piece0, owned, term
-    )
-    piece1 = add_up(got1)
-    small = small.sum(0)
-    term = term + jnp.sum(piece1 * piece1) + jnp.sum(small * small) / groups
-    terms = exchange(jnp.full((devices, 1, 128), term, f32), ("dp", "expert"))
-    pieces = jnp.stack([piece0, piece1]).astype(bf16)
+    got, small, activations = fence(got, small, activations)
+    pieces, small, terms = settle(groups, small, squares, got)
+    terms = exchange(terms, ("dp", "expert"))
     mine = jnp.stack([pieces] + [swap(pieces, "expert", 2 * k) for k in range(1, groups // 2)])
     other = swap(mine, "expert", 1)
     share_router = jnp.concatenate(

time: 426 us -> 416 us (0.977)
  starting transfers between devices: 81 us -> 70.8 us
  other arithmetic: 18.7 us -> 13.1 us
  waiting for transfers between devices: 14.5 us -> 19.9 us
    ppermute x40 -> x35, starting transfers between devices: 52.3 us -> 42.2 us  [swap(): return lax.ppermute(x, axis, [(i, i ^ k) for i in range(n)])]
    ppermute x40 -> x35, waiting for transfers between devices: 7.41 us -> 13.6 us  [swap(): return lax.ppermute(x, axis, [(i, i ^ k) for i in range(n)])]
    reduce_sum x4 -> x0, other arithmetic: 5.67 us -> none  [the longest x2 5.03 us: shards(): term = jnp.sum(piece0 * piece0) + jnp.sum(owned * owned)]
  transfers between devices with their start and end apart: 46 -> 41, of which waited for: 5 -> 6; matrix products, arithmetic and copies ran while one was open for 5% -> 3% of each run, Pallas kernels for 66% -> 68%
where the time goes in v4:
time: 416 us; the launch traced here: 410 us
  Pallas kernels  289 us (69%)
  starting transfers between devices  70.8 us (17%)
  waiting for transfers between devices  19.9 us (5%)
  local copies, waits for them, and re-layouts  13.4 us (3%)
  other arithmetic  13.1 us (3%)
  between operations  4.26 us (1%)
    pallas_call x2, Pallas kernels, attend_back(): call(functools.partial(attend_back_kernel, part), 'attend_back', grid=(t...  65.6 us
    pallas_call x3, Pallas kernels, run_experts(): call(functools.partial(experts_kernel, cap, nb, gated is None), 'experts'...  54.3 us
    ppermute x35, starting transfers between devices, swap(): return lax.ppermute(x, axis, [(i, i ^ k) for i in range(n)])  42.2 us
    pallas_call x1, Pallas kernels, attend(): call(attend_kernel, 'attend', grid=(n,), in_specs=[per_image(D), full(wT)...  40.6 us
    pallas_call x2, Pallas kernels, spread(): call(functools.partial(spread_kernel, pad, together), 'spread', grid=(exp...  28.7 us
    all_to_all x6, starting transfers between devices, exchange(): return lax.all_to_all(x, axis, split_axis=0, concat_axis=0, tiled=True)  28.6 us
    pallas_call x1, Pallas kernels, combine(): call(functools.partial(combine_kernel, cap, experts), 'combine', grid=(t...  26.4 us
    pallas_call x1, Pallas kernels, weight_grads(): call(functools.partial(weights_kernel, groups), 'weight_grads', grid=(FF...  23.5 us
  transfers between devices with their start and end apart: 41, of which 6 were waited for; matrix products, arithmetic and copies ran while one was open for 3% of the time, Pallas kernels for 68%

profile of v4, /device:TPU:0, one launch (start us, length us, event | category | flops | bytes accessed | tf_op | source)
XLA Modules:
  0.0 410.1 jit_solution(8752782638827833883)
XLA Ops:
  17.9 5.1 %route.1 = (s32[4,8,720]{2,1,0:T(8,128)}, s32[2880,8]{1,0:T(8,128)}) custom-call(s32[3]{0:T(128)} %pad_add_fusion.where, s32[4,2,720]{2,1,0:T(2,128)} %bitcast.93, s32[4,2,720]{2,1,0:T(2,128)} %bitcast.94), custom_call_target="tpu_custom_call" | custom-call | flops 100000000 | bytes 100000 | tf_op jit(solution)/shard_map/route/pallas_call | solution.py:179
  23.1 4.8 %collective-permute-done.1 = bf16[80,512]{1,0:T(8,128)(2,1)S(1)} collective-permute-done((bf16[80,512]{1,0:T(8,128)(2,1)S(1)}, bf16[80,512]{1,0:T(8,128)(2,1)S(1)}, u32[]{:S(2)}, u32[]{:S(2)}) %collective-permute-start.1) | collective-permute-done | bytes 81952 | tf_op jit(solution)/shard_map/ppermute | solution.py:860
  31.6 14.1 %spread.2 = bf16[8,384,512]{2,1,0:T(8,128)(2,1)} custom-call(s32[3]{0:T(128)} %pad_add_fusion.where, s32[4,8,720]{2,1,0:T(8,128)} %get-tuple-element.195.pos, bf16[2880,512]{1,0:T(8,128)(2,1)} %refs_12_.1), custom_call_target="tpu_custom_call" | custom-call | flops 100000000 | bytes 100000 | tf_op jit(solution)/shard_map/spread/pallas_call | solution.py:218
  45.7 4.6 %all-to-all-start = ((bf16[8,384,512]{2,1,0:T(8,128)(2,1)}), bf16[8,384,512]{2,1,0:T(8,128)(2,1)}, u32[]{:S(2)}, u32[]{:S(2)}) async-start(bf16[8,384,512]{2,1,0:T(8,128)(2,1)} %spread.2), calls=%async_computation | async-start | bytes 6291456 | tf_op jit(solution)/shard_map/all_to_all | solution.py:864
  57.6 3.8 assemble.1
  61.4 40.6 %attend.1 = (bf16[2880,1536]{1,0:T(8,128)(2,1)}, bf16[4,512,720]{2,1,0:T(8,128)(2,1)}, f32[4,8,720]{2,1,0:T(8,128)}, f32[2880,512]{1,0:T(8,128)}, bf16[2880,512]{1,0:T(8,128)(2,1)}, /*index=5*/f32[4,8,720]{2,1,0:T(8,128)}) custom-call(bf16[2880,512]{1,0:T(8,128)(2,1)} %tok.7, bf16[1536,512]{1,0:T(8,128)(2,1)} %get-tuple-element.201.wT, ...), custom_call_target="tpu_custom_call" | custom-call | flops 100000000 | bytes 100000 | tf_op jit(solution)/shard_map/attend/pallas_call | solution.py:266
  102.1 14.6 %spread.3 = (bf16[384,512]{1,0:T(8,128)(2,1)}, bf16[384,512]{1,0:T(8,128)(2,1)}, bf16[384,512]{1,0:T(8,128)(2,1)}, bf16[384,512]{1,0:T(8,128)(2,1)}, bf16[384,51...) custom-call(s32[3]{0:T(128)} %pad_add_fusion.where, ...), custom_call_target="tpu_custom_call" | custom-call | flops 100000000 | bytes 100000 | tf_op jit(solution)/shard_map/spread/pallas_call | solution.py:218
  116.7 6.5 %collective-permute-done.7.refs_7_.refs_9_ = bf16[512,512]{1,0:T(8,128)(2,1)S(1)} collective-permute-done((bf16[512,512]{1,0:T(8,128)(2,1)S(1)}, bf16[512,512]{1,0:T(8,128)(2,1)S(1)}, u32[]{:S(2)}, u32[]{:S(2)}) %collective-permute-start.7) | collective-permute-done | bytes 524320 | tf_op jit(solution)/shard_map/ppermute | solution.py:860
  128.8 14.9 %experts.3 = (bf16[384,512]{1,0:T(8,128)(2,1)}, bf16[384,512]{1,0:T(8,128)(2,1)}, bf16[8,384,512]{2,1,0:T(8,128)(2,1)}, bf16[768,512]{1,0:T(8,128)(2,1)}, bf16[7...) custom-call(s32[2]{0:T(128)} %iota_xor_fusion.sources, s32[3]{0:T(128)} %pad_add_fusion.where, ...), custom_call_target="tpu_custom_call" | custom-call | flops 16000000000 | bytes 100000 | tf_op jit(solution)/shard_map/experts/pallas_call | solution.py:378
  149.6 24.5 %experts.4 = (bf16[384,512]{1,0:T(8,128)(2,1)}, bf16[384,512]{1,0:T(8,128)(2,1)}, bf16[384,512]{1,0:T(8,128)(2,1)}, bf16[384,512]{1,0:T(8,128)(2,1)}, bf16[8,384...) custom-call(s32[4]{0:T(128)} %broadcast_xor_fusion.sources, ...), custom_call_target="tpu_custom_call", output_to_operand_aliasing={{4}: (15, {})} | custom-call | flops 32000000000 | bytes 100000 | tf_op jit(solution)/shard_map/experts/pallas_call | solution.py:378
  178.2 14.9 %experts.5 = (bf16[384,512]{1,0:T(8,128)(2,1)}, bf16[384,512]{1,0:T(8,128)(2,1)}, bf16[8,384,512]{2,1,0:T(8,128)(2,1)}, bf16[768,512]{1,0:T(8,128)(2,1)}, bf16[7...) custom-call(s32[2]{0:T(128)} %broadcast_xor_fusion.1.sources, ...), custom_call_target="tpu_custom_call", output_to_operand_aliasing={{2}: (13, {})} | custom-call | flops 16000000000 | bytes 100000 | tf_op jit(solution)/shard_map/experts/pallas_call | solution.py:378
  195.7 23.5 %weight_grads.1 = (bf16[1024,512]{1,0:T(8,128)(2,1)}, bf16[1024,512]{1,0:T(8,128)(2,1)}, bf16[1024,512]{1,0:T(8,128)(2,1)}, bf16[1024,512]{1,0:T(8,128)(2,1)}) custom-call(bf16[768,512]{1,0:T(8,128)(2,1)} %get-tuple-element.260.refs_0_, bf16[1536,512]{1,0:T(8,128)(2,1)} %get-tuple-element.261.refs_1_, bf16[768,512]{1,0:T(8,128)(2,1)} %get-tuple-element.262.refs_2_, ...), custom_call_target="tpu_custom_call" | custom-call | flops 100000000 | bytes 100000 | tf_op jit(solution)/shard_map/weight_grads/pallas_call | solution.py:442
  221.1 3.8 all-to-all-start.1
  229.4 26.4 %combine.1 = (f32[2880,512]{1,0:T(8,128)}, f32[2,512]{1,0:T(2,128)}, f32[8,512]{1,0:T(8,128)}) custom-call(s32[3]{0:T(128)} %pad_add_fusion.where, bf16[384,512]{1,0:T(8,128)(2,1)} %get-tuple-element.278.refs_0_, bf16[384,512]{1,0:T(8,128)(2,1)} %copy-done.11, bf16[384,512]{1,0:T(8,128)(2,1)} %copy-done.12, bf16[384,512]{1,0:T(8,128)(2,1)} %copy-done.13, ...), custom_call_target="tpu_custom_call" | custom-call | flops 100000000 | bytes 100000 | tf_op jit(solution)/shard_map/combine/pallas_call | solution.py:511
  255.8 32.8 %attend_back.2 = (bf16[2880,768]{1,0:T(8,128)(2,1)}, bf16[8,4,128,128]{3,2,1,0:T(8,128)(2,1)}) custom-call(bf16[2880,512]{1,0:T(8,128)(2,1)} %tok.7, f32[2880,512]{1,0:T(8,128)} %get-tuple-element.304.dmid, bf16[2880,1536]{1,0:T(8,128)(2,1)} %get-tuple-element.290.proj, bf16[4,512,720]{2,1,0:T(8,128)(2,1)} %get-tuple-element.291.ctxT, ...), custom_call_target="tpu_custom_call" | custom-call | flops 100000000 | bytes 100000 | tf_op jit(solution)/shard_map/attend_back/pallas_call | solution.py:638
  288.6 4.5 %all-to-all-start.2 = ((bf16[8,4,128,128]{3,2,1,0:T(8,128)(2,1)}), bf16[8,4,128,128]{3,2,1,0:T(8,128)(2,1)}, u32[]{:S(2)}, u32[]{:S(2)}) async-start(bf16[8,4,128,128]{3,2,1,0:T(8,128)(2,1)} %get-tuple-element.295), calls=%async_computation.2 | async-start | bytes 2097152 | tf_op jit(solution)/shard_map/all_to_all | solution.py:864
  293.1 32.8 %attend_back.3 = (bf16[2880,768]{1,0:T(8,128)(2,1)}, bf16[8,4,128,128]{3,2,1,0:T(8,128)(2,1)}) custom-call(bf16[2880,512]{1,0:T(8,128)(2,1)} %tok.7, f32[2880,512]{1,0:T(8,128)} %get-tuple-element.304.dmid, bf16[2880,1536]{1,0:T(8,128)(2,1)} %get-tuple-element.290.proj, bf16[4,512,720]{2,1,0:T(8,128)(2,1)} %get-tuple-element.291.ctxT, ...), custom_call_target="tpu_custom_call" | custom-call | flops 100000000 | bytes 100000 | tf_op jit(solution)/shard_map/attend_back/pallas_call | solution.py:638
  325.9 4.2 %all-to-all-start.3 = ((bf16[8,4,128,128]{3,2,1,0:T(8,128)(2,1)}), bf16[8,4,128,128]{3,2,1,0:T(8,128)(2,1)S(1)}, u32[]{:S(2)}, u32[]{:S(2)}) async-start(bf16[8,4,128,128]{3,2,1,0:T(8,128)(2,1)} %get-tuple-element.303), calls=%async_computation.3 | async-start | bytes 2097152 | tf_op jit(solution)/shard_map/all_to_all | solution.py:864
  330.2 15.4 %enter.1 = (f32[2880,512]{1,0:T(8,128)}, f32[2,512]{1,0:T(2,128)}, f32[1024,512]{1,0:T(8,128)}, f32[1,512]{1,0:T(1,128)}) custom-call(bf16[2880,512]{1,0:T(8,128)(2,1)} %tok.7, f32[2880,512]{1,0:T(8,128)} %get-tuple-element.304.dmid, bf16[2880,768]{1,0:T(8,128)(2,1)} %get-tuple-element.305.dp0, bf16[2880,768]{1,0:T(8,128)(2,1)} %get-tuple-element.306.dp1, ...), custom_call_target="tpu_custom_call" | custom-call | flops 100000000 | bytes 100000 | tf_op jit(solution)/shard_map/enter/pallas_call | solution.py:698
  347.2 5.6 %all-to-all-start.4 = ((f32[32,12,128]{2,1,0:T(8,128)}), f32[32,12,128]{2,1,0:T(8,128)S(1)}, u32[]{:S(2)}, u32[]{:S(2)}) async-start(f32[32,12,128]{2,1,0:T(8,128)} %bitcast.27), calls=%async_computation.4 | async-start | bytes 524288 | tf_op jit(solution)/shard_map/all_to_all | solution.py:864
  360.2 14.0 %finish.1 = bf16[2880,512]{1,0:T(8,128)(2,1)} custom-call(s32[3]{0:T(128)} %pad_add_fusion.where, bf16[8,384,512]{2,1,0:T(8,128)(2,1)} %copy-done, s32[2880,8]{1,0:T(8,128)} %get-tuple-element.286.refs_8_.cols, f32[2880,512]{1,0:T(8,128)} %get-tuple-element.322.refs_11_.mid), custom_call_target="tpu_custom_call" | custom-call | flops 100000000 | bytes 100000 | tf_op jit(solution)/shard_map/finish/pallas_call | solution.py:546
  380.3 5.9 %all-to-all-start.5 = ((f32[32,1,128]{2,1,0:T(1,128)}), f32[32,1,128]{2,1,0:T(1,128)S(1)}, u32[]{:S(2)}, u32[]{:S(2)}) async-start(f32[32,1,128]{2,1,0:T(1,128)} %get-tuple-element.331), calls=%async_computation.5 | async-start | bytes 32768 | tf_op jit(solution)/shard_map/all_to_all | solution.py:864
  387.1 6.2 %all-to-all-done.5 = f32[32,1,128]{2,1,0:T(1,128)S(1)} async-done(((f32[32,1,128]{2,1,0:T(1,128)}), f32[32,1,128]{2,1,0:T(1,128)S(1)}, u32[]{:S(2)}, u32[]{:S(2)}) %all-to-all-start.5) | async-done | bytes 16416 | tf_op jit(solution)/shard_map/all_to_all | solution.py:864
  399.3 9.5 %adam.1 = (f32[512,384]{1,0:T(8,128)}, f32[512,384]{1,0:T(8,128)}, f32[512,384]{1,0:T(8,128)}, bf16[512,384]{1,0:T(8,128)(2,1)}, f32[128,512]{1,0:T(8,128)}, /*i...) custom-call(s32[3]{0:T(128)} %pad_add_fusion.where, ...), custom_call_target="tpu_custom_call" | custom-call | flops 100000000 | bytes 100000 | tf_op jit(solution)/shard_map/adam/pallas_call | solution.py:809
  (195 shorter events, 72.8 us)
Async XLA Ops:
  7.4 20.5 %collective-permute-start.1 = (bf16[80,512]{1,0:T(8,128)(2,1)S(1)}, bf16[80,512]{1,0:T(8,128)(2,1)S(1)}, u32[]{:S(2)}, u32[]{:S(2)}) collective-permute-start(bf16[80,512]{1,0:T(8,128)(2,1)S(1)} %concatenate.24), channel_id=1, source_target_pairs={{0,16},{8,24},{16,0},{24,8},{1,17},{9,25},{17,1},{25,9},{2,18},{10... | collective-permute-start | bytes 245768 | tf_op jit(solution)/shard_map/ppermute | solution.py:860
  11.3 34.4 %collective-permute-start.6 = (bf16[512,512]{1,0:T(8,128)(2,1)S(1)}, bf16[512,512]{1,0:T(8,128)(2,1)}, u32[]{:S(2)}, u32[]{:S(2)}) collective-permute-start(bf16[512,512]{1,0:T(8,128)(2,1)S(1)} %convert_bitcast_fusion.1.refs_4_.refs_6_), channel_id=1, source_target_pairs={{0,16},{8,24},{16,0},{24,8},{1,17},{9,25},{17,1},{25,9},{2,18},{10... | collective-permute-start | bytes 1572872 | tf_op jit(solution)/shard_map/ppermute | solution.py:860
  45.7 82.4 %all-to-all-start = ((bf16[8,384,512]{2,1,0:T(8,128)(2,1)}), bf16[8,384,512]{2,1,0:T(8,128)(2,1)}, u32[]{:S(2)}, u32[]{:S(2)}) async-start(bf16[8,384,512]{2,1,0:T(8,128)(2,1)} %spread.2), calls=%async_computation | async-start | bytes 6291456 | tf_op jit(solution)/shard_map/all_to_all | solution.py:864
  51.1 72.1 %collective-permute-start.8 = (bf16[1024,512]{1,0:T(8,128)(2,1)S(1)}, bf16[1024,512]{1,0:T(8,128)(2,1)}, u32[]{:S(2)}, u32[]{:S(2)}) collective-permute-start(bf16[1024,512]{1,0:T(8,128)(2,1)S(1)} %pad_maximum_fusion), channel_id=1, source_target_pairs={{0,8},{8,0},{16,24},{24,16},{1,9},{9,1},{17,25},{25,17},{2,10},{10... | collective-permute-start | bytes 3145736 | tf_op jit(solution)/shard_map/ppermute | solution.py:860
  53.5 69.7 %collective-permute-start.9 = (bf16[1024,512]{1,0:T(8,128)(2,1)S(1)}, bf16[1024,512]{1,0:T(8,128)(2,1)}, u32[]{:S(2)}, u32[]{:S(2)}) collective-permute-start(bf16[1024,512]{1,0:T(8,128)(2,1)S(1)} %pad_maximum_fusion), channel_id=1, source_target_pairs={{0,24},{8,16},{16,8},{24,0},{1,25},{9,17},{17,9},{25,1},{2,26},{10... | collective-permute-start | bytes 3145736 | tf_op jit(solution)/shard_map/ppermute | solution.py:860
  56.1 67.0 %collective-permute-start.7 = (bf16[512,512]{1,0:T(8,128)(2,1)S(1)}, bf16[512,512]{1,0:T(8,128)(2,1)S(1)}, u32[]{:S(2)}, u32[]{:S(2)}) collective-permute-start(bf16[512,512]{1,0:T(8,128)(2,1)S(1)} %convert_bitcast_fusion.refs_6_.refs_8_), channel_id=1, source_target_pairs={{0,16},{8,24},{16,0},{24,8},{1,17},{9,25},{17,1},{25,9},{2,18},{10... | collective-permute-start | bytes 1572872 | tf_op jit(solution)/shard_map/ppermute | solution.py:860
  124.4 19.4 %collective-permute-start.12 = (bf16[384,512]{1,0:T(8,128)(2,1)}, bf16[384,512]{1,0:T(8,128)(2,1)S(1)}, u32[]{:S(2)}, u32[]{:S(2)}) collective-permute-start(bf16[384,512]{1,0:T(8,128)(2,1)} %get-tuple-element.226), channel_id=1, source_target_pairs={{0,2},{1,3},{2,0},{3,1},{4,6},{5,7},{6,4},{7,5},{8,10},{9,11},{10,... | collective-permute-start | bytes 1179656 | tf_op jit(solution)/shard_map/ppermute | solution.py:860
  146.5 29.4 %collective-permute-start.16 = (bf16[384,512]{1,0:T(8,128)(2,1)S(1)}, bf16[384,512]{1,0:T(8,128)(2,1)S(1)}, u32[]{:S(2)}, u32[]{:S(2)}) collective-permute-start(bf16[384,512]{1,0:T(8,128)(2,1)S(1)} %copy-done.31), channel_id=1, source_target_pairs={{0,6},{1,7},{2,4},{3,5},{4,2},{5,3},{6,0},{7,1},{8,14},{9,15},{10,... | collective-permute-start | bytes 1179656 | tf_op jit(solution)/shard_map/ppermute | solution.py:860
  149.2 28.3 %collective-permute-start.17 = (bf16[384,512]{1,0:T(8,128)(2,1)S(1)}, bf16[384,512]{1,0:T(8,128)(2,1)S(1)}, u32[]{:S(2)}, u32[]{:S(2)}) collective-permute-start(bf16[384,512]{1,0:T(8,128)(2,1)S(1)} %copy-done.30), channel_id=1, source_target_pairs={{0,7},{1,6},{2,5},{3,4},{4,3},{5,2},{6,1},{7,0},{8,15},{9,14},{10,... | collective-permute-start | bytes 1179656 | tf_op jit(solution)/shard_map/ppermute | solution.py:860
  149.2 28.5 %collective-permute-start.18 = (bf16[384,512]{1,0:T(8,128)(2,1)}, bf16[384,512]{1,0:T(8,128)(2,1)S(1)}, u32[]{:S(2)}, u32[]{:S(2)}) collective-permute-start(bf16[384,512]{1,0:T(8,128)(2,1)} %get-tuple-element.249), channel_id=1, source_target_pairs={{0,1},{1,0},{2,3},{3,2},{4,5},{5,4},{6,7},{7,6},{8,9},{9,8},{10,11... | collective-permute-start | bytes 1179656 | tf_op jit(solution)/shard_map/ppermute | solution.py:860
  174.1 21.2 %collective-permute-start.19 = (bf16[384,512]{1,0:T(8,128)(2,1)}, bf16[384,512]{1,0:T(8,128)(2,1)S(1)}, u32[]{:S(2)}, u32[]{:S(2)}) collective-permute-start(bf16[384,512]{1,0:T(8,128)(2,1)} %get-tuple-element.251), channel_id=1, source_target_pairs={{0,2},{1,3},{2,0},{3,1},{4,6},{5,7},{6,4},{7,5},{8,10},{9,11},{10,... | collective-permute-start | bytes 1179656 | tf_op jit(solution)/shard_map/ppermute | solution.py:860
  175.9 43.3 %collective-permute-start.20 = (bf16[384,512]{1,0:T(8,128)(2,1)}, bf16[384,512]{1,0:T(8,128)(2,1)S(1)}, u32[]{:S(2)}, u32[]{:S(2)}) collective-permute-start(bf16[384,512]{1,0:T(8,128)(2,1)} %get-tuple-element.252), channel_id=1, source_target_pairs={{0,3},{1,2},{2,1},{3,0},{4,7},{5,6},{6,5},{7,4},{8,11},{9,10},{10,... | collective-permute-start | bytes 1179656 | tf_op jit(solution)/shard_map/ppermute | solution.py:860
  175.9 44.1 %collective-permute-start.21 = (bf16[384,512]{1,0:T(8,128)(2,1)}, bf16[384,512]{1,0:T(8,128)(2,1)S(1)}, u32[]{:S(2)}, u32[]{:S(2)}) collective-permute-start(bf16[384,512]{1,0:T(8,128)(2,1)} %get-tuple-element.253), channel_id=1, source_target_pairs={{0,4},{1,5},{2,6},{3,7},{4,0},{5,1},{6,2},{7,3},{8,12},{9,13},{10,... | collective-permute-start | bytes 1179656 | tf_op jit(solution)/shard_map/ppermute | solution.py:860
  177.4 42.5 %collective-permute-start.22 = (bf16[384,512]{1,0:T(8,128)(2,1)}, bf16[384,512]{1,0:T(8,128)(2,1)S(1)}, u32[]{:S(2)}, u32[]{:S(2)}) collective-permute-start(bf16[384,512]{1,0:T(8,128)(2,1)} %get-tuple-element.254), channel_id=1, source_target_pairs={{0,5},{1,4},{2,7},{3,6},{4,1},{5,0},{6,3},{7,2},{8,13},{9,12},{10,... | collective-permute-start | bytes 1179656 | tf_op jit(solution)/shard_map/ppermute | solution.py:860
  193.1 26.9 %collective-permute-start.23 = (bf16[384,512]{1,0:T(8,128)(2,1)}, bf16[384,512]{1,0:T(8,128)(2,1)S(1)}, u32[]{:S(2)}, u32[]{:S(2)}) collective-permute-start(bf16[384,512]{1,0:T(8,128)(2,1)} %get-tuple-element.258), channel_id=1, source_target_pairs={{0,6},{1,7},{2,4},{3,5},{4,2},{5,3},{6,0},{7,1},{8,14},{9,15},{10,... | collective-permute-start | bytes 1179656 | tf_op jit(solution)/shard_map/ppermute | solution.py:860
  195.3 24.7 %collective-permute-start.24 = (bf16[384,512]{1,0:T(8,128)(2,1)}, bf16[384,512]{1,0:T(8,128)(2,1)S(1)}, u32[]{:S(2)}, u32[]{:S(2)}) collective-permute-start(bf16[384,512]{1,0:T(8,128)(2,1)} %get-tuple-element.259), channel_id=1, source_target_pairs={{0,7},{1,6},{2,5},{3,4},{4,3},{5,2},{6,1},{7,0},{8,15},{9,14},{10,... | collective-permute-start | bytes 1179656 | tf_op jit(solution)/shard_map/ppermute | solution.py:860
  221.1 67.5 %all-to-all-start.1 = ((bf16[8,384,512]{2,1,0:T(8,128)(2,1)}), bf16[8,384,512]{2,1,0:T(8,128)(2,1)S(1)}, u32[]{:S(2)}, u32[]{:S(2)}) async-start(bf16[8,384,512]{2,1,0:T(8,128)(2,1)} %get-tuple-element.277), calls=%async_computation.1 | async-start | bytes 6291456 | tf_op jit(solution)/shard_map/all_to_all | solution.py:864
  224.9 101.0 %collective-permute-start.25 = (bf16[1024,512]{1,0:T(8,128)(2,1)}, bf16[1024,512]{1,0:T(8,128)(2,1)}, u32[]{:S(2)}, u32[]{:S(2)}) collective-permute-start(bf16[1024,512]{1,0:T(8,128)(2,1)} %get-tuple-element.300), channel_id=1, source_target_pairs={{0,8},{8,0},{16,24},{24,16},{1,9},{9,1},{17,25},{25,17},{2,10},{10... | collective-permute-start | bytes 3145736 | tf_op jit(solution)/shard_map/ppermute | solution.py:860
  225.0 100.9 %collective-permute-start.26 = (bf16[1024,512]{1,0:T(8,128)(2,1)}, bf16[1024,512]{1,0:T(8,128)(2,1)}, u32[]{:S(2)}, u32[]{:S(2)}) collective-permute-start(bf16[1024,512]{1,0:T(8,128)(2,1)} %get-tuple-element.301), channel_id=1, source_target_pairs={{0,16},{8,24},{16,0},{24,8},{1,17},{9,25},{17,1},{25,9},{2,18},{10... | collective-permute-start | bytes 3145736 | tf_op jit(solution)/shard_map/ppermute | solution.py:860
  228.2 97.7 %collective-permute-start.27 = (bf16[1024,512]{1,0:T(8,128)(2,1)}, bf16[1024,512]{1,0:T(8,128)(2,1)}, u32[]{:S(2)}, u32[]{:S(2)}) collective-permute-start(bf16[1024,512]{1,0:T(8,128)(2,1)} %get-tuple-element.302), channel_id=1, source_target_pairs={{0,24},{8,16},{16,8},{24,0},{1,25},{9,17},{17,9},{25,1},{2,26},{10... | collective-permute-start | bytes 3145736 | tf_op jit(solution)/shard_map/ppermute | solution.py:860
  288.6 37.3 %all-to-all-start.2 = ((bf16[8,4,128,128]{3,2,1,0:T(8,128)(2,1)}), bf16[8,4,128,128]{3,2,1,0:T(8,128)(2,1)}, u32[]{:S(2)}, u32[]{:S(2)}) async-start(bf16[8,4,128,128]{3,2,1,0:T(8,128)(2,1)} %get-tuple-element.295), calls=%async_computation.2 | async-start | bytes 2097152 | tf_op jit(solution)/shard_map/all_to_all | solution.py:864
  325.9 19.6 %all-to-all-start.3 = ((bf16[8,4,128,128]{3,2,1,0:T(8,128)(2,1)}), bf16[8,4,128,128]{3,2,1,0:T(8,128)(2,1)S(1)}, u32[]{:S(2)}, u32[]{:S(2)}) async-start(bf16[8,4,128,128]{3,2,1,0:T(8,128)(2,1)} %get-tuple-element.303), calls=%async_computation.3 | async-start | bytes 2097152 | tf_op jit(solution)/shard_map/all_to_all | solution.py:864
  347.2 27.1 %all-to-all-start.4 = ((f32[32,12,128]{2,1,0:T(8,128)}), f32[32,12,128]{2,1,0:T(8,128)S(1)}, u32[]{:S(2)}, u32[]{:S(2)}) async-start(f32[32,12,128]{2,1,0:T(8,128)} %bitcast.27), calls=%async_computation.4 | async-start | bytes 524288 | tf_op jit(solution)/shard_map/all_to_all | solution.py:864
  376.8 19.2 %collective-permute-start.31 = (bf16[2,128,128]{2,1,0:T(8,128)(2,1)}, bf16[2,128,128]{2,1,0:T(8,128)(2,1)S(1)}, u32[]{:S(2)}, u32[]{:S(2)}) collective-permute-start(bf16[2,128,128]{2,1,0:T(8,128)(2,1)} %get-tuple-element.332), channel_id=1, source_target_pairs={{0,2},{1,3},{2,0},{3,1},{4,6},{5,7},{6,4},{7,5},{8,10},{9,11},{10,... | collective-permute-start | bytes 196616 | tf_op jit(solution)/shard_map/ppermute | solution.py:860
  (58 other events, 828.7 us)

commit v5 on v4

--- a/solution.py
+++ b/solution.py
@@ -293,15 +293,15 @@
 
 
 def experts_kernel(cap, nb, first, sources, where, *refs):
-    rows, (u0, u1), gw, rT = refs[:nb], refs[nb : nb + 2], refs[nb + 2 : nb + 8], refs[nb + 8]
-    refs = refs[nb + 9 :] if first else refs[nb + 10 :]
+    rows, (u0, u1), gw, rT = refs[:nb], refs[nb : nb + 2], refs[nb + 2 : nb + 9], refs[nb + 9]
+    refs = refs[nb + 10 :] if first else refs[nb + 11 :]
     dr = refs[:nb]
     gated, xs, db, act, dh, gb, sems = refs[nb:]
     s = pl.program_id(0)
     pad = rows[0].shape[0]
     me = where[2]
-    iw = [gw[0], gw[4].at[:D], gw[1], gw[5].at[:D]]
-    xw = [gw[2], gw[4].at[D:], gw[3], gw[5].at[D:]]
+    iw = [gw[0], gw[6].at[:D], gw[1], gw[2]]
+    xw = [gw[3], gw[6].at[D:], gw[4], gw[5]]
     chunks, cols = len(iw), iw[0].shape[1]
     for i in range(nb // 2):
 
@@ -395,7 +395,7 @@
         + [sds(u.shape, bf16)]
         + [sds((nb * pad, D), bf16)] * 2
         + [sds((nb * pad, hidden), bf16)] * 2,
-        input_output_aliases={nb + 11: nb} if prior else {},
+        input_output_aliases={nb + 12: nb} if prior else {},
     )(where[2] ^ jnp.asarray(ks, i32), where, *rows, u, u, *gw, rT, *prior)
     return out[:nb], out[nb], out[nb + 1 :]
 
@@ -943,8 +943,9 @@
     up_slots = spread(where, pos, cotangent, pad, True)
     near, up_slots, in_w[2], own_in = fence(near, up_slots, in_w[2], own_in)
     own_e = jnp.concatenate([own_in, own_out], axis=0)
-    others = [swap(own_e, "dp", k) for k in (1, 3)]
-    out_w = [own_out, None, swap(own_out, "dp", 2), None]
+    in_w[3] = swap(in_w[2], "dp", 1)
+    out_w = [own_out, None, swap(own_out, "dp", 2), swap(own_out, "dp", 3)]
+    both = swap(own_e, "dp", 1)
     far = swap(jnp.stack([mine] + near), "expert", 1)
     up = exchange(up_slots, "expert")
     wT, ow, rT, nm = assemble(where, got, near, far, experts)
@@ -953,8 +954,8 @@
     blocks = spread(where, pos, sec, pad, False)
     near = [k for k in range(2, groups) if (k >> 1) & ((k >> 1) - 1) == 0]
     distant = [k for k in range(2, groups) if (k >> 1) & ((k >> 1) - 1)]
-    in_w, out_w, others, blocks = fence(in_w, out_w, others, blocks)
-    weights = [in_w[0], in_w[2], out_w[0], out_w[2], *others]
+    in_w, out_w, both, blocks = fence(in_w, out_w, both, blocks)
+    weights = [in_w[0], in_w[2], in_w[3], out_w[0], out_w[2], out_w[3], both]
     gated, dr, kept = None, {}, []
 
     def experts_on(ks, rows):

time: 416 us -> 410 us (0.986)
  waiting for transfers between devices: 19.9 us -> 14.3 us
    ppermute x35 -> x36, waiting for transfers between devices: 13.6 us -> 8.07 us  [swap(): return lax.ppermute(x, axis, [(i, i ^ k) for i in range(n)])]
    ppermute x35 -> x36, starting transfers between devices: 42.2 us -> 42.8 us  [swap(): return lax.ppermute(x, axis, [(i, i ^ k) for i in range(n)])]
  transfers between devices with their start and end apart: 41 -> 42, of which waited for: 6 -> 5; matrix products, arithmetic and copies ran while one was open for 3% -> 4% of each run, Pallas kernels for 68% -> 69%
where the time goes in v5:
time: 410 us; the launch traced here: 404 us
  Pallas kernels  289 us (70%)
  starting transfers between devices  71.4 us (17%)
  waiting for transfers between devices  14.3 us (3%)
  other arithmetic  13.1 us (3%)
  local copies, waits for them, and re-layouts  12 us (3%)
  between operations  4.29 us (1%)
    pallas_call x2, Pallas kernels, attend_back(): call(functools.partial(attend_back_kernel, part), 'attend_back', grid=(t...  65.6 us
    pallas_call x3, Pallas kernels, run_experts(): call(functools.partial(experts_kernel, cap, nb, gated is None), 'experts'...  54.4 us
    ppermute x36, starting transfers between devices, swap(): return lax.ppermute(x, axis, [(i, i ^ k) for i in range(n)])  42.8 us
    pallas_call x1, Pallas kernels, attend(): call(attend_kernel, 'attend', grid=(n,), in_specs=[per_image(D), full(wT)...  40.6 us
    pallas_call x2, Pallas kernels, spread(): call(functools.partial(spread_kernel, pad, together), 'spread', grid=(exp...  28.7 us
    all_to_all x6, starting transfers between devices, exchange(): return lax.all_to_all(x, axis, split_axis=0, concat_axis=0, tiled=True)  28.6 us
    pallas_call x1, Pallas kernels, combine(): call(functools.partial(combine_kernel, cap, experts), 'combine', grid=(t...  26.4 us
    pallas_call x1, Pallas kernels, weight_grads(): call(functools.partial(weights_kernel, groups), 'weight_grads', grid=(FF...  23.4 us
  transfers between devices with their start and end apart: 42, of which 5 were waited for; matrix products, arithmetic and copies ran while one was open for 4% of the time, Pallas kernels for 69%

profile of v5, /device:TPU:0, one launch (start us, length us, event | category | flops | bytes accessed | tf_op | source)
XLA Modules:
  0.0 403.7 jit_solution(16488337561548025843)
XLA Ops:
  4.3 3.1 collective-permute-start
  17.9 5.1 %route.1 = (s32[4,8,720]{2,1,0:T(8,128)}, s32[2880,8]{1,0:T(8,128)}) custom-call(s32[3]{0:T(128)} %pad_add_fusion.where, s32[4,2,720]{2,1,0:T(2,128)} %bitcast.93, s32[4,2,720]{2,1,0:T(2,128)} %bitcast.94), custom_call_target="tpu_custom_call" | custom-call | flops 100000000 | bytes 100000 | tf_op jit(solution)/shard_map/route/pallas_call | solution.py:179
  23.0 4.9 %collective-permute-done.1 = bf16[80,512]{1,0:T(8,128)(2,1)S(1)} collective-permute-done((bf16[80,512]{1,0:T(8,128)(2,1)S(1)}, bf16[80,512]{1,0:T(8,128)(2,1)S(1)}, u32[]{:S(2)}, u32[]{:S(2)}) %collective-permute-start.1) | collective-permute-done | bytes 81952 | tf_op jit(solution)/shard_map/ppermute | solution.py:860
  31.6 14.1 %spread.2 = bf16[8,384,512]{2,1,0:T(8,128)(2,1)} custom-call(s32[3]{0:T(128)} %pad_add_fusion.where, s32[4,8,720]{2,1,0:T(8,128)} %get-tuple-element.196.pos, bf16[2880,512]{1,0:T(8,128)(2,1)} %refs_12_.1), custom_call_target="tpu_custom_call" | custom-call | flops 100000000 | bytes 100000 | tf_op jit(solution)/shard_map/spread/pallas_call | solution.py:218
  45.7 4.6 %all-to-all-start = ((bf16[8,384,512]{2,1,0:T(8,128)(2,1)}), bf16[8,384,512]{2,1,0:T(8,128)(2,1)}, u32[]{:S(2)}, u32[]{:S(2)}) async-start(bf16[8,384,512]{2,1,0:T(8,128)(2,1)} %spread.2), calls=%async_computation | async-start | bytes 6291456 | tf_op jit(solution)/shard_map/all_to_all | solution.py:864
  58.5 3.8 assemble.1
  62.2 40.6 %attend.1 = (bf16[2880,1536]{1,0:T(8,128)(2,1)}, bf16[4,512,720]{2,1,0:T(8,128)(2,1)}, f32[4,8,720]{2,1,0:T(8,128)}, f32[2880,512]{1,0:T(8,128)}, bf16[2880,512]{1,0:T(8,128)(2,1)}, /*index=5*/f32[4,8,720]{2,1,0:T(8,128)}) custom-call(bf16[2880,512]{1,0:T(8,128)(2,1)} %tok.7, bf16[1536,512]{1,0:T(8,128)(2,1)} %get-tuple-element.202.wT, ...), custom_call_target="tpu_custom_call" | custom-call | flops 100000000 | bytes 100000 | tf_op jit(solution)/shard_map/attend/pallas_call | solution.py:266
  102.9 14.6 %spread.3 = (bf16[384,512]{1,0:T(8,128)(2,1)}, bf16[384,512]{1,0:T(8,128)(2,1)}, bf16[384,512]{1,0:T(8,128)(2,1)}, bf16[384,512]{1,0:T(8,128)(2,1)}, bf16[384,51...) custom-call(s32[3]{0:T(128)} %pad_add_fusion.where, ...), custom_call_target="tpu_custom_call" | custom-call | flops 100000000 | bytes 100000 | tf_op jit(solution)/shard_map/spread/pallas_call | solution.py:218
  122.3 14.9 %experts.3 = (bf16[384,512]{1,0:T(8,128)(2,1)}, bf16[384,512]{1,0:T(8,128)(2,1)}, bf16[8,384,512]{2,1,0:T(8,128)(2,1)}, bf16[768,512]{1,0:T(8,128)(2,1)}, bf16[7...) custom-call(s32[2]{0:T(128)} %iota_xor_fusion.sources, s32[3]{0:T(128)} %pad_add_fusion.where, ...), custom_call_target="tpu_custom_call" | custom-call | flops 16000000000 | bytes 100000 | tf_op jit(solution)/shard_map/experts/pallas_call | solution.py:378
  143.3 24.5 %experts.4 = (bf16[384,512]{1,0:T(8,128)(2,1)}, bf16[384,512]{1,0:T(8,128)(2,1)}, bf16[384,512]{1,0:T(8,128)(2,1)}, bf16[384,512]{1,0:T(8,128)(2,1)}, bf16[8,384...) custom-call(s32[4]{0:T(128)} %broadcast_xor_fusion.sources, ...), custom_call_target="tpu_custom_call", output_to_operand_aliasing={{4}: (16, {})} | custom-call | flops 32000000000 | bytes 100000 | tf_op jit(solution)/shard_map/experts/pallas_call | solution.py:378
  171.9 15.0 %experts.5 = (bf16[384,512]{1,0:T(8,128)(2,1)}, bf16[384,512]{1,0:T(8,128)(2,1)}, bf16[8,384,512]{2,1,0:T(8,128)(2,1)}, bf16[768,512]{1,0:T(8,128)(2,1)}, bf16[7...) custom-call(s32[2]{0:T(128)} %broadcast_xor_fusion.1.sources, ...), custom_call_target="tpu_custom_call", output_to_operand_aliasing={{2}: (14, {})} | custom-call | flops 16000000000 | bytes 100000 | tf_op jit(solution)/shard_map/experts/pallas_call | solution.py:378
  189.5 23.4 %weight_grads.1 = (bf16[1024,512]{1,0:T(8,128)(2,1)}, bf16[1024,512]{1,0:T(8,128)(2,1)}, bf16[1024,512]{1,0:T(8,128)(2,1)}, bf16[1024,512]{1,0:T(8,128)(2,1)}) custom-call(bf16[768,512]{1,0:T(8,128)(2,1)} %get-tuple-element.262.refs_0_, bf16[1536,512]{1,0:T(8,128)(2,1)} %get-tuple-element.263.refs_1_, bf16[768,512]{1,0:T(8,128)(2,1)} %get-tuple-element.264.refs_2_, ...), custom_call_target="tpu_custom_call" | custom-call | flops 100000000 | bytes 100000 | tf_op jit(solution)/shard_map/weight_grads/pallas_call | solution.py:442
  214.7 3.8 all-to-all-start.1
  223.0 26.4 %combine.1 = (f32[2880,512]{1,0:T(8,128)}, f32[2,512]{1,0:T(2,128)}, f32[8,512]{1,0:T(8,128)}) custom-call(s32[3]{0:T(128)} %pad_add_fusion.where, bf16[384,512]{1,0:T(8,128)(2,1)} %get-tuple-element.280.refs_0_, bf16[384,512]{1,0:T(8,128)(2,1)} %copy-done.11, bf16[384,512]{1,0:T(8,128)(2,1)} %copy-done.12, bf16[384,512]{1,0:T(8,128)(2,1)} %copy-done.13, ...), custom_call_target="tpu_custom_call" | custom-call | flops 100000000 | bytes 100000 | tf_op jit(solution)/shard_map/combine/pallas_call | solution.py:511
  249.4 32.8 %attend_back.2 = (bf16[2880,768]{1,0:T(8,128)(2,1)}, bf16[8,4,128,128]{3,2,1,0:T(8,128)(2,1)}) custom-call(bf16[2880,512]{1,0:T(8,128)(2,1)} %tok.7, f32[2880,512]{1,0:T(8,128)} %get-tuple-element.306.dmid, bf16[2880,1536]{1,0:T(8,128)(2,1)} %get-tuple-element.292.proj, bf16[4,512,720]{2,1,0:T(8,128)(2,1)} %get-tuple-element.293.ctxT, ...), custom_call_target="tpu_custom_call" | custom-call | flops 100000000 | bytes 100000 | tf_op jit(solution)/shard_map/attend_back/pallas_call | solution.py:638
  282.2 4.5 %all-to-all-start.2 = ((bf16[8,4,128,128]{3,2,1,0:T(8,128)(2,1)}), bf16[8,4,128,128]{3,2,1,0:T(8,128)(2,1)}, u32[]{:S(2)}, u32[]{:S(2)}) async-start(bf16[8,4,128,128]{3,2,1,0:T(8,128)(2,1)} %get-tuple-element.297), calls=%async_computation.2 | async-start | bytes 2097152 | tf_op jit(solution)/shard_map/all_to_all | solution.py:864
  286.7 32.8 %attend_back.3 = (bf16[2880,768]{1,0:T(8,128)(2,1)}, bf16[8,4,128,128]{3,2,1,0:T(8,128)(2,1)}) custom-call(bf16[2880,512]{1,0:T(8,128)(2,1)} %tok.7, f32[2880,512]{1,0:T(8,128)} %get-tuple-element.306.dmid, bf16[2880,1536]{1,0:T(8,128)(2,1)} %get-tuple-element.292.proj, bf16[4,512,720]{2,1,0:T(8,128)(2,1)} %get-tuple-element.293.ctxT, ...), custom_call_target="tpu_custom_call" | custom-call | flops 100000000 | bytes 100000 | tf_op jit(solution)/shard_map/attend_back/pallas_call | solution.py:638
  319.6 4.2 %all-to-all-start.3 = ((bf16[8,4,128,128]{3,2,1,0:T(8,128)(2,1)}), bf16[8,4,128,128]{3,2,1,0:T(8,128)(2,1)S(1)}, u32[]{:S(2)}, u32[]{:S(2)}) async-start(bf16[8,4,128,128]{3,2,1,0:T(8,128)(2,1)} %get-tuple-element.305), calls=%async_computation.3 | async-start | bytes 2097152 | tf_op jit(solution)/shard_map/all_to_all | solution.py:864
  323.8 15.4 %enter.1 = (f32[2880,512]{1,0:T(8,128)}, f32[2,512]{1,0:T(2,128)}, f32[1024,512]{1,0:T(8,128)}, f32[1,512]{1,0:T(1,128)}) custom-call(bf16[2880,512]{1,0:T(8,128)(2,1)} %tok.7, f32[2880,512]{1,0:T(8,128)} %get-tuple-element.306.dmid, bf16[2880,768]{1,0:T(8,128)(2,1)} %get-tuple-element.307.dp0, bf16[2880,768]{1,0:T(8,128)(2,1)} %get-tuple-element.308.dp1, ...), custom_call_target="tpu_custom_call" | custom-call | flops 100000000 | bytes 100000 | tf_op jit(solution)/shard_map/enter/pallas_call | solution.py:698
  340.8 5.6 %all-to-all-start.4 = ((f32[32,12,128]{2,1,0:T(8,128)}), f32[32,12,128]{2,1,0:T(8,128)S(1)}, u32[]{:S(2)}, u32[]{:S(2)}) async-start(f32[32,12,128]{2,1,0:T(8,128)} %bitcast.27), calls=%async_computation.4 | async-start | bytes 524288 | tf_op jit(solution)/shard_map/all_to_all | solution.py:864
  353.9 14.0 %finish.1 = bf16[2880,512]{1,0:T(8,128)(2,1)} custom-call(s32[3]{0:T(128)} %pad_add_fusion.where, bf16[8,384,512]{2,1,0:T(8,128)(2,1)} %copy-done, s32[2880,8]{1,0:T(8,128)} %get-tuple-element.288.refs_8_.cols, f32[2880,512]{1,0:T(8,128)} %get-tuple-element.324.refs_11_.mid), custom_call_target="tpu_custom_call" | custom-call | flops 100000000 | bytes 100000 | tf_op jit(solution)/shard_map/finish/pallas_call | solution.py:546
  374.0 5.9 %all-to-all-start.5 = ((f32[32,1,128]{2,1,0:T(1,128)}), f32[32,1,128]{2,1,0:T(1,128)S(1)}, u32[]{:S(2)}, u32[]{:S(2)}) async-start(f32[32,1,128]{2,1,0:T(1,128)} %get-tuple-element.333), calls=%async_computation.5 | async-start | bytes 32768 | tf_op jit(solution)/shard_map/all_to_all | solution.py:864
  380.8 6.2 %all-to-all-done.5 = f32[32,1,128]{2,1,0:T(1,128)S(1)} async-done(((f32[32,1,128]{2,1,0:T(1,128)}), f32[32,1,128]{2,1,0:T(1,128)S(1)}, u32[]{:S(2)}, u32[]{:S(2)}) %all-to-all-start.5) | async-done | bytes 16416 | tf_op jit(solution)/shard_map/all_to_all | solution.py:864
  392.9 9.5 %adam.1 = (f32[512,384]{1,0:T(8,128)}, f32[512,384]{1,0:T(8,128)}, f32[512,384]{1,0:T(8,128)}, bf16[512,384]{1,0:T(8,128)(2,1)}, f32[128,512]{1,0:T(8,128)}, /*i...) custom-call(s32[3]{0:T(128)} %pad_add_fusion.where, ...), custom_call_target="tpu_custom_call" | custom-call | flops 100000000 | bytes 100000 | tf_op jit(solution)/shard_map/adam/pallas_call | solution.py:809
  (197 shorter events, 69.8 us)
Async XLA Ops:
  7.4 20.5 %collective-permute-start.1 = (bf16[80,512]{1,0:T(8,128)(2,1)S(1)}, bf16[80,512]{1,0:T(8,128)(2,1)S(1)}, u32[]{:S(2)}, u32[]{:S(2)}) collective-permute-start(bf16[80,512]{1,0:T(8,128)(2,1)S(1)} %concatenate.24), channel_id=1, source_target_pairs={{0,16},{8,24},{16,0},{24,8},{1,17},{9,25},{17,1},{25,9},{2,18},{10... | collective-permute-start | bytes 245768 | tf_op jit(solution)/shard_map/ppermute | solution.py:860
  11.3 34.4 %collective-permute-start.6 = (bf16[512,512]{1,0:T(8,128)(2,1)S(1)}, bf16[512,512]{1,0:T(8,128)(2,1)}, u32[]{:S(2)}, u32[]{:S(2)}) collective-permute-start(bf16[512,512]{1,0:T(8,128)(2,1)S(1)} %convert_bitcast_fusion.1.refs_4_.refs_6_), channel_id=1, source_target_pairs={{0,16},{8,24},{16,0},{24,8},{1,17},{9,25},{17,1},{25,9},{2,18},{10... | collective-permute-start | bytes 1572872 | tf_op jit(solution)/shard_map/ppermute | solution.py:860
  45.7 76.6 %all-to-all-start = ((bf16[8,384,512]{2,1,0:T(8,128)(2,1)}), bf16[8,384,512]{2,1,0:T(8,128)(2,1)}, u32[]{:S(2)}, u32[]{:S(2)}) async-start(bf16[8,384,512]{2,1,0:T(8,128)(2,1)} %spread.2), calls=%async_computation | async-start | bytes 6291456 | tf_op jit(solution)/shard_map/all_to_all | solution.py:864
  51.1 66.4 %collective-permute-start.10 = (bf16[1024,512]{1,0:T(8,128)(2,1)S(1)}, bf16[1024,512]{1,0:T(8,128)(2,1)}, u32[]{:S(2)}, u32[]{:S(2)}) collective-permute-start(bf16[1024,512]{1,0:T(8,128)(2,1)S(1)} %pad_maximum_fusion), channel_id=1, source_target_pairs={{0,8},{8,0},{16,24},{24,16},{1,9},{9,1},{17,25},{25,17},{2,10},{10... | collective-permute-start | bytes 3145736 | tf_op jit(solution)/shard_map/ppermute | solution.py:860
  53.5 64.0 %collective-permute-start.8 = (bf16[512,512]{1,0:T(8,128)(2,1)S(1)}, bf16[512,512]{1,0:T(8,128)(2,1)S(1)}, u32[]{:S(2)}, u32[]{:S(2)}) collective-permute-start(bf16[512,512]{1,0:T(8,128)(2,1)S(1)} %convert_bitcast_fusion.refs_7_.refs_9_), channel_id=1, source_target_pairs={{0,16},{8,24},{16,0},{24,8},{1,17},{9,25},{17,1},{25,9},{2,18},{10... | collective-permute-start | bytes 1572872 | tf_op jit(solution)/shard_map/ppermute | solution.py:860
  54.8 62.7 %collective-permute-start.9 = (bf16[512,512]{1,0:T(8,128)(2,1)S(1)}, bf16[512,512]{1,0:T(8,128)(2,1)S(1)}, u32[]{:S(2)}, u32[]{:S(2)}) collective-permute-start(bf16[512,512]{1,0:T(8,128)(2,1)S(1)} %convert_bitcast_fusion.refs_7_.refs_9_), channel_id=1, source_target_pairs={{0,24},{8,16},{16,8},{24,0},{1,25},{9,17},{17,9},{25,1},{2,26},{10... | collective-permute-start | bytes 1572872 | tf_op jit(solution)/shard_map/ppermute | solution.py:860
  56.1 61.4 %collective-permute-start.7 = (bf16[512,512]{1,0:T(8,128)(2,1)}, bf16[512,512]{1,0:T(8,128)(2,1)}, u32[]{:S(2)}, u32[]{:S(2)}) collective-permute-start(bf16[512,512]{1,0:T(8,128)(2,1)} %collective-permute-done.6.refs_5_.refs_7_), channel_id=1, source_target_pairs={{0,8},{8,0},{16,24},{24,16},{1,9},{9,1},{17,25},{25,17},{2,10},{10... | collective-permute-start | bytes 1572872 | tf_op jit(solution)/shard_map/ppermute | solution.py:860
  140.2 29.4 %collective-permute-start.17 = (bf16[384,512]{1,0:T(8,128)(2,1)S(1)}, bf16[384,512]{1,0:T(8,128)(2,1)S(1)}, u32[]{:S(2)}, u32[]{:S(2)}) collective-permute-start(bf16[384,512]{1,0:T(8,128)(2,1)S(1)} %copy-done.32), channel_id=1, source_target_pairs={{0,6},{1,7},{2,4},{3,5},{4,2},{5,3},{6,0},{7,1},{8,14},{9,15},{10,... | collective-permute-start | bytes 1179656 | tf_op jit(solution)/shard_map/ppermute | solution.py:860
  142.8 28.3 %collective-permute-start.18 = (bf16[384,512]{1,0:T(8,128)(2,1)S(1)}, bf16[384,512]{1,0:T(8,128)(2,1)S(1)}, u32[]{:S(2)}, u32[]{:S(2)}) collective-permute-start(bf16[384,512]{1,0:T(8,128)(2,1)S(1)} %copy-done.31), channel_id=1, source_target_pairs={{0,7},{1,6},{2,5},{3,4},{4,3},{5,2},{6,1},{7,0},{8,15},{9,14},{10,... | collective-permute-start | bytes 1179656 | tf_op jit(solution)/shard_map/ppermute | solution.py:860
  142.8 28.5 %collective-permute-start.19 = (bf16[384,512]{1,0:T(8,128)(2,1)}, bf16[384,512]{1,0:T(8,128)(2,1)S(1)}, u32[]{:S(2)}, u32[]{:S(2)}) collective-permute-start(bf16[384,512]{1,0:T(8,128)(2,1)} %get-tuple-element.251), channel_id=1, source_target_pairs={{0,1},{1,0},{2,3},{3,2},{4,5},{5,4},{6,7},{7,6},{8,9},{9,8},{10,11... | collective-permute-start | bytes 1179656 | tf_op jit(solution)/shard_map/ppermute | solution.py:860
  167.8 21.3 %collective-permute-start.20 = (bf16[384,512]{1,0:T(8,128)(2,1)}, bf16[384,512]{1,0:T(8,128)(2,1)S(1)}, u32[]{:S(2)}, u32[]{:S(2)}) collective-permute-start(bf16[384,512]{1,0:T(8,128)(2,1)} %get-tuple-element.253), channel_id=1, source_target_pairs={{0,2},{1,3},{2,0},{3,1},{4,6},{5,7},{6,4},{7,5},{8,10},{9,11},{10,... | collective-permute-start | bytes 1179656 | tf_op jit(solution)/shard_map/ppermute | solution.py:860
  169.5 43.3 %collective-permute-start.21 = (bf16[384,512]{1,0:T(8,128)(2,1)}, bf16[384,512]{1,0:T(8,128)(2,1)S(1)}, u32[]{:S(2)}, u32[]{:S(2)}) collective-permute-start(bf16[384,512]{1,0:T(8,128)(2,1)} %get-tuple-element.254), channel_id=1, source_target_pairs={{0,3},{1,2},{2,1},{3,0},{4,7},{5,6},{6,5},{7,4},{8,11},{9,10},{10,... | collective-permute-start | bytes 1179656 | tf_op jit(solution)/shard_map/ppermute | solution.py:860
  169.5 44.1 %collective-permute-start.22 = (bf16[384,512]{1,0:T(8,128)(2,1)}, bf16[384,512]{1,0:T(8,128)(2,1)S(1)}, u32[]{:S(2)}, u32[]{:S(2)}) collective-permute-start(bf16[384,512]{1,0:T(8,128)(2,1)} %get-tuple-element.255), channel_id=1, source_target_pairs={{0,4},{1,5},{2,6},{3,7},{4,0},{5,1},{6,2},{7,3},{8,12},{9,13},{10,... | collective-permute-start | bytes 1179656 | tf_op jit(solution)/shard_map/ppermute | solution.py:860
  171.1 42.5 %collective-permute-start.23 = (bf16[384,512]{1,0:T(8,128)(2,1)}, bf16[384,512]{1,0:T(8,128)(2,1)S(1)}, u32[]{:S(2)}, u32[]{:S(2)}) collective-permute-start(bf16[384,512]{1,0:T(8,128)(2,1)} %get-tuple-element.256), channel_id=1, source_target_pairs={{0,5},{1,4},{2,7},{3,6},{4,1},{5,0},{6,3},{7,2},{8,13},{9,12},{10,... | collective-permute-start | bytes 1179656 | tf_op jit(solution)/shard_map/ppermute | solution.py:860
  186.9 26.8 %collective-permute-start.24 = (bf16[384,512]{1,0:T(8,128)(2,1)}, bf16[384,512]{1,0:T(8,128)(2,1)S(1)}, u32[]{:S(2)}, u32[]{:S(2)}) collective-permute-start(bf16[384,512]{1,0:T(8,128)(2,1)} %get-tuple-element.260), channel_id=1, source_target_pairs={{0,6},{1,7},{2,4},{3,5},{4,2},{5,3},{6,0},{7,1},{8,14},{9,15},{10,... | collective-permute-start | bytes 1179656 | tf_op jit(solution)/shard_map/ppermute | solution.py:860
  189.1 24.6 %collective-permute-start.25 = (bf16[384,512]{1,0:T(8,128)(2,1)}, bf16[384,512]{1,0:T(8,128)(2,1)S(1)}, u32[]{:S(2)}, u32[]{:S(2)}) collective-permute-start(bf16[384,512]{1,0:T(8,128)(2,1)} %get-tuple-element.261), channel_id=1, source_target_pairs={{0,7},{1,6},{2,5},{3,4},{4,3},{5,2},{6,1},{7,0},{8,15},{9,14},{10,... | collective-permute-start | bytes 1179656 | tf_op jit(solution)/shard_map/ppermute | solution.py:860
  214.7 67.5 %all-to-all-start.1 = ((bf16[8,384,512]{2,1,0:T(8,128)(2,1)}), bf16[8,384,512]{2,1,0:T(8,128)(2,1)S(1)}, u32[]{:S(2)}, u32[]{:S(2)}) async-start(bf16[8,384,512]{2,1,0:T(8,128)(2,1)} %get-tuple-element.279), calls=%async_computation.1 | async-start | bytes 6291456 | tf_op jit(solution)/shard_map/all_to_all | solution.py:864
  218.6 101.0 %collective-permute-start.26 = (bf16[1024,512]{1,0:T(8,128)(2,1)}, bf16[1024,512]{1,0:T(8,128)(2,1)}, u32[]{:S(2)}, u32[]{:S(2)}) collective-permute-start(bf16[1024,512]{1,0:T(8,128)(2,1)} %get-tuple-element.302), channel_id=1, source_target_pairs={{0,8},{8,0},{16,24},{24,16},{1,9},{9,1},{17,25},{25,17},{2,10},{10... | collective-permute-start | bytes 3145736 | tf_op jit(solution)/shard_map/ppermute | solution.py:860
  219.8 99.7 %collective-permute-start.27 = (bf16[1024,512]{1,0:T(8,128)(2,1)}, bf16[1024,512]{1,0:T(8,128)(2,1)}, u32[]{:S(2)}, u32[]{:S(2)}) collective-permute-start(bf16[1024,512]{1,0:T(8,128)(2,1)} %get-tuple-element.303), channel_id=1, source_target_pairs={{0,16},{8,24},{16,0},{24,8},{1,17},{9,25},{17,1},{25,9},{2,18},{10... | collective-permute-start | bytes 3145736 | tf_op jit(solution)/shard_map/ppermute | solution.py:860
  221.9 97.7 %collective-permute-start.28 = (bf16[1024,512]{1,0:T(8,128)(2,1)}, bf16[1024,512]{1,0:T(8,128)(2,1)}, u32[]{:S(2)}, u32[]{:S(2)}) collective-permute-start(bf16[1024,512]{1,0:T(8,128)(2,1)} %get-tuple-element.304), channel_id=1, source_target_pairs={{0,24},{8,16},{16,8},{24,0},{1,25},{9,17},{17,9},{25,1},{2,26},{10... | collective-permute-start | bytes 3145736 | tf_op jit(solution)/shard_map/ppermute | solution.py:860
  282.2 37.3 %all-to-all-start.2 = ((bf16[8,4,128,128]{3,2,1,0:T(8,128)(2,1)}), bf16[8,4,128,128]{3,2,1,0:T(8,128)(2,1)}, u32[]{:S(2)}, u32[]{:S(2)}) async-start(bf16[8,4,128,128]{3,2,1,0:T(8,128)(2,1)} %get-tuple-element.297), calls=%async_computation.2 | async-start | bytes 2097152 | tf_op jit(solution)/shard_map/all_to_all | solution.py:864
  319.6 19.6 %all-to-all-start.3 = ((bf16[8,4,128,128]{3,2,1,0:T(8,128)(2,1)}), bf16[8,4,128,128]{3,2,1,0:T(8,128)(2,1)S(1)}, u32[]{:S(2)}, u32[]{:S(2)}) async-start(bf16[8,4,128,128]{3,2,1,0:T(8,128)(2,1)} %get-tuple-element.305), calls=%async_computation.3 | async-start | bytes 2097152 | tf_op jit(solution)/shard_map/all_to_all | solution.py:864
  340.8 27.1 %all-to-all-start.4 = ((f32[32,12,128]{2,1,0:T(8,128)}), f32[32,12,128]{2,1,0:T(8,128)S(1)}, u32[]{:S(2)}, u32[]{:S(2)}) async-start(f32[32,12,128]{2,1,0:T(8,128)} %bitcast.27), calls=%async_computation.4 | async-start | bytes 524288 | tf_op jit(solution)/shard_map/all_to_all | solution.py:864
  370.5 19.2 %collective-permute-start.32 = (bf16[2,128,128]{2,1,0:T(8,128)(2,1)}, bf16[2,128,128]{2,1,0:T(8,128)(2,1)S(1)}, u32[]{:S(2)}, u32[]{:S(2)}) collective-permute-start(bf16[2,128,128]{2,1,0:T(8,128)(2,1)} %get-tuple-element.334), channel_id=1, source_target_pairs={{0,2},{1,3},{2,0},{3,1},{4,6},{5,7},{6,4},{7,5},{8,10},{9,11},{10,... | collective-permute-start | bytes 196616 | tf_op jit(solution)/shard_map/ppermute | solution.py:860
  (59 other events, 840.2 us)
